TPU v7x, 128 devices: a whole 4x4x4 slice. The times are simulated.
128 devices in a mesh: lat: 128 (over y, x, z, core).
Axes of the slice: x: 4, y: 4, z: 4, core: 2. Of those that a mesh axis runs over, the one named last changes fastest.
Arguments:
- features: bfloat16 [256, 32, 8192], P('lat'), may hold values from -6 to 6
- cotangent: bfloat16 [256, 32, 8192], P('lat'), may hold values from -18 to 18
- basis_table: bfloat16 [256, 9, 9, 9], P('lat'), may hold values from -1.75 to 1.75
- lon_reach: int32 [256, 9], P('lat'), may hold values from 0 to 4, as said below
- weights: bfloat16 [9, 32, 32], replicated, may hold values from -0.375 to 0.375
Outputs:
- grad_input: bfloat16 [256, 32, 8192], P('lat')
- grad_weight: float32 [9, 32, 32], replicated
Inputs may be any that keep to these rules, and one draw needn't show every extreme that they name: `lon_reach`: entry 4 (the output cycle's own cycle) of every cycle is 4.
All inputs are finite; a program needn't handle non-finite values.
Results may differ from a plain program's by a relative error of at most 0.0065.
Values may be sent and summed in bfloat16 or wider, within the bound.
No kernel may reach another device: no remote copies, remote signals or barrier semaphores. Data moves between devices by JAX's collectives and lax.ppermute only.
A program may use at most 128 MiB of HBM per device.

v0:
```python
import math

import jax
import jax.numpy as jnp
from jax import lax
from jax.sharding import PartitionSpec as P

RAD = 4
LON_HALF = 4


def passed_along(array, axis, by):
    peers = lax.axis_size(axis)
    pairs = [(i, i + by) for i in range(peers) if 0 <= i + by < peers]
    return lax.ppermute(array, axis, pairs)


def extend_cycles(fields, hop_count, fetcher):
    blocks = []
    for place in range(2 * hop_count + 1):
        offset = hop_count - place
        if offset == 0:
            blocks.append(fields)
        else:
            blocks.append(fetcher(offset))
    joined = []
    for member in range(len(fields)):
        whole = jnp.concatenate([block[member] for block in blocks], axis=0)
        joined.append(whole)
    return tuple(joined)


def build_filters(basis_part, weights):
    return jnp.einsum(
        "rjdk,koi->rjdoi", basis_part, weights, preferred_element_type=jnp.float32
    ).astype(jnp.bfloat16)


def shifted_sum(matrix, window, channels, direction):
    lon_taps = 2 * LON_HALF + 1
    summed = jnp.zeros((channels, window.shape[1]), jnp.float32)
    for first in range(0, lon_taps, 3):
        last = min(first + 3, lon_taps)
        product = jnp.dot(
            matrix[first * channels : last * channels], window, preferred_element_type=jnp.float32
        )
        for column in range(first, last):
            piece = product[(column - first) * channels : (column - first + 1) * channels]
            summed = summed + jnp.roll(piece, direction * (column - LON_HALF), axis=-1)
    return summed


def forward_cycles(extended, filt, cycle_count):
    channels = extended.shape[1]
    cycle_taps = 2 * RAD + 1
    lon_taps = 2 * LON_HALF + 1
    flat_rows = extended.reshape(-1, extended.shape[2])
    matrices = jnp.transpose(filt, (0, 2, 3, 1, 4)).reshape(
        cycle_count, lon_taps * channels, cycle_taps * channels
    )

    def forward_one_cycle(cycle_index):
        window = lax.dynamic_slice_in_dim(
            flat_rows, cycle_index * channels, cycle_taps * channels, 0
        )
        return shifted_sum(matrices[cycle_index], window, channels, -1)

    return lax.map(forward_one_cycle, jnp.arange(cycle_count, dtype=jnp.int32))


def activation_grad(pre_act, cot_part):
    sigmoid_v = jax.nn.sigmoid(pre_act)
    return (cot_part.astype(jnp.float32) * sigmoid_v * (1.0 + pre_act * (1.0 - sigmoid_v))).astype(
        jnp.bfloat16
    )


def input_grad(delta_ext, filt_ext, cycle_count):
    channels = delta_ext.shape[1]
    cycle_taps = 2 * RAD + 1
    lon_taps = 2 * LON_HALF + 1
    flat_rows = delta_ext.reshape(-1, delta_ext.shape[2])

    def input_one_cycle(cycle_index):
        filt_window = lax.dynamic_slice_in_dim(filt_ext, cycle_index, cycle_taps, 0)
        picked = jnp.stack(
            [filt_window[place, cycle_taps - 1 - place] for place in range(cycle_taps)], axis=0
        )
        matrix = jnp.transpose(picked, (1, 3, 0, 2)).reshape(
            lon_taps * channels, cycle_taps * channels
        )
        window = lax.dynamic_slice_in_dim(
            flat_rows, cycle_index * channels, cycle_taps * channels, 0
        )
        return shifted_sum(matrix, window, channels, 1)

    return lax.map(input_one_cycle, jnp.arange(cycle_count, dtype=jnp.int32))


def weight_grad(delta, extended, basis_own):
    channels = delta.shape[1]
    cycle_taps = 2 * RAD + 1
    lon_taps = 2 * LON_HALF + 1
    flat_rows = extended.reshape(-1, extended.shape[2])

    def weight_one_cycle(cycle_index):
        delta_cycle = delta[cycle_index]
        rolled = jnp.concatenate(
            [jnp.roll(delta_cycle, column - LON_HALF, axis=-1) for column in range(lon_taps)],
            axis=0,
        )
        window = lax.dynamic_slice_in_dim(
            flat_rows, cycle_index * channels, cycle_taps * channels, 0
        )
        correl = lax.dot_general(
            rolled, window, (((1,), (1,)), ((), ())), preferred_element_type=jnp.float32
        )
        correl = correl.reshape(lon_taps, channels, cycle_taps, channels)
        return jnp.einsum("jdk,doji->koi", basis_own[cycle_index].astype(jnp.float32), correl)

    return jnp.sum(lax.map(weight_one_cycle, jnp.arange(delta.shape[0], dtype=jnp.int32)), axis=0)


def body(features, cotangent, basis_table, lon_reach, weights):
    cycle_count = features.shape[0]
    longitude = features.shape[2]
    lon_taps = 2 * LON_HALF + 1
    offsets_lon = jnp.arange(lon_taps, dtype=jnp.int32) - LON_HALF
    inside = jnp.abs(offsets_lon)[None, None, :] <= lon_reach[:, :, None]
    masked = jnp.where(inside[..., None], basis_table, jnp.zeros_like(basis_table))
    rim_depth = RAD
    hop_count = -(-rim_depth // cycle_count)
    near_hops = -(-RAD // cycle_count)
    feat_ext, basis_ext = extend_cycles(
        (features, masked),
        hop_count,
        lambda offset: passed_along((features, masked), "lat", offset),
    )
    filt_ext = build_filters(basis_ext, weights)
    pre_act = forward_cycles(feat_ext, filt_ext[RAD : RAD + cycle_count], cycle_count)
    delta = activation_grad(pre_act, cotangent)
    (delta_ext,) = extend_cycles(
        (delta,), near_hops, lambda offset: passed_along((delta,), "lat", offset)
    )
    grad_input = input_grad(delta_ext, filt_ext, cycle_count).astype(jnp.bfloat16)
    partial_w = weight_grad(delta, feat_ext, masked)
    summed_w = lax.psum(partial_w, "lat")
    scale_w = 1.0 / math.sqrt(lax.axis_size("lat") * cycle_count * longitude)
    return (grad_input, summed_w * scale_w)


def solution(mesh):
    in_specs = (
        P("lat", None, None),
        P("lat", None, None),
        P("lat", None, None, None),
        P("lat", None),
        P(),
    )
    out_specs = (P("lat", None, None), P())
    return jax.shard_map(body, mesh=mesh, in_specs=in_specs, out_specs=out_specs, check_vma=False)
```

profile of v0, /device:TPU:22, one launch (start us, length us, event | category | flops | bytes accessed | tf_op | source)
XLA Modules:
  0.0 252.7 jit_solution(17122488887826875174)
XLA Ops:
  2.5 6.2 %collective-permute-start.3 = (bf16[2,9,9,9]{3,0,2,1:T(2,128)(2,1)S(1)}, bf16[2,9,9,9]{3,0,2,1:T(2,128)(2,1)S(1)}, u32[]{:S(2)}, u32[]{:S(2)}) collective-permute-start(bf16[2,9,9,9]{3,0,2,1:T(2,128)(2,1)S(1)} %broadcast_select_fusion), channel_id=1, source_target_pairs={{2,0},{3,1},{4,2},{5,3},{6,4},{7,5},{8,6},{9,7},{10,8},{11,9},{12,... | collective-permute-start | bytes 8756 | tf_op jit(solution)/shard_map/ppermute | solution.py:15
  8.7 1.9 collective-permute-start.2
  10.6 2.4 collective-permute-start.1
  13.0 2.6 %collective-permute-start = (bf16[2,9,9,9]{3,0,2,1:T(2,128)(2,1)S(1)}, bf16[2,9,9,9]{3,0,2,1:T(2,128)(2,1)S(1)}, u32[]{:S(2)}, u32[]{:S(2)}) collective-permute-start(bf16[2,9,9,9]{3,0,2,1:T(2,128)(2,1)S(1)} %broadcast_select_fusion), channel_id=1, source_target_pairs={{0,2},{1,3},{2,4},{3,5},{4,6},{5,7},{6,8},{7,9},{8,10},{9,11},{10,... | collective-permute-start | bytes 8756 | tf_op jit(solution)/shard_map/ppermute | solution.py:15
  15.6 5.5 %collective-permute-start.6 = (bf16[2,32,8192]{2,1,0:T(8,128)(2,1)}, bf16[2,32,8192]{2,1,0:T(8,128)(2,1)}, u32[]{:S(2)}, u32[]{:S(2)}) collective-permute-start(bf16[2,32,8192]{2,1,0:T(8,128)(2,1)} %param.11), channel_id=1, source_target_pairs={{1,0},{2,1},{3,2},{4,3},{5,4},{6,5},{7,6},{8,7},{9,8},{10,9},{11,1... | collective-permute-start | bytes 3145736 | tf_op jit(solution)/shard_map/ppermute | solution.py:15
  22.4 1.9 collective-permute-start.5
  24.4 1.9 collective-permute-start.4
  26.3 6.0 %collective-permute-start.7 = (bf16[2,32,8192]{2,1,0:T(8,128)(2,1)}, bf16[2,32,8192]{2,1,0:T(8,128)(2,1)}, u32[]{:S(2)}, u32[]{:S(2)}) collective-permute-start(bf16[2,32,8192]{2,1,0:T(8,128)(2,1)} %param.11), channel_id=1, source_target_pairs={{2,0},{3,1},{4,2},{5,3},{6,4},{7,5},{8,6},{9,7},{10,8},{11,9},{12,... | collective-permute-start | bytes 3145736 | tf_op jit(solution)/shard_map/ppermute | solution.py:15
  32.4 1.4 concatenate.100
  33.8 3.1 %convolution_convert_fusion = bf16[10,9,9,32,32]{4,0,3,2,1:T(8,128)(2,1)S(1)} fusion(bf16[10,9,9,9]{3,0,2,1:T(8,128)(2,1)S(1)} %concatenate.100, bf16[9,32,32,1,1]{2,1,0,4,3:T(8,128)(2,1)S(1)} %bitcast.177), kind=kOutput, calls=%fused_computation.86 | convolution fusion | flops 15759360 | bytes 1691892 | tf_op jit(solution)/shard_map/rjdk,koi->rjdoi/dot_general | solution.py:34
  36.9 4.0 %copy-done.4 = bf16[10,9,9,32,32]{4,0,3,2,1:T(8,128)(2,1)} copy-done((bf16[10,9,9,32,32]{4,0,3,2,1:T(8,128)(2,1)}, bf16[10,9,9,32,32]{4,0,3,2,1:T(8,128)(2,1)S(1)}, u32[]{:S(2)}) %copy-start.4) | copy-done | bytes 1658904
  41.0 1.6 slice_bitcast_fusion
  44.9 9.9 %collective-permute-done.4 = bf16[2,32,8192]{2,1,0:T(8,128)(2,1)} collective-permute-done((bf16[2,32,8192]{2,1,0:T(8,128)(2,1)}, bf16[2,32,8192]{2,1,0:T(8,128)(2,1)}, u32[]{:S(2)}, u32[]{:S(2)}) %collective-permute-start.4) | collective-permute-done | bytes 1048608 | tf_op jit(solution)/shard_map/ppermute | solution.py:15
  54.8 1.3 constant_dynamic-update-slice_fusion.5
  56.1 1.4 constant_dynamic-update-slice_fusion.4
  57.6 1.3 constant_dynamic-update-slice_fusion.2
  58.9 1.3 constant_dynamic-update-slice_fusion.1
  60.3 2.3 copy-done.2
  62.5 25.6 %while.33 = (s32[]{:T(128)}, f32[2,32,8192]{2,1,0:T(8,128)S(1)}, s32[2]{0:T(128)S(1)}, bf16[2,288,288]{2,1,0:T(8,128)(2,1)S(1)}, bf16[320,8192]{1,0:T(8,128)(2,1)}) while((s32[]{:T(128)}, f32[2,32,8192]{2,1,0:T(8,128)S(1)}, s32[2]{0:T(128)S(1)}, bf16[2,288,288]{2,1,0:T(8,128)(2,1)S(1)}, bf16[320,8192]{1,0:T(8,128)(2,1)}) %tuple.141), condition=%wide.region_1.2_spmd.clone, body=%wide.region_0.1_spmd.sunk.clone | while | flops 1363148800 | bytes 66937100 | solution.py:68
  65.6 3.8 %fusion.167 = f32[96,8192]{1,0:T(8,128)S(1)} fusion(bf16[320,8192]{1,0:T(8,128)(2,1)} %get-tuple-element.475, s32[]{:T(128)S(6)} %select_n.37, bf16[2,288,288]{2,1,0:T(8,128)(2,1)S(1)} %get-tuple-element.474, s32[]{:T(128)S(6)} %select_n.38, s32[]{:T(128)S(6)} %add.329), kind=kOutput, calls=%fused_computation.clone.1.clone | convolution fusion | flops 452984832 | bytes 7938060 | tf_op jit(solution)/shard_map/while/body/eval_jaxpr/dot_general | solution.py:44
  70.5 1.3 fusion.163
  72.3 1.3 fusion.164
  78.3 3.8 %fusion.167 = f32[96,8192]{1,0:T(8,128)S(1)} fusion(bf16[320,8192]{1,0:T(8,128)(2,1)} %get-tuple-element.475, s32[]{:T(128)S(6)} %select_n.37, bf16[2,288,288]{2,1,0:T(8,128)(2,1)S(1)} %get-tuple-element.474, s32[]{:T(128)S(6)} %select_n.38, s32[]{:T(128)S(6)} %add.329), kind=kOutput, calls=%fused_computation.clone.1.clone | convolution fusion | flops 452984832 | bytes 7938060 | tf_op jit(solution)/shard_map/while/body/eval_jaxpr/dot_general | solution.py:44
  83.2 1.3 fusion.163
  85.0 1.3 fusion.164
  88.1 3.0 %multiply_convert_fusion = bf16[2,32,8192]{2,1,0:T(8,128)(2,1)} fusion(f32[2,32,8192]{2,1,0:T(8,128)S(1)} %get-tuple-element.88, bf16[2,32,8192]{2,1,0:T(8,128)(2,1)} %param.12), kind=kLoop, calls=%fused_computation.87 | loop fusion | flops 5242880 | bytes 4194304 | tf_op jit(solution)/shard_map/convert_element_type | solution.py:73
  91.1 3.8 %collective-permute-start.11 = (bf16[2,32,8192]{2,1,0:T(8,128)(2,1)}, bf16[2,32,8192]{2,1,0:T(8,128)(2,1)}, u32[]{:S(2)}, u32[]{:S(2)}) collective-permute-start(bf16[2,32,8192]{2,1,0:T(8,128)(2,1)} %multiply_convert_fusion), channel_id=1, source_target_pairs={{2,0},{3,1},{4,2},{5,3},{6,4},{7,5},{8,6},{9,7},{10,8},{11,9},{12,... | collective-permute-start | bytes 3145736 | tf_op jit(solution)/shard_map/ppermute | solution.py:15
  94.9 8.0 %collective-permute-start.10 = (bf16[2,32,8192]{2,1,0:T(8,128)(2,1)}, bf16[2,32,8192]{2,1,0:T(8,128)(2,1)}, u32[]{:S(2)}, u32[]{:S(2)}) collective-permute-start(bf16[2,32,8192]{2,1,0:T(8,128)(2,1)} %multiply_convert_fusion), channel_id=1, source_target_pairs={{1,0},{2,1},{3,2},{4,3},{5,4},{6,5},{7,6},{8,7},{9,8},{10,9},{11,1... | collective-permute-start | bytes 3145736 | tf_op jit(solution)/shard_map/ppermute | solution.py:15
  102.9 2.5 collective-permute-start.9
  105.4 3.6 %collective-permute-start.8 = (bf16[2,32,8192]{2,1,0:T(8,128)(2,1)}, bf16[2,32,8192]{2,1,0:T(8,128)(2,1)S(1)}, u32[]{:S(2)}, u32[]{:S(2)}) collective-permute-start(bf16[2,32,8192]{2,1,0:T(8,128)(2,1)} %multiply_convert_fusion), channel_id=1, source_target_pairs={{0,2},{1,3},{2,4},{3,5},{4,6},{5,7},{6,8},{7,9},{8,10},{9,11},{10,... | collective-permute-start | bytes 3145736 | tf_op jit(solution)/shard_map/ppermute | solution.py:15
  109.0 23.8 %while.35 = (s32[]{:T(128)}, f32[2,9,32,32]{3,1,2,0:T(8,128)S(1)}, s32[2]{0:T(128)S(1)}, bf16[2,9,9,9]{1,3,2,0:T(8,128)(2,1)S(1)}, bf16[2,32,8192]{2,1,0:T(8,128)(2,1)}, /*index=5*/bf16[320,8192]{1,0:T(8,128)(2,1)}) while((s32[]{:T(128)}, f32[2,9,32,32]{3,1,2,0:T(8,128)S(1)}, s32[2]{0:T(128)S(1)}, ...), condition=%wide.region_5.6_spmd.clone, body=%wide.region_4.5_spmd.sunk.clone | while | flops 1368836096 | bytes 46074088 | solution.py:121
  114.8 1.6 constant_dynamic-update-slice_fusion.13
  117.3 2.6 %fusion.203 = bf16[288,288]{1,0:T(8,128)(2,1)S(1)} fusion(bf16[288,8192]{1,0:T(8,128)(2,1)S(1)} %maximum_dynamic-update-slice_fusion.31, bf16[320,8192]{1,0:T(8,128)(2,1)S(1)} %bitcast.182, s32[]{:T(128)S(6)} %select_n.42), kind=kOutput, calls=%fused_computation.68.clone.1.clone | convolution fusion | flops 1358954496 | bytes 9603076 | tf_op jit(solution)/shard_map/while/body/eval_jaxpr/dot_general | solution.py:115
  126.7 1.6 constant_dynamic-update-slice_fusion.13
  129.1 2.6 %fusion.203 = bf16[288,288]{1,0:T(8,128)(2,1)S(1)} fusion(bf16[288,8192]{1,0:T(8,128)(2,1)S(1)} %maximum_dynamic-update-slice_fusion.31, bf16[320,8192]{1,0:T(8,128)(2,1)S(1)} %bitcast.182, s32[]{:T(128)S(6)} %select_n.42), kind=kOutput, calls=%fused_computation.68.clone.1.clone | convolution fusion | flops 1358954496 | bytes 9603076 | tf_op jit(solution)/shard_map/while/body/eval_jaxpr/dot_general | solution.py:115
  132.9 72.7 %psum.7 = f32[9,32,32]{2,0,1:T(8,128)S(1)} all-reduce(f32[9,32,32]{2,0,1:T(8,128)S(1)} %reduce_sum.9), channel_id=1, replica_groups=mesh['lat'=128] {'lat'}, use_global_device_ids=true, to_apply=%region_7.8 | all-reduce | flops 9216 | bytes 73728 | tf_op jit(solution)/shard_map/psum | solution.py:147
  206.4 1.4 constant_dynamic-update-slice_fusion.9
  207.8 1.3 constant_dynamic-update-slice_fusion.8
  209.1 1.3 constant_dynamic-update-slice_fusion.7
  210.4 1.3 constant_dynamic-update-slice_fusion.6
  211.7 2.3 copy-done.3
  214.0 37.8 %while.34 = (s32[]{:T(128)}, bf16[2,32,8192]{2,1,0:T(8,128)(2,1)S(1)}, s32[2]{0:T(128)S(1)}, bf16[10,9,9,32,32]{4,0,3,2,1:T(8,128)(2,1)}, bf16[320,8192]{1,0:T(8,128)(2,1)}) while((s32[]{:T(128)}, bf16[2,32,8192]{2,1,0:T(8,128)(2,1)S(1)}, s32[2]{0:T(128)S(1)}, bf16[10,9,9,32,32]{4,0,3,2,1:T(8,128)(2,1)}, ...), condition=%wide.region_3.4_spmd.clone, body=%wide.region_2.3_spmd.sunk.clone | while | flops 1363148800 | bytes 70291936 | solution.py:97
  217.2 4.4 %constant_dynamic-slice_fusion.11 = (bf16[1,1,9,32,32]{4,0,3,2,1:T(2,128)(2,1)S(1)}, bf16[1,1,9,32,32]{4,0,3,2,1:T(2,128)(2,1)S(1)}, bf16[1,1,9,32,32]{4,0,3,2,1...) fusion(bf16[10,9,9,32,32]{4,0,3,2,1:T(8,128)(2,1)} %get-tuple-e, ...), kind=kLoop, calls=%fused_computation.67.clone.1.clone | loop fusion | bytes 331844 | tf_op jit(solution)/shard_map/while/body/eval_jaxpr/slice | solution.py:87
  223.6 3.7 %fusion.189 = f32[96,8192]{1,0:T(8,128)S(1)} fusion(bf16[96,288]{0,1:T(8,128)(2,1)S(1)} %slice.550, bf16[320,8192]{1,0:T(8,128)(2,1)} %get-tuple-element.490, s32[]{:T(128)S(6)} %select_n.40), kind=kOutput, calls=%fused_computation.22.clone.1.clone | convolution fusion | flops 452984832 | bytes 7919620 | tf_op jit(solution)/shard_map/while/body/eval_jaxpr/dot_general | solution.py:44
  230.1 1.3 fusion.185
  236.1 4.2 %constant_dynamic-slice_fusion.11 = (bf16[1,1,9,32,32]{4,0,3,2,1:T(2,128)(2,1)S(1)}, bf16[1,1,9,32,32]{4,0,3,2,1:T(2,128)(2,1)S(1)}, bf16[1,1,9,32,32]{4,0,3,2,1...) fusion(bf16[10,9,9,32,32]{4,0,3,2,1:T(8,128)(2,1)} %get-tuple-e, ...), kind=kLoop, calls=%fused_computation.67.clone.1.clone | loop fusion | bytes 331844 | tf_op jit(solution)/shard_map/while/body/eval_jaxpr/slice | solution.py:87
  242.4 3.7 %fusion.189 = f32[96,8192]{1,0:T(8,128)S(1)} fusion(bf16[96,288]{0,1:T(8,128)(2,1)S(1)} %slice.550, bf16[320,8192]{1,0:T(8,128)(2,1)} %get-tuple-element.490, s32[]{:T(128)S(6)} %select_n.40), kind=kOutput, calls=%fused_computation.22.clone.1.clone | convolution fusion | flops 452984832 | bytes 7919620 | tf_op jit(solution)/shard_map/while/body/eval_jaxpr/dot_general | solution.py:44
  248.9 1.3 fusion.185
  (206 shorter events, 38.3 us)
Async XLA Ops:
  0.6 33.1 %copy-start = (bf16[9,32,32]{2,1,0:T(8,128)(2,1)S(1)}, bf16[9,32,32]{2,1,0:T(8,128)(2,1)}, u32[]{:S(2)}) copy-start(bf16[9,32,32]{2,1,0:T(8,128)(2,1)} %param.15) | copy-start | bytes 55300
  2.5 19.9 %collective-permute-start.3 = (bf16[2,9,9,9]{3,0,2,1:T(2,128)(2,1)S(1)}, bf16[2,9,9,9]{3,0,2,1:T(2,128)(2,1)S(1)}, u32[]{:S(2)}, u32[]{:S(2)}) collective-permute-start(bf16[2,9,9,9]{3,0,2,1:T(2,128)(2,1)S(1)} %broadcast_select_fusion), channel_id=1, source_target_pairs={{2,0},{3,1},{4,2},{5,3},{6,4},{7,5},{8,6},{9,7},{10,8},{11,9},{12,... | collective-permute-start | bytes 8756 | tf_op jit(solution)/shard_map/ppermute | solution.py:15
  8.7 15.7 %collective-permute-start.2 = (bf16[2,9,9,9]{3,0,2,1:T(2,128)(2,1)S(1)}, bf16[2,9,9,9]{3,0,2,1:T(2,128)(2,1)S(1)}, u32[]{:S(2)}, u32[]{:S(2)}) collective-permute-start(bf16[2,9,9,9]{3,0,2,1:T(2,128)(2,1)S(1)} %broadcast_select_fusion), channel_id=1, source_target_pairs={{1,0},{2,1},{3,2},{4,3},{5,4},{6,5},{7,6},{8,7},{9,8},{10,9},{11,1... | collective-permute-start | bytes 8756 | tf_op jit(solution)/shard_map/ppermute | solution.py:15
  10.6 15.7 %collective-permute-start.1 = (bf16[2,9,9,9]{3,0,2,1:T(2,128)(2,1)S(1)}, bf16[2,9,9,9]{3,0,2,1:T(2,128)(2,1)S(1)}, u32[]{:S(2)}, u32[]{:S(2)}) collective-permute-start(bf16[2,9,9,9]{3,0,2,1:T(2,128)(2,1)S(1)} %broadcast_select_fusion), channel_id=1, source_target_pairs={{0,1},{1,2},{2,3},{3,4},{4,5},{5,6},{6,7},{7,8},{8,9},{9,10},{10,1... | collective-permute-start | bytes 8756 | tf_op jit(solution)/shard_map/ppermute | solution.py:15
  13.0 19.3 %collective-permute-start = (bf16[2,9,9,9]{3,0,2,1:T(2,128)(2,1)S(1)}, bf16[2,9,9,9]{3,0,2,1:T(2,128)(2,1)S(1)}, u32[]{:S(2)}, u32[]{:S(2)}) collective-permute-start(bf16[2,9,9,9]{3,0,2,1:T(2,128)(2,1)S(1)} %broadcast_select_fusion), channel_id=1, source_target_pairs={{0,2},{1,3},{2,4},{3,5},{4,6},{5,7},{6,8},{7,9},{8,10},{9,11},{10,... | collective-permute-start | bytes 8756 | tf_op jit(solution)/shard_map/ppermute | solution.py:15
  15.6 42.0 %collective-permute-start.6 = (bf16[2,32,8192]{2,1,0:T(8,128)(2,1)}, bf16[2,32,8192]{2,1,0:T(8,128)(2,1)}, u32[]{:S(2)}, u32[]{:S(2)}) collective-permute-start(bf16[2,32,8192]{2,1,0:T(8,128)(2,1)} %param.11), channel_id=1, source_target_pairs={{1,0},{2,1},{3,2},{4,3},{5,4},{6,5},{7,6},{8,7},{9,8},{10,9},{11,1... | collective-permute-start | bytes 3145736 | tf_op jit(solution)/shard_map/ppermute | solution.py:15
  22.4 33.7 %collective-permute-start.5 = (bf16[2,32,8192]{2,1,0:T(8,128)(2,1)}, bf16[2,32,8192]{2,1,0:T(8,128)(2,1)}, u32[]{:S(2)}, u32[]{:S(2)}) collective-permute-start(bf16[2,32,8192]{2,1,0:T(8,128)(2,1)} %param.11), channel_id=1, source_target_pairs={{0,1},{1,2},{2,3},{3,4},{4,5},{5,6},{6,7},{7,8},{8,9},{9,10},{10,1... | collective-permute-start | bytes 3145736 | tf_op jit(solution)/shard_map/ppermute | solution.py:15
  24.4 30.4 %collective-permute-start.4 = (bf16[2,32,8192]{2,1,0:T(8,128)(2,1)}, bf16[2,32,8192]{2,1,0:T(8,128)(2,1)}, u32[]{:S(2)}, u32[]{:S(2)}) collective-permute-start(bf16[2,32,8192]{2,1,0:T(8,128)(2,1)} %param.11), channel_id=1, source_target_pairs={{0,2},{1,3},{2,4},{3,5},{4,6},{5,7},{6,8},{7,9},{8,10},{9,11},{10,... | collective-permute-start | bytes 3145736 | tf_op jit(solution)/shard_map/ppermute | solution.py:15
  26.3 32.6 %collective-permute-start.7 = (bf16[2,32,8192]{2,1,0:T(8,128)(2,1)}, bf16[2,32,8192]{2,1,0:T(8,128)(2,1)}, u32[]{:S(2)}, u32[]{:S(2)}) collective-permute-start(bf16[2,32,8192]{2,1,0:T(8,128)(2,1)} %param.11), channel_id=1, source_target_pairs={{2,0},{3,1},{4,2},{5,3},{6,4},{7,5},{8,6},{9,7},{10,8},{11,9},{12,... | collective-permute-start | bytes 3145736 | tf_op jit(solution)/shard_map/ppermute | solution.py:15
  36.9 4.1 %copy-start.4 = (bf16[10,9,9,32,32]{4,0,3,2,1:T(8,128)(2,1)}, bf16[10,9,9,32,32]{4,0,3,2,1:T(8,128)(2,1)S(1)}, u32[]{:S(2)}) copy-start(bf16[10,9,9,32,32]{4,0,3,2,1:T(8,128)(2,1)S(1)} %convolution_convert_fusion) | copy-start | bytes 4976644
  44.9 12.7 %copy-start.6 = (bf16[2,32,8192]{2,1,0:T(8,128)(2,1)S(1)}, bf16[2,32,8192]{2,1,0:T(8,128)(2,1)}, u32[]{:S(2)}) copy-start(bf16[2,32,8192]{2,1,0:T(8,128)(2,1)} %param.11) | copy-start | bytes 3145732
  56.1 6.5 %copy-start.5 = (f32[2,32,8192]{2,1,0:T(8,128)S(1)}, f32[2,32,8192]{2,1,0:T(8,128)}, u32[]{:S(2)}) copy-start(f32[2,32,8192]{2,1,0:T(8,128)} %custom-call.13) | copy-start | bytes 6291460
  60.2 2.3 copy-start.2
  65.6 4.9 %slice-start = ((s8[5242880]{0:T(1024)(128)(4,1)}), s8[4194304]{0:T(1024)(128)(4,1)S(1)}, s32[]{:S(2)}) async-start(s8[5242880]{0:T(1024)(128)(4,1)} %bitcast.179), calls=%async_computation | async-start | bytes 8388608 | tf_op jit(solution)/shard_map/while
  65.6 4.9 %slice-start.1 = ((s8[5242880]{0:T(1024)(128)(4,1)}), s8[1048576]{0:T(1024)(128)(4,1)S(1)}, s32[]{:S(2)}) async-start(s8[5242880]{0:T(1024)(128)(4,1)} %bitcast.179), calls=%async_computation.1 | async-start | bytes 2097152 | tf_op jit(solution)/shard_map/while
  78.3 4.9 %slice-start = ((s8[5242880]{0:T(1024)(128)(4,1)}), s8[4194304]{0:T(1024)(128)(4,1)S(1)}, s32[]{:S(2)}) async-start(s8[5242880]{0:T(1024)(128)(4,1)} %bitcast.179), calls=%async_computation | async-start | bytes 8388608 | tf_op jit(solution)/shard_map/while
  78.3 4.9 %slice-start.1 = ((s8[5242880]{0:T(1024)(128)(4,1)}), s8[1048576]{0:T(1024)(128)(4,1)S(1)}, s32[]{:S(2)}) async-start(s8[5242880]{0:T(1024)(128)(4,1)} %bitcast.179), calls=%async_computation.1 | async-start | bytes 2097152 | tf_op jit(solution)/shard_map/while
  91.1 119.2 %collective-permute-start.11 = (bf16[2,32,8192]{2,1,0:T(8,128)(2,1)}, bf16[2,32,8192]{2,1,0:T(8,128)(2,1)}, u32[]{:S(2)}, u32[]{:S(2)}) collective-permute-start(bf16[2,32,8192]{2,1,0:T(8,128)(2,1)} %multiply_convert_fusion), channel_id=1, source_target_pairs={{2,0},{3,1},{4,2},{5,3},{6,4},{7,5},{8,6},{9,7},{10,8},{11,9},{12,... | collective-permute-start | bytes 3145736 | tf_op jit(solution)/shard_map/ppermute | solution.py:15
  94.9 114.2 %collective-permute-start.10 = (bf16[2,32,8192]{2,1,0:T(8,128)(2,1)}, bf16[2,32,8192]{2,1,0:T(8,128)(2,1)}, u32[]{:S(2)}, u32[]{:S(2)}) collective-permute-start(bf16[2,32,8192]{2,1,0:T(8,128)(2,1)} %multiply_convert_fusion), channel_id=1, source_target_pairs={{1,0},{2,1},{3,2},{4,3},{5,4},{6,5},{7,6},{8,7},{9,8},{10,9},{11,1... | collective-permute-start | bytes 3145736 | tf_op jit(solution)/shard_map/ppermute | solution.py:15
  102.9 103.5 %collective-permute-start.9 = (bf16[2,32,8192]{2,1,0:T(8,128)(2,1)}, bf16[2,32,8192]{2,1,0:T(8,128)(2,1)}, u32[]{:S(2)}, u32[]{:S(2)}) collective-permute-start(bf16[2,32,8192]{2,1,0:T(8,128)(2,1)} %multiply_convert_fusion), channel_id=1, source_target_pairs={{0,1},{1,2},{2,3},{3,4},{4,5},{5,6},{6,7},{7,8},{8,9},{9,10},{10,1... | collective-permute-start | bytes 3145736 | tf_op jit(solution)/shard_map/ppermute | solution.py:15
  105.4 100.9 %collective-permute-start.8 = (bf16[2,32,8192]{2,1,0:T(8,128)(2,1)}, bf16[2,32,8192]{2,1,0:T(8,128)(2,1)S(1)}, u32[]{:S(2)}, u32[]{:S(2)}) collective-permute-start(bf16[2,32,8192]{2,1,0:T(8,128)(2,1)} %multiply_convert_fusion), channel_id=1, source_target_pairs={{0,2},{1,3},{2,4},{3,5},{4,6},{5,7},{6,8},{7,9},{8,10},{9,11},{10,... | collective-permute-start | bytes 3145736 | tf_op jit(solution)/shard_map/ppermute | solution.py:15
  113.9 3.4 %slice-start.2 = ((s8[5242880]{0:T(1024)(128)(4,1)}), s8[4194304]{0:T(1024)(128)(4,1)S(1)}, s32[]{:S(2)}) async-start(s8[5242880]{0:T(1024)(128)(4,1)} %bitcast.181), calls=%async_computation.2 | async-start | bytes 8388608 | tf_op jit(solution)/shard_map/while
  114.6 2.6 %slice-start.3 = ((s8[5242880]{0:T(1024)(128)(4,1)}), s8[1048576]{0:T(1024)(128)(4,1)S(1)}, s32[]{:S(2)}) async-start(s8[5242880]{0:T(1024)(128)(4,1)} %bitcast.181), calls=%async_computation.3 | async-start | bytes 2097152 | tf_op jit(solution)/shard_map/while
  125.7 3.4 %slice-start.2 = ((s8[5242880]{0:T(1024)(128)(4,1)}), s8[4194304]{0:T(1024)(128)(4,1)S(1)}, s32[]{:S(2)}) async-start(s8[5242880]{0:T(1024)(128)(4,1)} %bitcast.181), calls=%async_computation.2 | async-start | bytes 8388608 | tf_op jit(solution)/shard_map/while
  126.5 2.6 %slice-start.3 = ((s8[5242880]{0:T(1024)(128)(4,1)}), s8[1048576]{0:T(1024)(128)(4,1)S(1)}, s32[]{:S(2)}) async-start(s8[5242880]{0:T(1024)(128)(4,1)} %bitcast.181), calls=%async_computation.3 | async-start | bytes 2097152 | tf_op jit(solution)/shard_map/while
  206.4 7.6 %copy-start.7 = (bf16[2,32,8192]{2,1,0:T(8,128)(2,1)S(1)}, bf16[2,32,8192]{2,1,0:T(8,128)(2,1)}, u32[]{:S(2)}) copy-start(bf16[2,32,8192]{2,1,0:T(8,128)(2,1)} %broadcast_convert_fusion) | copy-start | bytes 3145732
  211.7 2.3 copy-start.3
  223.4 4.4 %slice-start.4 = ((s8[5242880]{0:T(1024)(128)(4,1)}), s8[1048576]{0:T(1024)(128)(4,1)S(1)}, s32[]{:S(2)}) async-start(s8[5242880]{0:T(1024)(128)(4,1)} %bitcast.184), calls=%async_computation.4 | async-start | bytes 2097152 | tf_op jit(solution)/shard_map/while
  223.6 4.2 %slice-start.5 = ((s8[5242880]{0:T(1024)(128)(4,1)}), s8[4194304]{0:T(1024)(128)(4,1)S(1)}, s32[]{:S(2)}) async-start(s8[5242880]{0:T(1024)(128)(4,1)} %bitcast.184), calls=%async_computation.5 | async-start | bytes 8388608 | tf_op jit(solution)/shard_map/while
  242.2 4.4 %slice-start.4 = ((s8[5242880]{0:T(1024)(128)(4,1)}), s8[1048576]{0:T(1024)(128)(4,1)S(1)}, s32[]{:S(2)}) async-start(s8[5242880]{0:T(1024)(128)(4,1)} %bitcast.184), calls=%async_computation.4 | async-start | bytes 2097152 | tf_op jit(solution)/shard_map/while
  242.4 4.2 %slice-start.5 = ((s8[5242880]{0:T(1024)(128)(4,1)}), s8[4194304]{0:T(1024)(128)(4,1)S(1)}, s32[]{:S(2)}) async-start(s8[5242880]{0:T(1024)(128)(4,1)} %bitcast.184), calls=%async_computation.5 | async-start | bytes 8388608 | tf_op jit(solution)/shard_map/while
  251.7 1.0 copy-start.8
  251.8 1.0 copy-start.1
where the time goes:
time: 256 us; the launch traced here: 253 us
  blocking collectives  72.7 us (28%)
  local copies, waits for them, and re-layouts  59.6 us (23%)
  starting transfers between devices  46.3 us (18%)
  matrix products  34.8 us (14%)
  loops' own time  16.2 us (6%)
  other arithmetic  12.1 us (5%)
  waiting for transfers between devices  9.91 us (4%)
    psum x1, blocking collectives, body(): summed_w = lax.psum(partial_w, 'lat')  72.7 us
    ppermute x12, starting transfers between devices, passed_along(): return lax.ppermute(array, axis, pairs)  46.3 us
    dot_general x12, matrix products, shifted_sum(): jnp.dot(matrix[first * channels:last * channels], window, preferred_eleme...  25.4 us
    unnamed x28, local copies, waits for them, and re-layouts  19.2 us
    ppermute x12, waiting for transfers between devices, passed_along(): return lax.ppermute(array, axis, pairs)  9.91 us
    slice x2, local copies, waits for them, and re-layouts, input_one_cycle(): filt_window[place, cycle_taps - 1 - place]  8.61 us
    slice x56, local copies, waits for them, and re-layouts, shifted_sum(): summed = summed + jnp.roll(piece, direction * (column - LON_HALF), axis=-1)  7.48 us
    another operation x1, loops' own time, input_grad(): return lax.map(input_one_cycle, jnp.arange(cycle_count, dtype=jnp.int32))  5.55 us
  transfers between devices with their start and end apart: 12, of which 1 were waited for; matrix products, arithmetic and copies ran while one was open for 15% of the time, Pallas kernels for 0%

commit v1 on v0

v1 whole, which is shorter than its diff:
```python
import functools
import math

import jax
import jax.numpy as jnp
from jax import lax
from jax.experimental import pallas as pl
from jax.experimental.pallas import tpu as pltpu
from jax.sharding import PartitionSpec as P

C = 32
K = 9
RAD = 4
TAPS = 9
OWN = 2
SPAN = OWN + 2 * RAD
ROWS = SPAN * C
BLOCK = OWN * C
DEEP = 3 * ROWS
OUT = 3 * BLOCK
PAD = 128
LANES = 128
TILE = 1024
VMEM = 56 * 1024 * 1024


def spread_matrix(kind, shape):
    row = lax.broadcasted_iota(jnp.int32, shape, 0)
    lane = lax.broadcasted_iota(jnp.int32, shape, 1)
    hit = (lane // C == row) if kind == "table" else (lane % C == row)
    return jnp.where(hit, 1.0, 0.0).astype(jnp.bfloat16)


def filter_kernel(table_ref, weight_ref, out_ref, table_wide, weight_wide):
    table_wide[...] = jnp.dot(
        table_ref[...],
        spread_matrix("table", (3 * SPAN, DEEP)),
        preferred_element_type=jnp.float32,
    )
    weight_wide[...] = jnp.dot(
        weight_ref[...], spread_matrix("weight", (C, DEEP)), preferred_element_type=jnp.float32
    )
    for group in range(3 * OWN):
        total = jnp.zeros((C, DEEP), jnp.float32)
        for k in range(K):
            at = group * K + k
            total = total + table_wide[at : at + 1, :] * weight_wide[k * C : (k + 1) * C, :]
        out_ref[group * C : (group + 1) * C, :] = total.astype(jnp.bfloat16)


def make_filter(table, weights):
    return pl.pallas_call(
        filter_kernel,
        out_shape=jax.ShapeDtypeStruct((OUT, DEEP), jnp.bfloat16),
        in_specs=[pl.BlockSpec(memory_space=pltpu.VMEM)] * 2,
        out_specs=pl.BlockSpec(memory_space=pltpu.VMEM),
        scratch_shapes=[
            pltpu.VMEM((3 * OWN * K, DEEP), jnp.float32),
            pltpu.VMEM((K * C, DEEP), jnp.float32),
        ],
        compiler_params=pltpu.CompilerParams(vmem_limit_bytes=VMEM),
        name="make_filter",
    )(table, weights)


def window_copies(blocks, x_ref, sems, parity, longitude):
    far_row = pl.multiple_of(BLOCK + 2 * BLOCK * parity, BLOCK)
    mate_row = pl.multiple_of(3 * BLOCK - 2 * BLOCK * parity, BLOCK)
    rows = (0, far_row, 2 * BLOCK, mate_row, 4 * BLOCK)
    tiles = longitude // TILE

    def tile_copies(tile):
        first = pl.multiple_of(tile * TILE, TILE)
        return [
            pltpu.make_async_copy(
                block.at[:, pl.ds(first, TILE)],
                x_ref.at[pl.ds(row, BLOCK), pl.ds(first + PAD, TILE)],
                sems.at[place, tile],
            )
            for place, (block, row) in enumerate(zip(blocks, rows))
        ]

    def edge_copies():
        copies = []
        for place, (block, row) in enumerate(zip(blocks, rows)):
            for side, (source, target) in enumerate(
                ((longitude - PAD, 0), (0, longitude + PAD))
            ):
                copies.append(
                    pltpu.make_async_copy(
                        block.at[:, pl.ds(source, PAD)],
                        x_ref.at[pl.ds(row, BLOCK), pl.ds(target, PAD)],
                        sems.at[place, tiles + side],
                    )
                )
        return copies

    return tile_copies, edge_copies


def pre_shift(x_ref, x3_ref, first):
    wide = x_ref[:, pl.ds(first, TILE + 2 * PAD)]
    for e in range(3):
        start = PAD + e - 1
        x3_ref[e * ROWS : (e + 1) * ROWS, :] = wide[:, start : start + TILE]


def conv_kernel(with_act, matrix_ref, low, far, own, mate, high, *rest):
    if with_act:
        cot_ref, out_ref, x_ref, x3_ref, p3_ref, sems = rest
    else:
        out_ref, x_ref, x3_ref, p3_ref, sems = rest
    longitude = own.shape[1]
    tiles = longitude // TILE
    parity = lax.rem(lax.axis_index("lat"), 2)
    tile_copies, edge_copies = window_copies(
        (low, far, own, mate, high), x_ref, sems, parity, longitude
    )
    for copy in edge_copies():
        copy.start()

    @pl.loop(0, tiles)
    def _(tile):
        for copy in tile_copies(tile):
            copy.start()

    for copy in edge_copies():
        copy.wait()
    for copy in tile_copies(0):
        copy.wait()

    @pl.loop(0, tiles)
    def _(tile):
        @pl.when(tile + 1 < tiles)
        def _():
            for copy in tile_copies(tile + 1):
                copy.wait()

        first = pl.multiple_of(tile * TILE, TILE)
        pre_shift(x_ref, x3_ref, first)
        p3_ref[:, pl.ds(first + PAD, TILE)] = jnp.dot(
            matrix_ref[...], x3_ref[...], preferred_element_type=jnp.float32
        )

    p3_ref[:, 0:PAD] = p3_ref[:, longitude : longitude + PAD]
    p3_ref[:, longitude + PAD : longitude + 2 * PAD] = p3_ref[:, PAD : 2 * PAD]

    @pl.loop(0, tiles)
    def _(tile):
        first = pl.multiple_of(tile * TILE, TILE)
        total = p3_ref[BLOCK : 2 * BLOCK, pl.ds(first + PAD, TILE)]
        for f in (0, 2):
            wide = p3_ref[f * BLOCK : (f + 1) * BLOCK, pl.ds(first, TILE + 2 * PAD)]
            start = PAD + 3 * (f - 1)
            total = total + wide[:, start : start + TILE]
        if with_act:
            cot = cot_ref[:, pl.ds(first, TILE)].astype(jnp.float32)
            sg = jax.nn.sigmoid(total)
            total = cot * sg * (1.0 + total * (1.0 - sg))
        out_ref[:, pl.ds(first, TILE)] = total.astype(out_ref.dtype)


def conv(matrix, blocks, cot=None):
    longitude = blocks[0].shape[1]
    tiles = longitude // TILE
    extra = [] if cot is None else [cot]
    return pl.pallas_call(
        functools.partial(conv_kernel, cot is not None),
        out_shape=jax.ShapeDtypeStruct((BLOCK, longitude), jnp.bfloat16),
        in_specs=[pl.BlockSpec(memory_space=pltpu.VMEM)]
        + [pl.BlockSpec(memory_space=pl.ANY)] * 5
        + [pl.BlockSpec(memory_space=pltpu.VMEM)] * len(extra),
        out_specs=pl.BlockSpec(memory_space=pltpu.VMEM),
        scratch_shapes=[
            pltpu.VMEM((ROWS, longitude + 2 * PAD), jnp.bfloat16),
            pltpu.VMEM((DEEP, TILE), jnp.bfloat16),
            pltpu.VMEM((OUT, longitude + 2 * PAD), jnp.float32),
            pltpu.SemaphoreType.DMA((5, tiles + 2)),
        ],
        compiler_params=pltpu.CompilerParams(vmem_limit_bytes=VMEM),
        cost_estimate=pl.CostEstimate(
            flops=2 * OUT * DEEP * longitude,
            bytes_accessed=7 * BLOCK * longitude * 2,
            transcendentals=0,
        ),
        name="forward_conv" if extra else "input_conv",
    )(matrix, *blocks, *extra)


def weight_kernel(scale, low, far, own, mate, high, delta, table_ref, out_ref, x_ref, x3_ref, d_ref, d3_ref, g_ref, w_ref, table_wide, sems, dsems):
    longitude = own.shape[1]
    tiles = longitude // TILE
    parity = lax.rem(lax.axis_index("lat"), 2)
    tile_copies, edge_copies = window_copies(
        (low, far, own, mate, high), x_ref, sems, parity, longitude
    )
    delta_copies = [
        pltpu.make_async_copy(
            delta.at[:, pl.ds(source, size)], d_ref.at[:, pl.ds(target, size)], dsems.at[at]
        )
        for at, (source, target, size) in enumerate(
            ((0, PAD, longitude), (longitude - PAD, 0, PAD), (0, longitude + PAD, PAD))
        )
    ]
    for copy in edge_copies() + delta_copies:
        copy.start()

    @pl.loop(0, tiles)
    def _(tile):
        for copy in tile_copies(tile):
            copy.start()

    table_wide[...] = jnp.dot(
        table_ref[...],
        spread_matrix("table", (3 * SPAN, DEEP)),
        preferred_element_type=jnp.float32,
    )
    g_ref[...] = jnp.zeros_like(g_ref)
    for copy in edge_copies() + delta_copies:
        copy.wait()
    for copy in tile_copies(0):
        copy.wait()

    @pl.loop(0, tiles)
    def _(tile):
        @pl.when(tile + 1 < tiles)
        def _():
            for copy in tile_copies(tile + 1):
                copy.wait()

        first = pl.multiple_of(tile * TILE, TILE)
        pre_shift(x_ref, x3_ref, first)
        wide = d_ref[:, pl.ds(first, TILE + 2 * PAD)]
        for f in range(3):
            start = PAD - 3 * (f - 1)
            d3_ref[f * BLOCK : (f + 1) * BLOCK, :] = wide[:, start : start + TILE]
        g_ref[...] += lax.dot_general(
            d3_ref[...],
            x3_ref[...],
            (((1,), (1,)), ((), ())),
            preferred_element_type=jnp.float32,
        )

    whole = DEEP // LANES
    for k in range(K):
        total = jnp.zeros((C, DEEP), jnp.float32)
        for group in range(3 * OWN):
            at = group * K + k
            total = total + table_wide[at : at + 1, :] * g_ref[group * C : (group + 1) * C, :]
        narrow = jnp.concatenate(
            [total[:, whole * LANES :], jnp.zeros((C, (whole + 1) * LANES - DEEP), jnp.float32)],
            axis=1,
        )
        for part in range(whole):
            narrow = narrow + total[:, part * LANES : (part + 1) * LANES]
        w_ref[k * C : (k + 1) * C, :] = narrow
    row = lax.broadcasted_iota(jnp.int32, (LANES, LANES), 0)
    lane = lax.broadcasted_iota(jnp.int32, (LANES, LANES), 1)
    result = jnp.zeros((K * C // 4, LANES), jnp.float32)
    for c in range(4):
        fold = jnp.where(lane == c * C + row % C, 1.0, 0.0)
        result = result + jnp.dot(
            w_ref[pl.ds(c, K * C // 4, stride=4), :],
            fold,
            preferred_element_type=jnp.float32,
            precision=lax.Precision.HIGHEST,
        )
    out_ref[...] = result * scale


def weight_part(blocks, delta, table, scale):
    longitude = delta.shape[1]
    tiles = longitude // TILE
    return pl.pallas_call(
        functools.partial(weight_kernel, scale),
        out_shape=jax.ShapeDtypeStruct((K * C // 4, LANES), jnp.float32),
        in_specs=[pl.BlockSpec(memory_space=pl.ANY)] * 6
        + [pl.BlockSpec(memory_space=pltpu.VMEM)],
        out_specs=pl.BlockSpec(memory_space=pltpu.VMEM),
        scratch_shapes=[
            pltpu.VMEM((ROWS, longitude + 2 * PAD), jnp.bfloat16),
            pltpu.VMEM((DEEP, TILE), jnp.bfloat16),
            pltpu.VMEM((BLOCK, longitude + 2 * PAD), jnp.bfloat16),
            pltpu.VMEM((OUT, TILE), jnp.bfloat16),
            pltpu.VMEM((OUT, DEEP), jnp.float32),
            pltpu.VMEM((K * C, LANES), jnp.float32),
            pltpu.VMEM((3 * OWN * K, DEEP), jnp.float32),
            pltpu.SemaphoreType.DMA((5, tiles + 2)),
            pltpu.SemaphoreType.DMA((3,)),
        ],
        compiler_params=pltpu.CompilerParams(vmem_limit_bytes=VMEM),
        cost_estimate=pl.CostEstimate(
            flops=2 * OUT * DEEP * longitude,
            bytes_accessed=6 * BLOCK * longitude * 2,
            transcendentals=0,
        ),
        name="weight_part",
    )(*blocks, delta, table)


def moved(array, by):
    peers = lax.axis_size("lat")
    return lax.ppermute(
        array, "lat", [(i, i + by) for i in range(peers) if 0 <= i + by < peers]
    )


def swapped(array, bit=1):
    return lax.ppermute(array, "lat", [(i, i ^ bit) for i in range(lax.axis_size("lat"))])


def around(own):
    low = moved(own, 2)
    high = moved(own, -2)
    mate = swapped(own)
    parity = lax.rem(lax.axis_index("lat"), 2)
    far = swapped(jnp.where(parity == 0, high, low))
    return low, far, own, mate, high


def as_table(padded):
    parts = padded.reshape(OWN, SPAN, 3, 3, K)
    return jnp.transpose(parts, (2, 0, 4, 3, 1)).reshape(3 * OWN * K, 3 * SPAN)


def forward_table(masked):
    return as_table(
        jnp.stack(
            [
                jnp.pad(masked[r], ((r, SPAN - TAPS - r), (0, 0), (0, 0)))
                for r in range(OWN)
            ]
        )
    )


def input_table(masked_ext):
    q = jnp.arange(OWN)[:, None, None]
    s = jnp.arange(SPAN)[None, :, None]
    j = jnp.arange(TAPS)[None, None, :]
    hit = (j == TAPS - 1 - (s - q))[..., None, None]
    picked = jnp.sum(jnp.where(hit, masked_ext[None], 0).astype(jnp.float32), axis=2)
    return as_table(picked[:, :, ::-1].astype(jnp.bfloat16))


def body(features, cotangent, basis_table, lon_reach, weights):
    longitude = features.shape[2]
    peers = lax.axis_size("lat")
    offsets = jnp.arange(TAPS, dtype=jnp.int32) - RAD
    inside = jnp.abs(offsets)[None, None, :] <= lon_reach[:, :, None]
    masked = jnp.where(inside[..., None], basis_table, jnp.zeros_like(basis_table))

    feat = around(features.reshape(BLOCK, longitude))
    table = forward_table(masked)
    matrix = make_filter(table, weights.reshape(K * C, C))
    masked_ext = jnp.concatenate(
        [moved(masked, 2), moved(masked, 1), masked, moved(masked, -1), moved(masked, -2)], axis=0
    )
    matrix_in = make_filter(
        input_table(masked_ext), jnp.transpose(weights, (0, 2, 1)).reshape(K * C, C)
    )

    delta = conv(matrix, feat, cotangent.reshape(BLOCK, longitude))
    near = around(delta)
    scale = 1.0 / math.sqrt(peers * OWN * longitude)
    total = weight_part(feat, delta, table, scale)
    for bit in (1, 8, 16, 32, 64, 2, 4):
        total = total + swapped(total, bit)
    grad_input = conv(matrix_in, near)
    return grad_input.reshape(OWN, C, longitude), total.reshape(K, C, C)


def solution(mesh):
    in_specs = (
        P("lat", None, None),
        P("lat", None, None),
        P("lat", None, None, None),
        P("lat", None),
        P(),
    )
    out_specs = (P("lat", None, None), P())
    return jax.shard_map(body, mesh=mesh, in_specs=in_specs, out_specs=out_specs, check_vma=False)
```

time: 256 us -> 141 us (0.55)
  the two profiles are of different devices: /device:TPU:22 before, /device:TPU:56 now
where the time goes in v1:
time: 141 us
  waiting for transfers between devices  51.4 us (36%)
  Pallas kernels  41.3 us (29%)
  starting transfers between devices  36.6 us (26%)
  local copies, waits for them, and re-layouts  8.36 us (6%)
  other arithmetic  1.92 us (1%)
    ppermute x8, starting transfers between devices, moved(): lax.ppermute(array, 'lat', [(i, i + by) for i in range(peers) if 0 <= i +...  32.8 us
    ppermute x8, waiting for transfers between devices, moved(): lax.ppermute(array, 'lat', [(i, i + by) for i in range(peers) if 0 <= i +...  30 us
    pallas_call x2, Pallas kernels, conv(): pl.pallas_call(functools.partial(conv_kernel, cot is not None), out_shape...  24.8 us
    ppermute x11, waiting for transfers between devices, swapped(): lax.ppermute(array, 'lat', [(i, i ^ bit) for i in range(lax.axis_size('la...  21.4 us
    pallas_call x1, Pallas kernels, weight_part(): pl.pallas_call(functools.partial(weight_kernel, scale), out_shape=jax.Sha...  11.6 us
    pallas_call x2, Pallas kernels, make_filter(): pl.pallas_call(filter_kernel, out_shape=jax.ShapeDtypeStruct((OUT, DEEP),...  4.93 us
    unnamed x21, local copies, waits for them, and re-layouts  4.28 us
    ppermute x11, starting transfers between devices, swapped(): lax.ppermute(array, 'lat', [(i, i ^ bit) for i in range(lax.axis_size('la...  3.79 us
  transfers between devices with their start and end apart: 19, of which 10 were waited for; matrix products, arithmetic and copies ran while one was open for 5% of the time, Pallas kernels for 12%

profile of v1, /device:TPU:56, one launch (start us, length us, event | category | flops | bytes accessed | tf_op | source)
XLA Modules:
  0.0 140.6 jit_solution(5623677987833007925)
XLA Ops:
  0.6 3.8 %collective-permute-start.4 = (bf16[64,8192]{1,0:T(8,128)(2,1)}, bf16[64,8192]{1,0:T(8,128)(2,1)S(1)}, u32[]{:S(2)}, u32[]{:S(2)}) collective-permute-start(bf16[64,8192]{1,0:T(8,128)(2,1)} %bitcast.20), channel_id=1, source_target_pairs={{0,2},{1,3},{2,4},{3,5},{4,6},{5,7},{6,8},{7,9},{8,10},{9,11},{10,... | collective-permute-start | bytes 3145736 | tf_op jit(solution)/shard_map/ppermute | solution.py:303
  4.5 2.0 %collective-permute-start.5 = (bf16[64,8192]{1,0:T(8,128)(2,1)}, bf16[64,8192]{1,0:T(8,128)(2,1)S(1)}, u32[]{:S(2)}, u32[]{:S(2)}) collective-permute-start(bf16[64,8192]{1,0:T(8,128)(2,1)} %bitcast.21), channel_id=1, source_target_pairs={{2,0},{3,1},{4,2},{5,3},{6,4},{7,5},{8,6},{9,7},{10,8},{11,9},{12,... | collective-permute-start | bytes 3145736 | tf_op jit(solution)/shard_map/ppermute | solution.py:303
  6.5 0.1 collective-permute-start.7
  6.6 21.0 %collective-permute-done.4.low = bf16[64,8192]{1,0:T(8,128)(2,1)S(1)} collective-permute-done((bf16[64,8192]{1,0:T(8,128)(2,1)}, bf16[64,8192]{1,0:T(8,128)(2,1)S(1)}, u32[]{:S(2)}, u32[]{:S(2)}) %collective-permute-start.4) | collective-permute-done | bytes 1048608 | tf_op jit(solution)/shard_map/ppermute | solution.py:303
  27.6 3.6 %collective-permute-done.5.high = bf16[64,8192]{1,0:T(8,128)(2,1)S(1)} collective-permute-done((bf16[64,8192]{1,0:T(8,128)(2,1)}, bf16[64,8192]{1,0:T(8,128)(2,1)S(1)}, u32[]{:S(2)}, u32[]{:S(2)}) %collective-permute-start.5) | collective-permute-done | bytes 1048608 | tf_op jit(solution)/shard_map/ppermute | solution.py:303
  31.2 0.1 broadcast_select_fusion.1
  31.3 0.8 copy-done.3
  32.2 0.7 copy-done.7
  32.8 0.1 broadcast_compare_fusion
  32.9 0.1 copy_select_fusion
  33.1 0.2 copy.32
  33.3 0.2 copy.33
  33.6 0.7 reshape.76.table_ref
  34.3 2.5 %make_filter.3.matrix_ref = bf16[192,960]{1,0:T(8,128)(2,1)} custom-call(bf16[54,30]{1,0:T(8,128)(2,1)} %reshape.76.table_ref, bf16[288,32]{1,0:T(8,128)(2,1)} %bitcast.15), custom_call_target="tpu_custom_call" | custom-call | tf_op jit(solution)/shard_map/make_filter/pallas_call | solution.py:52
  36.7 12.7 %forward_conv.1.own.delta = bf16[64,8192]{1,0:T(8,128)(2,1)} custom-call(bf16[192,960]{1,0:T(8,128)(2,1)} %make_filter.3.matrix_ref, bf16[64,8192]{1,0:T(8,128)(2,1)} %copy-done.2, bf16[64,8192]{1,0:T(8,128)(2,1)} %collective-permute-done.6.far, bf16[64,8192]{1,0:T(8,128)(2,1)} %bitcast.23, bf16[64,8192]{1,0:T(8,128)(2,1)} %collective-permute-done.7.mate, ...), custom_call_target="tpu_custom_call" | custom-call | flops 3019898880 | bytes 7340032 | tf_op jit(solution)/shard_map/forward_conv/pallas_call | solution.py:167
  49.5 3.5 %collective-permute-start.8 = (bf16[64,8192]{1,0:T(8,128)(2,1)}, bf16[64,8192]{1,0:T(8,128)(2,1)S(1)}, u32[]{:S(2)}, u32[]{:S(2)}) collective-permute-start(bf16[64,8192]{1,0:T(8,128)(2,1)} %forward_conv.1.own.delta), channel_id=1, source_target_pairs={{0,2},{1,3},{2,4},{3,5},{4,6},{5,7},{6,8},{7,9},{8,10},{9,11},{10,... | collective-permute-start | bytes 3145736 | tf_op jit(solution)/shard_map/ppermute | solution.py:303
  53.0 2.9 %collective-permute-start.9 = (bf16[64,8192]{1,0:T(8,128)(2,1)}, bf16[64,8192]{1,0:T(8,128)(2,1)S(1)}, u32[]{:S(2)}, u32[]{:S(2)}) collective-permute-start(bf16[64,8192]{1,0:T(8,128)(2,1)} %forward_conv.1.own.delta), channel_id=1, source_target_pairs={{2,0},{3,1},{4,2},{5,3},{6,4},{7,5},{8,6},{9,7},{10,8},{11,9},{12,... | collective-permute-start | bytes 3145736 | tf_op jit(solution)/shard_map/ppermute | solution.py:303
  55.9 3.4 %collective-permute-start = (bf16[2,9,9,9]{3,2,1,0:T(8,128)(2,1)S(1)}, bf16[2,9,9,9]{3,2,1,0:T(8,128)(2,1)}, u32[]{:S(2)}, u32[]{:S(2)}) collective-permute-start(bf16[2,9,9,9]{3,2,1,0:T(8,128)(2,1)S(1)} %copy_select_fusion), channel_id=1, source_target_pairs={{0,2},{1,3},{2,4},{3,5},{4,6},{5,7},{6,8},{7,9},{8,10},{9,11},{10,... | collective-permute-start | bytes 8756 | tf_op jit(solution)/shard_map/ppermute | solution.py:303
  59.3 1.9 %collective-permute-start.1 = (bf16[2,9,9,9]{3,2,1,0:T(8,128)(2,1)S(1)}, bf16[2,9,9,9]{3,2,1,0:T(8,128)(2,1)S(1)}, u32[]{:S(2)}, u32[]{:S(2)}) collective-permute-start(bf16[2,9,9,9]{3,2,1,0:T(8,128)(2,1)S(1)} %copy_select_fusion), channel_id=1, source_target_pairs={{0,1},{1,2},{2,3},{3,4},{4,5},{5,6},{6,7},{7,8},{8,9},{9,10},{10,1... | collective-permute-start | bytes 8756 | tf_op jit(solution)/shard_map/ppermute | solution.py:303
  61.2 2.2 %collective-permute-start.11 = (bf16[64,8192]{1,0:T(8,128)(2,1)}, bf16[64,8192]{1,0:T(8,128)(2,1)S(1)}, u32[]{:S(2)}, u32[]{:S(2)}) collective-permute-start(bf16[64,8192]{1,0:T(8,128)(2,1)} %forward_conv.1.own.delta), channel_id=1, source_target_pairs={{0,1},{1,0},{2,3},{3,2},{4,5},{5,4},{6,7},{7,6},{8,9},{9,8},{10,11... | collective-permute-start | bytes 3145736 | tf_op jit(solution)/shard_map/ppermute | solution.py:309
  63.4 11.6 %weight_part.1 = f32[72,128]{1,0:T(8,128)} custom-call(bf16[64,8192]{1,0:T(8,128)(2,1)} %copy-done.2, bf16[64,8192]{1,0:T(8,128)(2,1)} %collective-permute-done.6.far, bf16[64,8192]{1,0:T(8,128)(2,1)} %bitcast.24, bf16[64,8192]{1,0:T(8,128)(2,1)} %collective-permute-done.7.mate, bf16[64,8192]{1,0:T(8,128)(2,1)} %copy-done.3, ...), custom_call_target="tpu_custom_call" | custom-call | flops 3019898880 | bytes 6291456 | tf_op jit(solution)/shard_map/weight_part/pallas_call | solution.py:274
  75.0 3.1 %collective-permute-done.8.low = bf16[64,8192]{1,0:T(8,128)(2,1)S(1)} collective-permute-done((bf16[64,8192]{1,0:T(8,128)(2,1)}, bf16[64,8192]{1,0:T(8,128)(2,1)S(1)}, u32[]{:S(2)}, u32[]{:S(2)}) %collective-permute-start.8) | collective-permute-done | bytes 1048608 | tf_op jit(solution)/shard_map/ppermute | solution.py:303
  78.1 2.3 %collective-permute-done.9.high = bf16[64,8192]{1,0:T(8,128)(2,1)S(1)} collective-permute-done((bf16[64,8192]{1,0:T(8,128)(2,1)}, bf16[64,8192]{1,0:T(8,128)(2,1)S(1)}, u32[]{:S(2)}, u32[]{:S(2)}) %collective-permute-start.9) | collective-permute-done | bytes 1048608 | tf_op jit(solution)/shard_map/ppermute | solution.py:303
  80.4 0.1 broadcast_select_fusion
  80.5 0.8 copy-done.1
  81.4 0.7 copy.24
  82.1 6.8 %collective-permute-start.2 = (bf16[2,9,9,9]{3,2,1,0:T(8,128)(2,1)S(1)}, bf16[2,9,9,9]{3,2,1,0:T(8,128)(2,1)S(1)}, u32[]{:S(2)}, u32[]{:S(2)}) collective-permute-start(bf16[2,9,9,9]{3,2,1,0:T(8,128)(2,1)S(1)} %copy_select_fusion), channel_id=1, source_target_pairs={{1,0},{2,1},{3,2},{4,3},{5,4},{6,5},{7,6},{8,7},{9,8},{10,9},{11,1... | collective-permute-start | bytes 8756 | tf_op jit(solution)/shard_map/ppermute | solution.py:303
  88.9 0.8 add.30
  89.7 0.1 collective-permute-start.13
  89.8 0.9 constant_dynamic-update-slice_fusion.4
  90.7 3.1 %collective-permute-done.13 = f32[72,128]{1,0:T(8,128)S(1)} collective-permute-done((f32[72,128]{1,0:T(8,128)S(1)}, f32[72,128]{1,0:T(8,128)S(1)}, u32[]{:S(2)}, u32[]{:S(2)}) %collective-permute-start.13) | collective-permute-done | bytes 36896 | tf_op jit(solution)/shard_map/ppermute | solution.py:309
  93.7 8.5 %collective-permute-start.3 = (bf16[2,9,9,9]{3,2,1,0:T(8,128)(2,1)S(1)}, bf16[2,9,9,9]{3,2,1,0:T(8,128)(2,1)S(1)}, u32[]{:S(2)}, u32[]{:S(2)}) collective-permute-start(bf16[2,9,9,9]{3,2,1,0:T(8,128)(2,1)S(1)} %copy_select_fusion), channel_id=1, source_target_pairs={{2,0},{3,1},{4,2},{5,3},{6,4},{7,5},{8,6},{9,7},{10,8},{11,9},{12,... | collective-permute-start | bytes 8756 | tf_op jit(solution)/shard_map/ppermute | solution.py:303
  102.3 0.1 collective-permute-start.14
  102.4 5.4 %collective-permute-done.14 = f32[72,128]{1,0:T(8,128)S(1)} collective-permute-done((f32[72,128]{1,0:T(8,128)S(1)}, f32[72,128]{1,0:T(8,128)S(1)}, u32[]{:S(2)}, u32[]{:S(2)}) %collective-permute-start.14) | collective-permute-done | bytes 36896 | tf_op jit(solution)/shard_map/ppermute | solution.py:309
  107.8 0.4 collective-permute-start.15
  108.2 0.1 constant_dynamic-update-slice_fusion.2
  108.4 3.4 %collective-permute-done.15 = f32[72,128]{1,0:T(8,128)S(1)} collective-permute-done((f32[72,128]{1,0:T(8,128)S(1)}, f32[72,128]{1,0:T(8,128)S(1)}, u32[]{:S(2)}, u32[]{:S(2)}) %collective-permute-start.15) | collective-permute-done | bytes 36896 | tf_op jit(solution)/shard_map/ppermute | solution.py:309
  111.8 0.9 collective-permute-start.16
  112.7 4.5 %collective-permute-done.16 = f32[72,128]{1,0:T(8,128)S(1)} collective-permute-done((f32[72,128]{1,0:T(8,128)S(1)}, f32[72,128]{1,0:T(8,128)S(1)}, u32[]{:S(2)}, u32[]{:S(2)}) %collective-permute-start.16) | collective-permute-done | bytes 36896 | tf_op jit(solution)/shard_map/ppermute | solution.py:309
  117.3 0.7 copy.22
  118.0 3.3 %collective-permute-done.17 = f32[72,128]{1,0:T(8,128)S(1)} collective-permute-done((f32[72,128]{1,0:T(8,128)S(1)}, f32[72,128]{1,0:T(8,128)S(1)}, u32[]{:S(2)}, u32[]{:S(2)}) %collective-permute-start.17) | collective-permute-done | bytes 36896 | tf_op jit(solution)/shard_map/ppermute | solution.py:309
  121.2 0.5 convert_reduce_fusion
  121.8 0.7 reshape.73.table_ref
  122.5 2.5 %make_filter.2.matrix_ref = bf16[192,960]{1,0:T(8,128)(2,1)} custom-call(bf16[54,30]{1,0:T(8,128)(2,1)} %reshape.73.table_ref, bf16[288,32]{1,0:T(8,128)(2,1)} %bitcast.17), custom_call_target="tpu_custom_call" | custom-call | tf_op jit(solution)/shard_map/make_filter/pallas_call | solution.py:52
  125.0 1.7 %collective-permute-done.18 = f32[72,128]{1,0:T(8,128)S(1)} collective-permute-done((f32[72,128]{1,0:T(8,128)S(1)}, f32[72,128]{1,0:T(8,128)S(1)}, u32[]{:S(2)}, u32[]{:S(2)}) %collective-permute-start.18) | collective-permute-done | bytes 36896 | tf_op jit(solution)/shard_map/ppermute | solution.py:309
  126.7 0.8 reshape.72
  127.5 1.0 copy-done.8
  128.5 12.1 %input_conv.1 = bf16[64,8192]{1,0:T(8,128)(2,1)} custom-call(bf16[192,960]{1,0:T(8,128)(2,1)} %make_filter.2.matrix_ref, bf16[64,8192]{1,0:T(8,128)(2,1)} %copy-done, bf16[64,8192]{1,0:T(8,128)(2,1)} %collective-permute-done.10.far, bf16[64,8192]{1,0:T(8,128)(2,1)} %forward_conv.1.own.delta, bf16[64,8192]{1,0:T(8,128)(2,1)} %copy-done.8, ...), custom_call_target="tpu_custom_call" | custom-call | flops 3019898880 | bytes 7340032 | tf_op jit(solution)/shard_map/input_conv/pallas_call | solution.py:167
  (49 shorter events, 0.4 us)
Async XLA Ops:
  0.6 27.0 %collective-permute-start.4 = (bf16[64,8192]{1,0:T(8,128)(2,1)}, bf16[64,8192]{1,0:T(8,128)(2,1)S(1)}, u32[]{:S(2)}, u32[]{:S(2)}) collective-permute-start(bf16[64,8192]{1,0:T(8,128)(2,1)} %bitcast.20), channel_id=1, source_target_pairs={{0,2},{1,3},{2,4},{3,5},{4,6},{5,7},{6,8},{7,9},{8,10},{9,11},{10,... | collective-permute-start | bytes 3145736 | tf_op jit(solution)/shard_map/ppermute | solution.py:303
  4.5 26.7 %collective-permute-start.5 = (bf16[64,8192]{1,0:T(8,128)(2,1)}, bf16[64,8192]{1,0:T(8,128)(2,1)S(1)}, u32[]{:S(2)}, u32[]{:S(2)}) collective-permute-start(bf16[64,8192]{1,0:T(8,128)(2,1)} %bitcast.21), channel_id=1, source_target_pairs={{2,0},{3,1},{4,2},{5,3},{6,4},{7,5},{8,6},{9,7},{10,8},{11,9},{12,... | collective-permute-start | bytes 3145736 | tf_op jit(solution)/shard_map/ppermute | solution.py:303
  6.5 30.2 %collective-permute-start.7 = (bf16[64,8192]{1,0:T(8,128)(2,1)}, bf16[64,8192]{1,0:T(8,128)(2,1)}, u32[]{:S(2)}, u32[]{:S(2)}) collective-permute-start(bf16[64,8192]{1,0:T(8,128)(2,1)} %bitcast.22), channel_id=1, source_target_pairs={{0,1},{1,0},{2,3},{3,2},{4,5},{5,4},{6,7},{7,6},{8,9},{9,8},{10,11... | collective-permute-start | bytes 3145736 | tf_op jit(solution)/shard_map/ppermute | solution.py:309
  6.6 26.3 %copy-start.5 = (bf16[2,9,9,9]{3,0,2,1:T(2,128)(2,1)S(1)}, bf16[2,9,9,9]{3,0,2,1:T(2,128)(2,1)}, u32[]{:S(2)}) copy-start(bf16[2,9,9,9]{3,0,2,1:T(2,128)(2,1)} %param.7) | copy-start | bytes 8752
  27.6 3.7 %copy-start.2 = (bf16[64,8192]{1,0:T(8,128)(2,1)}, bf16[64,8192]{1,0:T(8,128)(2,1)S(1)}, u32[]{:S(2)}) copy-start(bf16[64,8192]{1,0:T(8,128)(2,1)S(1)} %collective-permute-done.4.low) | copy-start | bytes 3145732
  31.2 1.0 copy-start.3
  32.2 0.7 copy-start.7
  32.2 4.6 %collective-permute-start.6 = (bf16[64,8192]{1,0:T(8,128)(2,1)S(1)}, bf16[64,8192]{1,0:T(8,128)(2,1)}, u32[]{:S(2)}, u32[]{:S(2)}) collective-permute-start(bf16[64,8192]{1,0:T(8,128)(2,1)S(1)} %broadcast_select_fusion.1), channel_id=1, source_target_pairs={{0,1},{1,0},{2,3},{3,2},{4,5},{5,4},{6,7},{7,6},{8,9},{9,8},{10,11... | collective-permute-start | bytes 3145736 | tf_op jit(solution)/shard_map/ppermute | solution.py:309
  49.5 28.6 %collective-permute-start.8 = (bf16[64,8192]{1,0:T(8,128)(2,1)}, bf16[64,8192]{1,0:T(8,128)(2,1)S(1)}, u32[]{:S(2)}, u32[]{:S(2)}) collective-permute-start(bf16[64,8192]{1,0:T(8,128)(2,1)} %forward_conv.1.own.delta), channel_id=1, source_target_pairs={{0,2},{1,3},{2,4},{3,5},{4,6},{5,7},{6,8},{7,9},{8,10},{9,11},{10,... | collective-permute-start | bytes 3145736 | tf_op jit(solution)/shard_map/ppermute | solution.py:303
  53.0 27.4 %collective-permute-start.9 = (bf16[64,8192]{1,0:T(8,128)(2,1)}, bf16[64,8192]{1,0:T(8,128)(2,1)S(1)}, u32[]{:S(2)}, u32[]{:S(2)}) collective-permute-start(bf16[64,8192]{1,0:T(8,128)(2,1)} %forward_conv.1.own.delta), channel_id=1, source_target_pairs={{2,0},{3,1},{4,2},{5,3},{6,4},{7,5},{8,6},{9,7},{10,8},{11,9},{12,... | collective-permute-start | bytes 3145736 | tf_op jit(solution)/shard_map/ppermute | solution.py:303
  55.9 33.8 %collective-permute-start = (bf16[2,9,9,9]{3,2,1,0:T(8,128)(2,1)S(1)}, bf16[2,9,9,9]{3,2,1,0:T(8,128)(2,1)}, u32[]{:S(2)}, u32[]{:S(2)}) collective-permute-start(bf16[2,9,9,9]{3,2,1,0:T(8,128)(2,1)S(1)} %copy_select_fusion), channel_id=1, source_target_pairs={{0,2},{1,3},{2,4},{3,5},{4,6},{5,7},{6,8},{7,9},{8,10},{9,11},{10,... | collective-permute-start | bytes 8756 | tf_op jit(solution)/shard_map/ppermute | solution.py:303
  59.3 43.0 %collective-permute-start.1 = (bf16[2,9,9,9]{3,2,1,0:T(8,128)(2,1)S(1)}, bf16[2,9,9,9]{3,2,1,0:T(8,128)(2,1)S(1)}, u32[]{:S(2)}, u32[]{:S(2)}) collective-permute-start(bf16[2,9,9,9]{3,2,1,0:T(8,128)(2,1)S(1)} %copy_select_fusion), channel_id=1, source_target_pairs={{0,1},{1,2},{2,3},{3,4},{4,5},{5,6},{6,7},{7,8},{8,9},{9,10},{10,1... | collective-permute-start | bytes 8756 | tf_op jit(solution)/shard_map/ppermute | solution.py:303
  61.2 66.2 %collective-permute-start.11 = (bf16[64,8192]{1,0:T(8,128)(2,1)}, bf16[64,8192]{1,0:T(8,128)(2,1)S(1)}, u32[]{:S(2)}, u32[]{:S(2)}) collective-permute-start(bf16[64,8192]{1,0:T(8,128)(2,1)} %forward_conv.1.own.delta), channel_id=1, source_target_pairs={{0,1},{1,0},{2,3},{3,2},{4,5},{5,4},{6,7},{7,6},{8,9},{9,8},{10,11... | collective-permute-start | bytes 3145736 | tf_op jit(solution)/shard_map/ppermute | solution.py:309
  75.0 6.4 %copy-start.4 = (bf16[9,32,32]{2,1,0:T(8,128)(2,1)S(1)}, bf16[9,32,32]{2,1,0:T(8,128)(2,1)}, u32[]{:S(2)}) copy-start(bf16[9,32,32]{2,1,0:T(8,128)(2,1)} %param.9) | copy-start | bytes 55300
  78.1 2.4 %copy-start = (bf16[64,8192]{1,0:T(8,128)(2,1)}, bf16[64,8192]{1,0:T(8,128)(2,1)S(1)}, u32[]{:S(2)}) copy-start(bf16[64,8192]{1,0:T(8,128)(2,1)S(1)} %collective-permute-done.8.low) | copy-start | bytes 3145732
  78.1 4.0 %collective-permute-start.12 = (f32[72,128]{1,0:T(8,128)}, f32[72,128]{1,0:T(8,128)}, u32[]{:S(2)}, u32[]{:S(2)}) collective-permute-start(f32[72,128]{1,0:T(8,128)} %weight_part.1), channel_id=1, source_target_pairs={{0,1},{1,0},{2,3},{3,2},{4,5},{5,4},{6,7},{7,6},{8,9},{9,8},{10,11... | collective-permute-start | bytes 110600 | tf_op jit(solution)/shard_map/ppermute | solution.py:309
  80.4 1.0 copy-start.1
  81.4 46.1 %collective-permute-start.10 = (bf16[64,8192]{1,0:T(8,128)(2,1)S(1)}, bf16[64,8192]{1,0:T(8,128)(2,1)}, u32[]{:S(2)}, u32[]{:S(2)}) collective-permute-start(bf16[64,8192]{1,0:T(8,128)(2,1)S(1)} %broadcast_select_fusion), channel_id=1, source_target_pairs={{0,1},{1,0},{2,3},{3,2},{4,5},{5,4},{6,7},{7,6},{8,9},{9,8},{10,11... | collective-permute-start | bytes 3145736 | tf_op jit(solution)/shard_map/ppermute | solution.py:309
  81.4 7.5 %copy-start.6 = (f32[72,128]{1,0:T(8,128)S(1)}, f32[72,128]{1,0:T(8,128)}, u32[]{:S(2)}) copy-start(f32[72,128]{1,0:T(8,128)} %weight_part.1) | copy-start | bytes 110596
  82.1 30.6 %collective-permute-start.2 = (bf16[2,9,9,9]{3,2,1,0:T(8,128)(2,1)S(1)}, bf16[2,9,9,9]{3,2,1,0:T(8,128)(2,1)S(1)}, u32[]{:S(2)}, u32[]{:S(2)}) collective-permute-start(bf16[2,9,9,9]{3,2,1,0:T(8,128)(2,1)S(1)} %copy_select_fusion), channel_id=1, source_target_pairs={{1,0},{2,1},{3,2},{4,3},{5,4},{6,5},{7,6},{8,7},{9,8},{10,9},{11,1... | collective-permute-start | bytes 8756 | tf_op jit(solution)/shard_map/ppermute | solution.py:303
  89.7 4.0 %collective-permute-start.13 = (f32[72,128]{1,0:T(8,128)S(1)}, f32[72,128]{1,0:T(8,128)S(1)}, u32[]{:S(2)}, u32[]{:S(2)}) collective-permute-start(f32[72,128]{1,0:T(8,128)S(1)} %add.30), channel_id=1, source_target_pairs={{0,8},{1,9},{2,10},{3,11},{4,12},{5,13},{6,14},{7,15},{8,0},{9,1},... | collective-permute-start | bytes 110600 | tf_op jit(solution)/shard_map/ppermute | solution.py:309
  93.7 23.5 %collective-permute-start.3 = (bf16[2,9,9,9]{3,2,1,0:T(8,128)(2,1)S(1)}, bf16[2,9,9,9]{3,2,1,0:T(8,128)(2,1)S(1)}, u32[]{:S(2)}, u32[]{:S(2)}) collective-permute-start(bf16[2,9,9,9]{3,2,1,0:T(8,128)(2,1)S(1)} %copy_select_fusion), channel_id=1, source_target_pairs={{2,0},{3,1},{4,2},{5,3},{6,4},{7,5},{8,6},{9,7},{10,8},{11,9},{12,... | collective-permute-start | bytes 8756 | tf_op jit(solution)/shard_map/ppermute | solution.py:303
  102.3 5.5 %collective-permute-start.14 = (f32[72,128]{1,0:T(8,128)S(1)}, f32[72,128]{1,0:T(8,128)S(1)}, u32[]{:S(2)}, u32[]{:S(2)}) collective-permute-start(f32[72,128]{1,0:T(8,128)S(1)} %add.31), channel_id=1, source_target_pairs={{0,16},{1,17},{2,18},{3,19},{4,20},{5,21},{6,22},{7,23},{8,24},{9,... | collective-permute-start | bytes 110600 | tf_op jit(solution)/shard_map/ppermute | solution.py:309
  107.8 4.0 %collective-permute-start.15 = (f32[72,128]{1,0:T(8,128)S(1)}, f32[72,128]{1,0:T(8,128)S(1)}, u32[]{:S(2)}, u32[]{:S(2)}) collective-permute-start(f32[72,128]{1,0:T(8,128)S(1)} %add.32), channel_id=1, source_target_pairs={{0,32},{1,33},{2,34},{3,35},{4,36},{5,37},{6,38},{7,39},{8,40},{9,... | collective-permute-start | bytes 110600 | tf_op jit(solution)/shard_map/ppermute | solution.py:309
  111.8 5.5 %collective-permute-start.16 = (f32[72,128]{1,0:T(8,128)S(1)}, f32[72,128]{1,0:T(8,128)S(1)}, u32[]{:S(2)}, u32[]{:S(2)}) collective-permute-start(f32[72,128]{1,0:T(8,128)S(1)} %add.33), channel_id=1, source_target_pairs={{0,64},{1,65},{2,66},{3,67},{4,68},{5,69},{6,70},{7,71},{8,72},{9,... | collective-permute-start | bytes 110600 | tf_op jit(solution)/shard_map/ppermute | solution.py:309
  117.3 4.0 %collective-permute-start.17 = (f32[72,128]{1,0:T(8,128)S(1)}, f32[72,128]{1,0:T(8,128)S(1)}, u32[]{:S(2)}, u32[]{:S(2)}) collective-permute-start(f32[72,128]{1,0:T(8,128)S(1)} %add.34), channel_id=1, source_target_pairs={{0,2},{1,3},{2,0},{3,1},{4,6},{5,7},{6,4},{7,5},{8,10},{9,11},{10,... | collective-permute-start | bytes 110600 | tf_op jit(solution)/shard_map/ppermute | solution.py:309
  121.2 5.5 %collective-permute-start.18 = (f32[72,128]{1,0:T(8,128)S(1)}, f32[72,128]{1,0:T(8,128)S(1)}, u32[]{:S(2)}, u32[]{:S(2)}) collective-permute-start(f32[72,128]{1,0:T(8,128)S(1)} %add.35), channel_id=1, source_target_pairs={{0,4},{1,5},{2,6},{3,7},{4,0},{5,1},{6,2},{7,3},{8,12},{9,13},{10,... | collective-permute-start | bytes 110600 | tf_op jit(solution)/shard_map/ppermute | solution.py:309
  127.5 1.0 copy-start.8

commit v2 on v1

--- a/solution.py
+++ b/solution.py
@@ -20,8 +20,8 @@
 OUT = 3 * BLOCK
 PAD = 128
 LANES = 128
-TILE = 1024
-VMEM = 56 * 1024 * 1024
+TILE = 2048
+VMEM = 28 * 1024 * 1024
 
 
 def spread_matrix(kind, shape):
@@ -63,43 +63,43 @@
     )(table, weights)
 
 
-def window_copies(blocks, x_ref, sems, parity, longitude):
+def window_copies(blocks, x_ref, sems, longitude):
+    parity = lax.rem(lax.axis_index("lat"), 2)
     far_row = pl.multiple_of(BLOCK + 2 * BLOCK * parity, BLOCK)
     mate_row = pl.multiple_of(3 * BLOCK - 2 * BLOCK * parity, BLOCK)
     rows = (0, far_row, 2 * BLOCK, mate_row, 4 * BLOCK)
     tiles = longitude // TILE
 
-    def tile_copies(tile):
-        first = pl.multiple_of(tile * TILE, TILE)
+    def copies(source, target, size, at):
         return [
             pltpu.make_async_copy(
-                block.at[:, pl.ds(first, TILE)],
-                x_ref.at[pl.ds(row, BLOCK), pl.ds(first + PAD, TILE)],
-                sems.at[place, tile],
+                block.at[:, pl.ds(source, size)],
+                x_ref.at[pl.ds(row, BLOCK), pl.ds(target, size)],
+                sems.at[place, at],
             )
             for place, (block, row) in enumerate(zip(blocks, rows))
         ]
 
-    def edge_copies():
-        copies = []
-        for place, (block, row) in enumerate(zip(blocks, rows)):
-            for side, (source, target) in enumerate(
-                ((longitude - PAD, 0), (0, longitude + PAD))
-            ):
-                copies.append(
-                    pltpu.make_async_copy(
-                        block.at[:, pl.ds(source, PAD)],
-                        x_ref.at[pl.ds(row, BLOCK), pl.ds(target, PAD)],
-                        sems.at[place, tiles + side],
-                    )
-                )
-        return copies
-
-    return tile_copies, edge_copies
+    main = [copies(tile * TILE, tile * TILE + PAD, TILE, tile) for tile in range(tiles)]
+    edges = copies(longitude - PAD, 0, PAD, tiles) + copies(0, longitude + PAD, PAD, tiles + 1)
+    return main, edges
+
+
+def start_all(main, edges):
+    for copy in main[0] + edges:
+        copy.start()
+    for some in main[1:]:
+        for copy in some:
+            copy.start()
+
+
+def wait_for(copies):
+    for copy in copies:
+        copy.wait()
 
 
 def pre_shift(x_ref, x3_ref, first):
-    wide = x_ref[:, pl.ds(first, TILE + 2 * PAD)]
+    wide = x_ref[:, first : first + TILE + 2 * PAD]
     for e in range(3):
         start = PAD + e - 1
         x3_ref[e * ROWS : (e + 1) * ROWS, :] = wide[:, start : start + TILE]
@@ -107,57 +107,56 @@
 
 def conv_kernel(with_act, matrix_ref, low, far, own, mate, high, *rest):
     if with_act:
-        cot_ref, out_ref, x_ref, x3_ref, p3_ref, sems = rest
+        cot_ref, out_ref, x_ref, x3_ref, p3_ref, o_ref, sems, out_sems = rest
     else:
-        out_ref, x_ref, x3_ref, p3_ref, sems = rest
+        out_ref, x_ref, x3_ref, p3_ref, o_ref, sems, out_sems = rest
     longitude = own.shape[1]
     tiles = longitude // TILE
-    parity = lax.rem(lax.axis_index("lat"), 2)
-    tile_copies, edge_copies = window_copies(
-        (low, far, own, mate, high), x_ref, sems, parity, longitude
-    )
-    for copy in edge_copies():
-        copy.start()
-
-    @pl.loop(0, tiles)
-    def _(tile):
-        for copy in tile_copies(tile):
-            copy.start()
-
-    for copy in edge_copies():
-        copy.wait()
-    for copy in tile_copies(0):
-        copy.wait()
-
-    @pl.loop(0, tiles)
-    def _(tile):
-        @pl.when(tile + 1 < tiles)
-        def _():
-            for copy in tile_copies(tile + 1):
-                copy.wait()
-
-        first = pl.multiple_of(tile * TILE, TILE)
-        pre_shift(x_ref, x3_ref, first)
-        p3_ref[:, pl.ds(first + PAD, TILE)] = jnp.dot(
-            matrix_ref[...], x3_ref[...], preferred_element_type=jnp.float32
-        )
-
-    p3_ref[:, 0:PAD] = p3_ref[:, longitude : longitude + PAD]
-    p3_ref[:, longitude + PAD : longitude + 2 * PAD] = p3_ref[:, PAD : 2 * PAD]
-
-    @pl.loop(0, tiles)
-    def _(tile):
-        first = pl.multiple_of(tile * TILE, TILE)
-        total = p3_ref[BLOCK : 2 * BLOCK, pl.ds(first + PAD, TILE)]
+    main, edges = window_copies((low, far, own, mate, high), x_ref, sems, longitude)
+    start_all(main, edges)
+    sends = []
+
+    def finish(first, last):
+        size = last - first
+        total = p3_ref[BLOCK : 2 * BLOCK, first + PAD : last + PAD]
         for f in (0, 2):
-            wide = p3_ref[f * BLOCK : (f + 1) * BLOCK, pl.ds(first, TILE + 2 * PAD)]
+            wide = p3_ref[f * BLOCK : (f + 1) * BLOCK, first : last + 2 * PAD]
             start = PAD + 3 * (f - 1)
-            total = total + wide[:, start : start + TILE]
+            total = total + wide[:, start : start + size]
         if with_act:
-            cot = cot_ref[:, pl.ds(first, TILE)].astype(jnp.float32)
+            cot = cot_ref[:, first:last].astype(jnp.float32)
             sg = jax.nn.sigmoid(total)
             total = cot * sg * (1.0 + total * (1.0 - sg))
-        out_ref[:, pl.ds(first, TILE)] = total.astype(out_ref.dtype)
+        o_ref[:, first:last] = total.astype(o_ref.dtype)
+
+    def send(first, last):
+        copy = pltpu.make_async_copy(
+            o_ref.at[:, first:last], out_ref.at[:, first:last], out_sems.at[len(sends)]
+        )
+        copy.start()
+        sends.append(copy)
+
+    wait_for(main[0] + edges)
+    for tile in range(tiles):
+        if tile + 1 < tiles:
+            wait_for(main[tile + 1])
+        first = tile * TILE
+        pre_shift(x_ref, x3_ref.at[tile % 2], first)
+        p3_ref[:, first + PAD : first + PAD + TILE] = jnp.dot(
+            matrix_ref[...], x3_ref[tile % 2], preferred_element_type=jnp.float32
+        )
+        if tile == 0:
+            p3_ref[:, longitude + PAD :] = p3_ref[:, PAD : 2 * PAD]
+        if tile == tiles - 1:
+            p3_ref[:, :PAD] = p3_ref[:, longitude : longitude + PAD]
+        if tile >= 1:
+            ready = (PAD if tile == 1 else first - TILE - PAD, first - PAD)
+            finish(*ready)
+            send(*ready)
+    for ready in ((longitude - TILE - PAD, longitude), (0, PAD)):
+        finish(*ready)
+        send(*ready)
+    wait_for(sends)
 
 
 def conv(matrix, blocks, cot=None):
@@ -170,12 +169,14 @@
         in_specs=[pl.BlockSpec(memory_space=pltpu.VMEM)]
         + [pl.BlockSpec(memory_space=pl.ANY)] * 5
         + [pl.BlockSpec(memory_space=pltpu.VMEM)] * len(extra),
-        out_specs=pl.BlockSpec(memory_space=pltpu.VMEM),
+        out_specs=pl.BlockSpec(memory_space=pl.ANY),
         scratch_shapes=[
             pltpu.VMEM((ROWS, longitude + 2 * PAD), jnp.bfloat16),
-            pltpu.VMEM((DEEP, TILE), jnp.bfloat16),
+            pltpu.VMEM((2, DEEP, TILE), jnp.bfloat16),
             pltpu.VMEM((OUT, longitude + 2 * PAD), jnp.float32),
+            pltpu.VMEM((BLOCK, longitude), jnp.bfloat16),
             pltpu.SemaphoreType.DMA((5, tiles + 2)),
+            pltpu.SemaphoreType.DMA((tiles + 1,)),
         ],
         compiler_params=pltpu.CompilerParams(vmem_limit_bytes=VMEM),
         cost_estimate=pl.CostEstimate(
@@ -187,13 +188,13 @@
     )(matrix, *blocks, *extra)
 
 
-def weight_kernel(scale, low, far, own, mate, high, delta, table_ref, out_ref, x_ref, x3_ref, d_ref, d3_ref, g_ref, w_ref, table_wide, sems, dsems):
+def weight_kernel(
+    scale, low, far, own, mate, high, delta, table_ref, out_ref,
+    x_ref, x3_ref, d_ref, d3_ref, g_ref, w_ref, table_wide, sems, dsems,
+):
     longitude = own.shape[1]
     tiles = longitude // TILE
-    parity = lax.rem(lax.axis_index("lat"), 2)
-    tile_copies, edge_copies = window_copies(
-        (low, far, own, mate, high), x_ref, sems, parity, longitude
-    )
+    main, edges = window_copies((low, far, own, mate, high), x_ref, sems, longitude)
     delta_copies = [
         pltpu.make_async_copy(
             delta.at[:, pl.ds(source, size)], d_ref.at[:, pl.ds(target, size)], dsems.at[at]
@@ -202,44 +203,34 @@
             ((0, PAD, longitude), (longitude - PAD, 0, PAD), (0, longitude + PAD, PAD))
         )
     ]
-    for copy in edge_copies() + delta_copies:
+    for copy in delta_copies:
         copy.start()
-
-    @pl.loop(0, tiles)
-    def _(tile):
-        for copy in tile_copies(tile):
-            copy.start()
-
+    start_all(main, edges)
     table_wide[...] = jnp.dot(
         table_ref[...],
         spread_matrix("table", (3 * SPAN, DEEP)),
         preferred_element_type=jnp.float32,
     )
-    g_ref[...] = jnp.zeros_like(g_ref)
-    for copy in edge_copies() + delta_copies:
-        copy.wait()
-    for copy in tile_copies(0):
-        copy.wait()
-
-    @pl.loop(0, tiles)
-    def _(tile):
-        @pl.when(tile + 1 < tiles)
-        def _():
-            for copy in tile_copies(tile + 1):
-                copy.wait()
-
-        first = pl.multiple_of(tile * TILE, TILE)
-        pre_shift(x_ref, x3_ref, first)
-        wide = d_ref[:, pl.ds(first, TILE + 2 * PAD)]
+    wait_for(main[0] + edges + delta_copies)
+    for tile in range(tiles):
+        if tile + 1 < tiles:
+            wait_for(main[tile + 1])
+        first = tile * TILE
+        pre_shift(x_ref, x3_ref.at[tile % 2], first)
+        wide = d_ref[:, first : first + TILE + 2 * PAD]
         for f in range(3):
             start = PAD - 3 * (f - 1)
-            d3_ref[f * BLOCK : (f + 1) * BLOCK, :] = wide[:, start : start + TILE]
-        g_ref[...] += lax.dot_general(
-            d3_ref[...],
-            x3_ref[...],
+            d3_ref[tile % 2, f * BLOCK : (f + 1) * BLOCK, :] = wide[:, start : start + TILE]
+        product = lax.dot_general(
+            d3_ref[tile % 2],
+            x3_ref[tile % 2],
             (((1,), (1,)), ((), ())),
             preferred_element_type=jnp.float32,
         )
+        if tile == 0:
+            g_ref[...] = product
+        else:
+            g_ref[...] += product
 
     whole = DEEP // LANES
     for k in range(K):
@@ -279,9 +270,9 @@
         out_specs=pl.BlockSpec(memory_space=pltpu.VMEM),
         scratch_shapes=[
             pltpu.VMEM((ROWS, longitude + 2 * PAD), jnp.bfloat16),
-            pltpu.VMEM((DEEP, TILE), jnp.bfloat16),
+            pltpu.VMEM((2, DEEP, TILE), jnp.bfloat16),
             pltpu.VMEM((BLOCK, longitude + 2 * PAD), jnp.bfloat16),
-            pltpu.VMEM((OUT, TILE), jnp.bfloat16),
+            pltpu.VMEM((2, OUT, TILE), jnp.bfloat16),
             pltpu.VMEM((OUT, DEEP), jnp.float32),
             pltpu.VMEM((K * C, LANES), jnp.float32),
             pltpu.VMEM((3 * OWN * K, DEEP), jnp.float32),
@@ -309,13 +300,21 @@
     return lax.ppermute(array, "lat", [(i, i ^ bit) for i in range(lax.axis_size("lat"))])
 
 
-def around(own):
-    low = moved(own, 2)
-    high = moved(own, -2)
-    mate = swapped(own)
+def around(own, low, high):
     parity = lax.rem(lax.axis_index("lat"), 2)
     far = swapped(jnp.where(parity == 0, high, low))
+    mate = swapped(own)
     return low, far, own, mate, high
+
+
+def chip_tables(masked):
+    parity = lax.rem(lax.axis_index("lat"), 2)
+    mate = swapped(masked)
+    pair = jnp.where(
+        parity == 0, jnp.concatenate([masked, mate]), jnp.concatenate([mate, masked])
+    )
+    whole = jnp.concatenate([moved(pair, 2), pair, moved(pair, -2)])
+    return lax.dynamic_slice_in_dim(whole, OWN * parity, SPAN, 0)
 
 
 def as_table(padded):
@@ -350,21 +349,29 @@
     inside = jnp.abs(offsets)[None, None, :] <= lon_reach[:, :, None]
     masked = jnp.where(inside[..., None], basis_table, jnp.zeros_like(basis_table))
 
-    feat = around(features.reshape(BLOCK, longitude))
+    own = features.reshape(BLOCK, longitude)
+    low, high = moved(own, 2), moved(own, -2)
     table = forward_table(masked)
     matrix = make_filter(table, weights.reshape(K * C, C))
-    masked_ext = jnp.concatenate(
-        [moved(masked, 2), moved(masked, 1), masked, moved(masked, -1), moved(masked, -2)], axis=0
-    )
+    masked_ext = chip_tables(masked)
+    low, high, own, matrix, masked_ext = lax.optimization_barrier(
+        (low, high, own, matrix, masked_ext)
+    )
+    feat = around(own, low, high)
     matrix_in = make_filter(
         input_table(masked_ext), jnp.transpose(weights, (0, 2, 1)).reshape(K * C, C)
     )
-
+    matrix, matrix_in = lax.optimization_barrier((matrix, matrix_in))
     delta = conv(matrix, feat, cotangent.reshape(BLOCK, longitude))
-    near = around(delta)
+
+    low, high = moved(delta, 2), moved(delta, -2)
     scale = 1.0 / math.sqrt(peers * OWN * longitude)
     total = weight_part(feat, delta, table, scale)
-    for bit in (1, 8, 16, 32, 64, 2, 4):
+    for bit in (1, 8, 16, 32, 64):
+        total = total + swapped(total, bit)
+    low, high, delta, total = lax.optimization_barrier((low, high, delta, total))
+    near = around(delta, low, high)
+    for bit in (2, 4):
         total = total + swapped(total, bit)
     grad_input = conv(matrix_in, near)
     return grad_input.reshape(OWN, C, longitude), total.reshape(K, C, C)

time: 141 us -> 122 us (0.87)
  the two profiles are of different devices: /device:TPU:56 before, /device:TPU:22 now
where the time goes in v2:
time: 122 us; the launch traced here: 121 us
  waiting for transfers between devices  49.1 us (40%)
  starting transfers between devices  32.8 us (27%)
  Pallas kernels  26.2 us (21%)
  local copies, waits for them, and re-layouts  6.28 us (5%)
  other arithmetic  5.68 us (5%)
    ppermute x12, waiting for transfers between devices, swapped(): lax.ppermute(array, 'lat', [(i, i ^ bit) for i in range(lax.axis_size('la...  31.1 us
    ppermute x6, starting transfers between devices, moved(): lax.ppermute(array, 'lat', [(i, i + by) for i in range(peers) if 0 <= i +...  22.1 us
    ppermute x6, waiting for transfers between devices, moved(): lax.ppermute(array, 'lat', [(i, i + by) for i in range(peers) if 0 <= i +...  18.1 us
    pallas_call x2, Pallas kernels, conv(): pl.pallas_call(functools.partial(conv_kernel, cot is not None), out_shape...  15.9 us
    ppermute x12, starting transfers between devices, swapped(): lax.ppermute(array, 'lat', [(i, i ^ bit) for i in range(lax.axis_size('la...  10.7 us
    pallas_call x1, Pallas kernels, weight_part(): pl.pallas_call(functools.partial(weight_kernel, scale), out_shape=jax.Sha...  8.73 us
    unnamed x10, local copies, waits for them, and re-layouts  3.31 us
  transfers between devices with their start and end apart: 18, of which 12 were waited for; matrix products, arithmetic and copies ran while one was open for 5% of the time, Pallas kernels for 9%

profile of v2, /device:TPU:22, one launch (start us, length us, event | category | flops | bytes accessed | tf_op | source)
XLA Modules:
  0.0 121.2 jit_solution(6623208402480186131)
XLA Ops:
  0.6 6.2 %collective-permute-start.1 = (bf16[64,8192]{1,0:T(8,128)(2,1)}, bf16[64,8192]{1,0:T(8,128)(2,1)S(1)}, u32[]{:S(2)}, u32[]{:S(2)}) collective-permute-start(bf16[64,8192]{1,0:T(8,128)(2,1)} %bitcast.own), channel_id=1, source_target_pairs={{2,0},{3,1},{4,2},{5,3},{6,4},{7,5},{8,6},{9,7},{10,8},{11,9},{12,... | collective-permute-start | bytes 3145736 | tf_op jit(solution)/shard_map/ppermute | solution.py:294
  6.9 1.9 %collective-permute-start = (bf16[64,8192]{1,0:T(8,128)(2,1)}, bf16[64,8192]{1,0:T(8,128)(2,1)S(1)}, u32[]{:S(2)}, u32[]{:S(2)}) collective-permute-start(bf16[64,8192]{1,0:T(8,128)(2,1)} %bitcast.own), channel_id=1, source_target_pairs={{0,2},{1,3},{2,4},{3,5},{4,6},{5,7},{6,8},{7,9},{8,10},{9,11},{10,... | collective-permute-start | bytes 3145736 | tf_op jit(solution)/shard_map/ppermute | solution.py:294
  8.9 0.9 copy_select_fusion
  9.8 0.1 collective-permute-start.2
  9.9 0.2 copy.31
  10.2 0.2 copy.32
  10.3 0.8 collective-permute-done.2
  11.2 6.0 %collective-permute-start.4 = (bf16[4,9,9,9]{3,2,1,0:T(8,128)(2,1)S(1)}, bf16[4,9,9,9]{3,2,1,0:T(8,128)(2,1)S(1)}, u32[]{:S(2)}, u32[]{:S(2)}) collective-permute-start(bf16[4,9,9,9]{3,2,1,0:T(8,128)(2,1)S(1)} %maximum_select_fusion), channel_id=1, source_target_pairs={{2,0},{3,1},{4,2},{5,3},{6,4},{7,5},{8,6},{9,7},{10,8},{11,9},{12,... | collective-permute-start | bytes 17504 | tf_op jit(solution)/shard_map/ppermute | solution.py:294
  17.2 1.9 %collective-permute-start.3 = (bf16[4,9,9,9]{3,2,1,0:T(8,128)(2,1)S(1)}, bf16[4,9,9,9]{3,2,1,0:T(8,128)(2,1)}, u32[]{:S(2)}, u32[]{:S(2)}) collective-permute-start(bf16[4,9,9,9]{3,2,1,0:T(8,128)(2,1)S(1)} %maximum_select_fusion), channel_id=1, source_target_pairs={{0,2},{1,3},{2,4},{3,5},{4,6},{5,7},{6,8},{7,9},{8,10},{9,11},{10,... | collective-permute-start | bytes 17504 | tf_op jit(solution)/shard_map/ppermute | solution.py:294
  19.2 0.1 reshape.75.table_ref
  19.3 0.7 copy-done.2
  20.1 0.8 make_filter.2.matrix_ref
  20.9 11.7 %collective-permute-done.4 = bf16[4,9,9,9]{3,2,1,0:T(8,128)(2,1)S(1)} collective-permute-done((bf16[4,9,9,9]{3,2,1,0:T(8,128)(2,1)S(1)}, bf16[4,9,9,9]{3,2,1,0:T(8,128)(2,1)S(1)}, u32[]{:S(2)}, u32[]{:S(2)}) %collective-permute-start.4) | collective-permute-done | bytes 5864 | tf_op jit(solution)/shard_map/ppermute | solution.py:294
  32.6 6.3 %collective-permute-done.3 = bf16[4,9,9,9]{3,2,1,0:T(8,128)(2,1)} collective-permute-done((bf16[4,9,9,9]{3,2,1,0:T(8,128)(2,1)S(1)}, bf16[4,9,9,9]{3,2,1,0:T(8,128)(2,1)}, u32[]{:S(2)}, u32[]{:S(2)}) %collective-permute-start.3) | collective-permute-done | bytes 5864 | tf_op jit(solution)/shard_map/ppermute | solution.py:294
  39.0 1.1 fusion.1
  40.1 1.1 broadcast_select_fusion.1
  41.2 0.5 collective-permute-start.6
  41.7 0.1 copy.28
  41.9 0.6 copy.26
  42.5 0.5 convert_reduce_fusion
  43.1 0.1 reshape.76.table_ref
  43.2 0.8 make_filter.3.matrix_ref
  44.0 0.2 collective-permute-done.5.far
  44.2 1.5 %collective-permute-done.6.mate = bf16[64,8192]{1,0:T(8,128)(2,1)} collective-permute-done((bf16[64,8192]{1,0:T(8,128)(2,1)}, bf16[64,8192]{1,0:T(8,128)(2,1)}, u32[]{:S(2)}, u32[]{:S(2)}) %collective-permute-start.6) | collective-permute-done | bytes 1048608 | tf_op jit(solution)/shard_map/ppermute | solution.py:300
  45.7 1.2 %copy-done.3 = bf16[2,32,8192]{2,1,0:T(8,128)(2,1)S(1)} copy-done((bf16[2,32,8192]{2,1,0:T(8,128)(2,1)S(1)}, bf16[2,32,8192]{2,1,0:T(8,128)(2,1)}, u32[]{:S(2)}) %copy-start.3) | copy-done | bytes 1048600
  46.9 8.3 %forward_conv.1.delta.own = bf16[64,8192]{1,0:T(8,128)(2,1)} custom-call(bf16[192,960]{1,0:T(8,128)(2,1)S(1)} %make_filter.2.matrix_ref, bf16[64,8192]{1,0:T(8,128)(2,1)S(1)} %collective-permute-done.low, bf16[64,8192]{1,0:T(8,128)(2,1)} %collective-permute-done.5.far, bf16[64,8192]{1,0:T(8,128)(2,1)} %bitcast.own, ...), custom_call_target="tpu_custom_call" | custom-call | flops 3019898880 | bytes 7340032 | tf_op jit(solution)/shard_map/forward_conv/pallas_call | solution.py:166
  55.2 1.9 %collective-permute-start.8 = (bf16[64,8192]{1,0:T(8,128)(2,1)}, bf16[64,8192]{1,0:T(8,128)(2,1)S(1)}, u32[]{:S(2)}, u32[]{:S(2)}) collective-permute-start(bf16[64,8192]{1,0:T(8,128)(2,1)} %forward_conv.1.delta.own), channel_id=1, source_target_pairs={{2,0},{3,1},{4,2},{5,3},{6,4},{7,5},{8,6},{9,7},{10,8},{11,9},{12,... | collective-permute-start | bytes 3145736 | tf_op jit(solution)/shard_map/ppermute | solution.py:294
  57.1 4.1 %collective-permute-start.7 = (bf16[64,8192]{1,0:T(8,128)(2,1)}, bf16[64,8192]{1,0:T(8,128)(2,1)S(1)}, u32[]{:S(2)}, u32[]{:S(2)}) collective-permute-start(bf16[64,8192]{1,0:T(8,128)(2,1)} %forward_conv.1.delta.own), channel_id=1, source_target_pairs={{0,2},{1,3},{2,4},{3,5},{4,6},{5,7},{6,8},{7,9},{8,10},{9,11},{10,... | collective-permute-start | bytes 3145736 | tf_op jit(solution)/shard_map/ppermute | solution.py:294
  61.3 8.7 %weight_part.1 = f32[72,128]{1,0:T(8,128)S(1)} custom-call(bf16[64,8192]{1,0:T(8,128)(2,1)S(1)} %collective-permute-done.low, bf16[64,8192]{1,0:T(8,128)(2,1)} %collective-permute-done.5.far, bf16[64,8192]{1,0:T(8,128)(2,1)} %bitcast.own, bf16[64,8192]{1,0:T(8,128)(2,1)} %collective-permute-done.6.mate, bf16[64,8192]{1,0:T(8,128)(2,1)S(1)} %collective-permute-done.1.high, ...), custom_call_target="tpu_custom_call" | custom-call | flops 3019898880 | bytes 6291456 | tf_op jit(solution)/shard_map/weight_part/pallas_call | solution.py:265
  70.1 1.2 collective-permute-done.9
  71.3 0.5 collective-permute-start.10
  71.8 9.3 %collective-permute-done.10 = f32[72,128]{1,0:T(8,128)S(1)} collective-permute-done((f32[72,128]{1,0:T(8,128)S(1)}, f32[72,128]{1,0:T(8,128)S(1)}, u32[]{:S(2)}, u32[]{:S(2)}) %collective-permute-start.10) | collective-permute-done | bytes 36896 | tf_op jit(solution)/shard_map/ppermute | solution.py:300
  81.1 1.1 collective-permute-start.11
  82.2 4.3 %collective-permute-done.11 = f32[72,128]{1,0:T(8,128)S(1)} collective-permute-done((f32[72,128]{1,0:T(8,128)S(1)}, f32[72,128]{1,0:T(8,128)S(1)}, u32[]{:S(2)}, u32[]{:S(2)}) %collective-permute-start.11) | collective-permute-done | bytes 36896 | tf_op jit(solution)/shard_map/ppermute | solution.py:300
  86.6 1.3 %collective-permute-start.12 = (f32[72,128]{1,0:T(8,128)S(1)}, f32[72,128]{1,0:T(8,128)S(1)}, u32[]{:S(2)}, u32[]{:S(2)}) collective-permute-start(f32[72,128]{1,0:T(8,128)S(1)} %add.36), channel_id=1, source_target_pairs={{0,32},{1,33},{2,34},{3,35},{4,36},{5,37},{6,38},{7,39},{8,40},{9,... | collective-permute-start | bytes 110600 | tf_op jit(solution)/shard_map/ppermute | solution.py:300
  87.9 2.7 %collective-permute-done.12 = f32[72,128]{1,0:T(8,128)S(1)} collective-permute-done((f32[72,128]{1,0:T(8,128)S(1)}, f32[72,128]{1,0:T(8,128)S(1)}, u32[]{:S(2)}, u32[]{:S(2)}) %collective-permute-start.12) | collective-permute-done | bytes 36896 | tf_op jit(solution)/shard_map/ppermute | solution.py:300
  90.6 0.3 collective-permute-start.13
  90.9 5.1 %collective-permute-done.13 = f32[72,128]{1,0:T(8,128)S(1)} collective-permute-done((f32[72,128]{1,0:T(8,128)S(1)}, f32[72,128]{1,0:T(8,128)S(1)}, u32[]{:S(2)}, u32[]{:S(2)}) %collective-permute-start.13) | collective-permute-done | bytes 36896 | tf_op jit(solution)/shard_map/ppermute | solution.py:300
  96.1 1.2 broadcast_select_fusion
  97.3 0.1 copy-done
  97.4 0.5 collective-permute-start.15
  97.9 4.0 %collective-permute-done.16 = f32[72,128]{1,0:T(8,128)S(1)} collective-permute-done((f32[72,128]{1,0:T(8,128)S(1)}, f32[72,128]{1,0:T(8,128)S(1)}, u32[]{:S(2)}, u32[]{:S(2)}) %collective-permute-start.16) | collective-permute-done | bytes 36896 | tf_op jit(solution)/shard_map/ppermute | solution.py:300
  101.8 6.2 %collective-permute-start.17 = (f32[72,128]{1,0:T(8,128)S(1)}, f32[72,128]{1,0:T(8,128)S(1)}, u32[]{:S(2)}, u32[]{:S(2)}) collective-permute-start(f32[72,128]{1,0:T(8,128)S(1)} %add.39), channel_id=1, source_target_pairs={{0,4},{1,5},{2,6},{3,7},{4,0},{5,1},{6,2},{7,3},{8,12},{9,13},{10,... | collective-permute-start | bytes 110600 | tf_op jit(solution)/shard_map/ppermute | solution.py:300
  108.1 1.9 %collective-permute-done.17 = f32[72,128]{1,0:T(8,128)S(1)} collective-permute-done((f32[72,128]{1,0:T(8,128)S(1)}, f32[72,128]{1,0:T(8,128)S(1)}, u32[]{:S(2)}, u32[]{:S(2)}) %collective-permute-start.17) | collective-permute-done | bytes 36896 | tf_op jit(solution)/shard_map/ppermute | solution.py:300
  110.0 0.6 add.40
  110.6 1.5 %reshape.72 = f32[9,32,32]{2,1,0:T(8,128)} reshape(f32[72,128]{1,0:T(8,128)} %add.40) | data formatting | bytes 73728 | tf_op jit(solution)/shard_map/reshape | solution.py:377
  112.2 1.2 %copy-done.1 = bf16[64,8192]{1,0:T(8,128)(2,1)S(1)} copy-done((bf16[64,8192]{1,0:T(8,128)(2,1)S(1)}, bf16[64,8192]{1,0:T(8,128)(2,1)}, u32[]{:S(2)}) %copy-start.1) | copy-done | bytes 1048600
  113.4 7.6 %input_conv.1 = bf16[64,8192]{1,0:T(8,128)(2,1)} custom-call(bf16[192,960]{1,0:T(8,128)(2,1)S(1)} %make_filter.3.matrix_ref, bf16[64,8192]{1,0:T(8,128)(2,1)S(1)} %copy-done.1, bf16[64,8192]{1,0:T(8,128)(2,1)S(1)} %collective-permute-done.14.far, bf16[64,8192]{1,0:T(8,128)(2,1)} %forward_conv.1.delta.own, bf16[64,8192]{1,0:T(8,128)(2,1)S(1)} %collective-permute-done.15.mate, ...), custom_call_target="tpu_custom_call" | custom-call | flops 3019898880 | bytes 7340032 | tf_op jit(solution)/shard_map/input_conv/pallas_call | solution.py:166
  (36 shorter events, 0.5 us)
Async XLA Ops:
  0.6 8.2 %copy-start.4 = (s32[2,9]{1,0:T(2,128)S(1)}, s32[2,9]{1,0:T(2,128)}, u32[]{:S(2)}) copy-start(s32[2,9]{1,0:T(2,128)} %param.8) | copy-start | bytes 220
  0.6 39.5 %collective-permute-start.1 = (bf16[64,8192]{1,0:T(8,128)(2,1)}, bf16[64,8192]{1,0:T(8,128)(2,1)S(1)}, u32[]{:S(2)}, u32[]{:S(2)}) collective-permute-start(bf16[64,8192]{1,0:T(8,128)(2,1)} %bitcast.own), channel_id=1, source_target_pairs={{2,0},{3,1},{4,2},{5,3},{6,4},{7,5},{8,6},{9,7},{10,8},{11,9},{12,... | collective-permute-start | bytes 3145736 | tf_op jit(solution)/shard_map/ppermute | solution.py:294
  6.9 33.3 %collective-permute-start = (bf16[64,8192]{1,0:T(8,128)(2,1)}, bf16[64,8192]{1,0:T(8,128)(2,1)S(1)}, u32[]{:S(2)}, u32[]{:S(2)}) collective-permute-start(bf16[64,8192]{1,0:T(8,128)(2,1)} %bitcast.own), channel_id=1, source_target_pairs={{0,2},{1,3},{2,4},{3,5},{4,6},{5,7},{6,8},{7,9},{8,10},{9,11},{10,... | collective-permute-start | bytes 3145736 | tf_op jit(solution)/shard_map/ppermute | solution.py:294
  9.8 1.3 %collective-permute-start.2 = (bf16[2,9,9,9]{3,2,1,0:T(8,128)(2,1)S(1)}, bf16[2,9,9,9]{3,2,1,0:T(8,128)(2,1)S(1)}, u32[]{:S(2)}, u32[]{:S(2)}) collective-permute-start(bf16[2,9,9,9]{3,2,1,0:T(8,128)(2,1)S(1)} %copy_select_fusion), channel_id=1, source_target_pairs={{0,1},{1,0},{2,3},{3,2},{4,5},{5,4},{6,7},{7,6},{8,9},{9,8},{10,11... | collective-permute-start | bytes 8756 | tf_op jit(solution)/shard_map/ppermute | solution.py:300
  11.2 21.5 %collective-permute-start.4 = (bf16[4,9,9,9]{3,2,1,0:T(8,128)(2,1)S(1)}, bf16[4,9,9,9]{3,2,1,0:T(8,128)(2,1)S(1)}, u32[]{:S(2)}, u32[]{:S(2)}) collective-permute-start(bf16[4,9,9,9]{3,2,1,0:T(8,128)(2,1)S(1)} %maximum_select_fusion), channel_id=1, source_target_pairs={{2,0},{3,1},{4,2},{5,3},{6,4},{7,5},{8,6},{9,7},{10,8},{11,9},{12,... | collective-permute-start | bytes 17504 | tf_op jit(solution)/shard_map/ppermute | solution.py:294
  17.2 21.7 %collective-permute-start.3 = (bf16[4,9,9,9]{3,2,1,0:T(8,128)(2,1)S(1)}, bf16[4,9,9,9]{3,2,1,0:T(8,128)(2,1)}, u32[]{:S(2)}, u32[]{:S(2)}) collective-permute-start(bf16[4,9,9,9]{3,2,1,0:T(8,128)(2,1)S(1)} %maximum_select_fusion), channel_id=1, source_target_pairs={{0,2},{1,3},{2,4},{3,5},{4,6},{5,7},{6,8},{7,9},{8,10},{9,11},{10,... | collective-permute-start | bytes 17504 | tf_op jit(solution)/shard_map/ppermute | solution.py:294
  19.2 0.9 copy-start.2
  41.2 3.0 %collective-permute-start.5 = (bf16[64,8192]{1,0:T(8,128)(2,1)}, bf16[64,8192]{1,0:T(8,128)(2,1)}, u32[]{:S(2)}, u32[]{:S(2)}) collective-permute-start(bf16[64,8192]{1,0:T(8,128)(2,1)} %broadcast_select_fusion.1), channel_id=1, source_target_pairs={{0,1},{1,0},{2,3},{3,2},{4,5},{5,4},{6,7},{7,6},{8,9},{9,8},{10,11... | collective-permute-start | bytes 3145736 | tf_op jit(solution)/shard_map/ppermute | solution.py:300
  41.2 4.5 %collective-permute-start.6 = (bf16[64,8192]{1,0:T(8,128)(2,1)}, bf16[64,8192]{1,0:T(8,128)(2,1)}, u32[]{:S(2)}, u32[]{:S(2)}) collective-permute-start(bf16[64,8192]{1,0:T(8,128)(2,1)} %bitcast.own), channel_id=1, source_target_pairs={{0,1},{1,0},{2,3},{3,2},{4,5},{5,4},{6,7},{7,6},{8,9},{9,8},{10,11... | collective-permute-start | bytes 3145736 | tf_op jit(solution)/shard_map/ppermute | solution.py:300
  45.7 1.2 %copy-start.3 = (bf16[2,32,8192]{2,1,0:T(8,128)(2,1)S(1)}, bf16[2,32,8192]{2,1,0:T(8,128)(2,1)}, u32[]{:S(2)}) copy-start(bf16[2,32,8192]{2,1,0:T(8,128)(2,1)} %param.6) | copy-start | bytes 3145732
  55.2 40.8 %collective-permute-start.8 = (bf16[64,8192]{1,0:T(8,128)(2,1)}, bf16[64,8192]{1,0:T(8,128)(2,1)S(1)}, u32[]{:S(2)}, u32[]{:S(2)}) collective-permute-start(bf16[64,8192]{1,0:T(8,128)(2,1)} %forward_conv.1.delta.own), channel_id=1, source_target_pairs={{2,0},{3,1},{4,2},{5,3},{6,4},{7,5},{8,6},{9,7},{10,8},{11,9},{12,... | collective-permute-start | bytes 3145736 | tf_op jit(solution)/shard_map/ppermute | solution.py:294
  57.1 38.9 %collective-permute-start.7 = (bf16[64,8192]{1,0:T(8,128)(2,1)}, bf16[64,8192]{1,0:T(8,128)(2,1)S(1)}, u32[]{:S(2)}, u32[]{:S(2)}) collective-permute-start(bf16[64,8192]{1,0:T(8,128)(2,1)} %forward_conv.1.delta.own), channel_id=1, source_target_pairs={{0,2},{1,3},{2,4},{3,5},{4,6},{5,7},{6,8},{7,9},{8,10},{9,11},{10,... | collective-permute-start | bytes 3145736 | tf_op jit(solution)/shard_map/ppermute | solution.py:294
  70.0 1.3 %collective-permute-start.9 = (f32[72,128]{1,0:T(8,128)S(1)}, f32[72,128]{1,0:T(8,128)S(1)}, u32[]{:S(2)}, u32[]{:S(2)}) collective-permute-start(f32[72,128]{1,0:T(8,128)S(1)} %weight_part.1), channel_id=1, source_target_pairs={{0,1},{1,0},{2,3},{3,2},{4,5},{5,4},{6,7},{7,6},{8,9},{9,8},{10,11... | collective-permute-start | bytes 110600 | tf_op jit(solution)/shard_map/ppermute | solution.py:300
  71.3 9.8 %collective-permute-start.10 = (f32[72,128]{1,0:T(8,128)S(1)}, f32[72,128]{1,0:T(8,128)S(1)}, u32[]{:S(2)}, u32[]{:S(2)}) collective-permute-start(f32[72,128]{1,0:T(8,128)S(1)} %add.34), channel_id=1, source_target_pairs={{0,8},{1,9},{2,10},{3,11},{4,12},{5,13},{6,14},{7,15},{8,0},{9,1},... | collective-permute-start | bytes 110600 | tf_op jit(solution)/shard_map/ppermute | solution.py:300
  81.1 5.5 %collective-permute-start.11 = (f32[72,128]{1,0:T(8,128)S(1)}, f32[72,128]{1,0:T(8,128)S(1)}, u32[]{:S(2)}, u32[]{:S(2)}) collective-permute-start(f32[72,128]{1,0:T(8,128)S(1)} %add.35), channel_id=1, source_target_pairs={{0,16},{1,17},{2,18},{3,19},{4,20},{5,21},{6,22},{7,23},{8,24},{9,... | collective-permute-start | bytes 110600 | tf_op jit(solution)/shard_map/ppermute | solution.py:300
  86.6 4.0 %collective-permute-start.12 = (f32[72,128]{1,0:T(8,128)S(1)}, f32[72,128]{1,0:T(8,128)S(1)}, u32[]{:S(2)}, u32[]{:S(2)}) collective-permute-start(f32[72,128]{1,0:T(8,128)S(1)} %add.36), channel_id=1, source_target_pairs={{0,32},{1,33},{2,34},{3,35},{4,36},{5,37},{6,38},{7,39},{8,40},{9,... | collective-permute-start | bytes 110600 | tf_op jit(solution)/shard_map/ppermute | solution.py:300
  90.6 5.5 %collective-permute-start.13 = (f32[72,128]{1,0:T(8,128)S(1)}, f32[72,128]{1,0:T(8,128)S(1)}, u32[]{:S(2)}, u32[]{:S(2)}) collective-permute-start(f32[72,128]{1,0:T(8,128)S(1)} %add.37), channel_id=1, source_target_pairs={{0,64},{1,65},{2,66},{3,67},{4,68},{5,69},{6,70},{7,71},{8,72},{9,... | collective-permute-start | bytes 110600 | tf_op jit(solution)/shard_map/ppermute | solution.py:300
  96.0 1.3 %copy-start = (bf16[64,8192]{1,0:T(8,128)(2,1)}, bf16[64,8192]{1,0:T(8,128)(2,1)S(1)}, u32[]{:S(2)}) copy-start(bf16[64,8192]{1,0:T(8,128)(2,1)S(1)} %collective-permute-done.7.low) | copy-start | bytes 3145732
  97.4 14.8 %collective-permute-start.14 = (bf16[64,8192]{1,0:T(8,128)(2,1)}, bf16[64,8192]{1,0:T(8,128)(2,1)S(1)}, u32[]{:S(2)}, u32[]{:S(2)}) collective-permute-start(bf16[64,8192]{1,0:T(8,128)(2,1)} %broadcast_select_fusion), channel_id=1, source_target_pairs={{0,1},{1,0},{2,3},{3,2},{4,5},{5,4},{6,7},{7,6},{8,9},{9,8},{10,11... | collective-permute-start | bytes 3145736 | tf_op jit(solution)/shard_map/ppermute | solution.py:300
  97.4 14.8 %collective-permute-start.15 = (bf16[64,8192]{1,0:T(8,128)(2,1)}, bf16[64,8192]{1,0:T(8,128)(2,1)S(1)}, u32[]{:S(2)}, u32[]{:S(2)}) collective-permute-start(bf16[64,8192]{1,0:T(8,128)(2,1)} %forward_conv.1.delta.own), channel_id=1, source_target_pairs={{0,1},{1,0},{2,3},{3,2},{4,5},{5,4},{6,7},{7,6},{8,9},{9,8},{10,11... | collective-permute-start | bytes 3145736 | tf_op jit(solution)/shard_map/ppermute | solution.py:300
  97.9 4.0 %collective-permute-start.16 = (f32[72,128]{1,0:T(8,128)S(1)}, f32[72,128]{1,0:T(8,128)S(1)}, u32[]{:S(2)}, u32[]{:S(2)}) collective-permute-start(f32[72,128]{1,0:T(8,128)S(1)} %add.38), channel_id=1, source_target_pairs={{0,2},{1,3},{2,0},{3,1},{4,6},{5,7},{6,4},{7,5},{8,10},{9,11},{10,... | collective-permute-start | bytes 110600 | tf_op jit(solution)/shard_map/ppermute | solution.py:300
  101.8 8.2 %collective-permute-start.17 = (f32[72,128]{1,0:T(8,128)S(1)}, f32[72,128]{1,0:T(8,128)S(1)}, u32[]{:S(2)}, u32[]{:S(2)}) collective-permute-start(f32[72,128]{1,0:T(8,128)S(1)} %add.39), channel_id=1, source_target_pairs={{0,4},{1,5},{2,6},{3,7},{4,0},{5,1},{6,2},{7,3},{8,12},{9,13},{10,... | collective-permute-start | bytes 110600 | tf_op jit(solution)/shard_map/ppermute | solution.py:300
  112.2 1.2 %copy-start.1 = (bf16[64,8192]{1,0:T(8,128)(2,1)S(1)}, bf16[64,8192]{1,0:T(8,128)(2,1)}, u32[]{:S(2)}) copy-start(bf16[64,8192]{1,0:T(8,128)(2,1)} %copy-done) | copy-start | bytes 3145732

commit v3 on v1

v3 whole, which is shorter than its diff:
```python
import functools
import math

import jax
import jax.numpy as jnp
from jax import lax
from jax.experimental import pallas as pl
from jax.experimental.pallas import tpu as pltpu
from jax.sharding import PartitionSpec as P

C = 32
K = 9
RAD = 4
TAPS = 9
OWN = 2
SPAN = OWN + 2 * RAD
CHIP = 2 * OWN
REACH = 3 * CHIP
BLOCK = OWN * C
STEP = 3 * BLOCK
DEEP = 3 * SPAN * C
OUT = 3 * BLOCK
PAD = 128
LANES = 128
VMEM = 24 * 1024 * 1024
SMALL = 8 * 1024 * 1024
LARGE = 58 * 1024 * 1024
ANY = pl.BlockSpec(memory_space=pl.ANY)
LOCAL = pl.BlockSpec(memory_space=pltpu.VMEM)


def core():
    return lax.rem(lax.axis_index("lat"), 2)


def spread_matrix(kind, shape):
    row = lax.broadcasted_iota(jnp.int32, shape, 0)
    lane = lax.broadcasted_iota(jnp.int32, shape, 1)
    hit = (lane // C == row) if kind == "table" else (lane % C == row)
    return jnp.where(hit, 1.0, 0.0).astype(jnp.bfloat16)


def filter_kernel(table_ref, weight_ref, out_ref, table_wide, weight_wide):
    table_wide[...] = jnp.dot(
        table_ref[...],
        spread_matrix("table", (3 * SPAN, DEEP)),
        preferred_element_type=jnp.float32,
    )
    weight_wide[...] = jnp.dot(
        weight_ref[...], spread_matrix("weight", (C, DEEP)), preferred_element_type=jnp.float32
    )
    for group in range(3 * CHIP):
        total = jnp.zeros((C, DEEP), jnp.float32)
        for k in range(K):
            at = group * K + k
            total = total + table_wide[at : at + 1, :] * weight_wide[k * C : (k + 1) * C, :]
        out_ref[group * C : (group + 1) * C, :] = total.astype(jnp.bfloat16)


def make_filter(table, weights):
    return pl.pallas_call(
        filter_kernel,
        out_shape=jax.ShapeDtypeStruct((2 * OUT, DEEP), jnp.bfloat16),
        in_specs=[LOCAL] * 2,
        out_specs=LOCAL,
        scratch_shapes=[
            pltpu.VMEM((3 * CHIP * K, DEEP), jnp.float32),
            pltpu.VMEM((K * C, DEEP), jnp.float32),
        ],
        compiler_params=pltpu.CompilerParams(vmem_limit_bytes=SMALL),
        name="make_filter",
    )(table, weights)


def wait_for(copies):
    for copy in copies:
        copy.wait()


def window_copies(own, mate, target, sems):
    longitude = own.shape[1]
    half = longitude // 2
    copies = []
    for side, (whole, place) in enumerate(((own, core()), (mate, 1 - core()))):
        row = pl.multiple_of(place * BLOCK, BLOCK)
        for at, (source, start, size) in enumerate(
            (
                (core() * half, PAD, half),
                (longitude - PAD - core() * half, 0, PAD),
                (half - core() * half, PAD + half, PAD),
            )
        ):
            copies.append(
                pltpu.make_async_copy(
                    whole.at[:, pl.ds(pl.multiple_of(source, PAD), size)],
                    target.at[pl.ds(row, BLOCK), pl.ds(start, size)],
                    sems.at[side, at],
                )
            )
    return copies


def window_kernel(own, mate, out_ref, sems):
    copies = window_copies(own, mate, out_ref, sems)
    for copy in copies:
        copy.start()
    wait_for(copies)


def chip_window(own, mate):
    return pl.pallas_call(
        window_kernel,
        out_shape=jax.ShapeDtypeStruct((2 * BLOCK, own.shape[1] // 2 + 2 * PAD), own.dtype),
        in_specs=[ANY, ANY],
        out_specs=LOCAL,
        scratch_shapes=[pltpu.SemaphoreType.DMA((2, 3))],
        compiler_params=pltpu.CompilerParams(vmem_limit_bytes=LARGE),
        name="chip_window",
    )(own, mate)


def join_kernel(got, whole, out, sem):
    half = whole.shape[1] // 2
    start = pl.multiple_of((1 - core()) * half, PAD)
    copy = pltpu.make_async_copy(got, out.at[:, pl.ds(start, half)], sem)
    copy.start()
    copy.wait()


def join(got, whole):
    return pl.pallas_call(
        join_kernel,
        out_shape=jax.ShapeDtypeStruct(whole.shape, whole.dtype),
        in_specs=[LOCAL, ANY],
        out_specs=ANY,
        scratch_shapes=[pltpu.SemaphoreType.DMA],
        input_output_aliases={1: 0},
        compiler_params=pltpu.CompilerParams(vmem_limit_bytes=VMEM),
        name="join",
    )(got, whole)


def in_parts(width):
    cut = width // 2 + PAD
    return ((0, cut), (cut, width - cut))


def chip_copies(blocks, width, x_ref, sems, start):
    cut = width // 2 + PAD
    return [
        [
            pltpu.make_async_copy(
                block.at[:, first : first + size],
                x_ref.at[
                    chip * 2 * BLOCK : (chip + 1) * 2 * BLOCK,
                    start + first : start + first + size,
                ],
                sems.at[at, chip],
            )
            for chip, block in enumerate(blocks)
        ]
        for at, (first, size) in enumerate(((0, cut), (cut, width - cut)))
    ]


def pre_shift(x_ref, x3_ref, first, size):
    for s in range(REACH):
        wide = x_ref[s * C : (s + 1) * C, first : first + size + 2 * PAD]
        for e in range(3):
            start = PAD + e - 1
            row = (3 * s + e) * C
            x3_ref[row : row + C, :] = wide[:, start : start + size]


def convolve(matrix_ref, x_ref, x3_ref, p3_ref, width, ready, finish):
    size = width // 2
    for tile in range(2):
        first = tile * size
        wait_for(ready[tile])
        pre_shift(x_ref, x3_ref.at[tile], first, size)
        for b in range(2):
            p3_ref[b * OUT : (b + 1) * OUT, first + PAD : first + PAD + size] = jnp.dot(
                matrix_ref[b * OUT : (b + 1) * OUT, :],
                x3_ref[tile, b * STEP : b * STEP + DEEP, :],
                preferred_element_type=jnp.float32,
            )
        finish(0 if tile == 0 else size - PAD, width if tile == 1 else size - PAD)


def post_shift(p3_ref, b, first, last):
    base = b * OUT
    total = p3_ref[base + BLOCK : base + 2 * BLOCK, first + PAD : last + PAD]
    for f in (0, 2):
        wide = p3_ref[base + f * BLOCK : base + (f + 1) * BLOCK, first : last + 2 * PAD]
        start = PAD + 3 * (f - 1)
        total = total + wide[:, start : start + last - first]
    return total


def forward_kernel(
    matrix_ref, table_ref, low, own, high, cot_own, cot_mate, out_ref, x_ref, x3_ref, p3_ref, cot_ref, sems, cot_sems
):
    width = own.shape[1]
    copies = chip_copies((low, own, high), width, x_ref, sems, PAD)
    cot_copies = window_copies(cot_own, cot_mate, cot_ref, cot_sems)
    out_ref[:C, width:] = table_ref[...]
    out_ref[C:, width:] = jnp.zeros((2 * BLOCK - C, LANES), out_ref.dtype)
    for copy in copies[0] + cot_copies + copies[1]:
        copy.start()

    def finish(first, last):
        if first == 0:
            wait_for(cot_copies)
        for b in range(2):
            rows = slice(b * BLOCK, (b + 1) * BLOCK)
            total = post_shift(p3_ref, b, first, last)
            cot = cot_ref[rows, first:last].astype(jnp.float32)
            sg = jax.nn.sigmoid(total)
            total = cot * sg * (1.0 + total * (1.0 - sg))
            out_ref[rows, first:last] = total.astype(out_ref.dtype)

    convolve(matrix_ref, x_ref, x3_ref, p3_ref, width, copies, finish)


def conv_scratch(width):
    return [
        pltpu.VMEM((REACH * C, width + 2 * PAD), jnp.bfloat16),
        pltpu.VMEM((2, 3 * REACH * C, width // 2), jnp.bfloat16),
        pltpu.VMEM((2 * OUT, width + 2 * PAD), jnp.float32),
    ]


def work(width, arrays):
    return pl.CostEstimate(
        flops=4 * OUT * DEEP * width,
        bytes_accessed=arrays * 2 * BLOCK * width * 2,
        transcendentals=0,
    )


def forward(matrix, chip_table, blocks, cots):
    width = blocks[0].shape[1]
    return pl.pallas_call(
        forward_kernel,
        out_shape=jax.ShapeDtypeStruct((2 * BLOCK, width + LANES), jnp.bfloat16),
        in_specs=[LOCAL] * 2 + [ANY] * 5,
        out_specs=LOCAL,
        scratch_shapes=conv_scratch(width)
        + [
            pltpu.VMEM((2 * BLOCK, width), jnp.bfloat16),
            pltpu.SemaphoreType.DMA((2, 3)),
            pltpu.SemaphoreType.DMA((2, 3)),
        ],
        compiler_params=pltpu.CompilerParams(vmem_limit_bytes=VMEM),
        cost_estimate=work(width, 5),
        name="forward_conv",
    )(matrix, chip_table, *blocks, *cots)


def input_filter(tables, weight_ref, matrix_ref, weight_wide, table_wide):
    weight_wide[...] = jnp.dot(
        weight_ref[...], spread_matrix("weight", (C, DEEP)), preferred_element_type=jnp.float32
    )
    row = lax.broadcasted_iota(jnp.int32, (3 * LANES, DEEP), 0)
    group = lax.broadcasted_iota(jnp.int32, (1, DEEP), 1) // C
    source = (group * 171) >> 9
    e = group - 3 * source
    for b in range(2):
        for q in range(OWN):
            whole = source + OWN * b
            tap = TAPS - 1 - source + q
            inside = jnp.logical_and(tap >= 0, tap < TAPS)
            wanted = (whole >> 2) * LANES + (whole & 3) * 3 * TAPS + 3 * tap + e
            wanted = jnp.where(inside, wanted, -1)
            picks = jnp.where(row == wanted, 1.0, 0.0).astype(jnp.bfloat16)
            table_wide[...] = jnp.dot(tables, picks, preferred_element_type=jnp.float32)
            for f in range(3):
                total = jnp.zeros((C, DEEP), jnp.float32)
                for k in range(K):
                    at = f * K + k
                    total = (
                        total
                        + table_wide[at : at + 1, :] * weight_wide[k * C : (k + 1) * C, :]
                    )
                first = b * OUT + f * BLOCK + q * C
                matrix_ref[first : first + C, :] = total.astype(jnp.bfloat16)


def backward_kernel(
    weight_ref, low, own, high, whole, give,
    x_ref, x3_ref, p3_ref, o_ref, t_ref, matrix_ref, weight_wide, table_wide,
    sems, table_sems, out_sems,
):
    width = own.shape[1] - LANES
    half = width - 2 * PAD
    table_copies = [
        pltpu.make_async_copy(
            block.at[0:C, width : width + LANES],
            t_ref.at[:, chip * LANES : (chip + 1) * LANES],
            table_sems.at[chip],
        )
        for chip, block in enumerate((low, own, high))
    ]
    copies = chip_copies((low, own, high), width, x_ref, sems, PAD)
    for copy in table_copies + copies[0] + copies[1]:
        copy.start()
    wait_for(table_copies)
    input_filter(t_ref[...], weight_ref, matrix_ref, weight_wide, table_wide)

    def finish(first, last):
        first, last = max(first, PAD), min(last, width - PAD)
        for b in range(2):
            total = post_shift(p3_ref, b, first, last)
            o_ref[b * BLOCK : (b + 1) * BLOCK, first - PAD : last - PAD] = total.astype(
                o_ref.dtype
            )

    convolve(matrix_ref, x_ref, x3_ref, p3_ref, width, copies, finish)
    mine = pl.multiple_of(core() * BLOCK, BLOCK)
    other = pl.multiple_of((1 - core()) * BLOCK, BLOCK)
    column = pl.multiple_of(core() * half, PAD)
    sends = [
        pltpu.make_async_copy(o_ref.at[pl.ds(other, BLOCK), :], give, out_sems.at[0]),
        pltpu.make_async_copy(
            o_ref.at[pl.ds(mine, BLOCK), :], whole.at[:, pl.ds(column, half)], out_sems.at[1]
        ),
    ]
    for copy in sends:
        copy.start()
    wait_for(sends)


def backward(weights, low, own, high):
    width = own.shape[1] - LANES
    half = width - 2 * PAD
    return pl.pallas_call(
        backward_kernel,
        out_shape=(
            jax.ShapeDtypeStruct((BLOCK, 2 * half), jnp.bfloat16),
            jax.ShapeDtypeStruct((BLOCK, half), jnp.bfloat16),
        ),
        in_specs=[LOCAL] + [ANY] * 3,
        out_specs=(ANY, ANY),
        scratch_shapes=conv_scratch(width)
        + [
            pltpu.VMEM((2 * BLOCK, half), jnp.bfloat16),
            pltpu.VMEM((C, 3 * LANES), jnp.bfloat16),
            pltpu.VMEM((2 * OUT, DEEP), jnp.bfloat16),
            pltpu.VMEM((K * C, DEEP), jnp.float32),
            pltpu.VMEM((C, DEEP), jnp.float32),
            pltpu.SemaphoreType.DMA((2, 3)),
            pltpu.SemaphoreType.DMA((3,)),
            pltpu.SemaphoreType.DMA((2,)),
        ],
        compiler_params=pltpu.CompilerParams(vmem_limit_bytes=VMEM + 2 * 1024 * 1024),
        cost_estimate=work(width, 4),
        name="input_conv",
    )(weights, low, own, high)


def weight_kernel(
    scale, low, own, high, delta, table_ref, out_ref,
    x_ref, x3_ref, d_ref, d3_ref, g_ref, w_ref, table_wide, sems, dsem,
):
    width = delta.shape[1] - LANES
    size = width // 2 - PAD
    copies = chip_copies((low, own, high), width, x_ref, sems, 0)
    copies[0].append(pltpu.make_async_copy(delta.at[:, 0:width], d_ref, dsem))
    for copy in copies[0] + copies[1]:
        copy.start()
    table_wide[...] = jnp.dot(
        table_ref[...],
        spread_matrix("table", (3 * SPAN, DEEP)),
        preferred_element_type=jnp.float32,
    )
    for tile in range(2):
        first = tile * size
        wait_for(copies[tile])
        pre_shift(x_ref, x3_ref.at[tile], first, size)
        wide = d_ref[:, first : first + size + 2 * PAD]
        for f in range(3):
            start = PAD - 3 * (f - 1)
            for b in range(2):
                row = b * OUT + f * BLOCK
                d3_ref[tile, row : row + BLOCK, :] = wide[
                    b * BLOCK : (b + 1) * BLOCK, start : start + size
                ]
        for b in range(2):
            rows = slice(b * OUT, (b + 1) * OUT)
            product = lax.dot_general(
                d3_ref[tile, rows, :],
                x3_ref[tile, b * STEP : b * STEP + DEEP, :],
                (((1,), (1,)), ((), ())),
                preferred_element_type=jnp.float32,
            )
            if tile == 0:
                g_ref[rows, :] = product
            else:
                g_ref[rows, :] += product

    whole = DEEP // LANES
    for k in range(K):
        total = jnp.zeros((C, DEEP), jnp.float32)
        for group in range(3 * CHIP):
            at = group * K + k
            total = total + table_wide[at : at + 1, :] * g_ref[group * C : (group + 1) * C, :]
        narrow = jnp.concatenate(
            [total[:, whole * LANES :], jnp.zeros((C, (whole + 1) * LANES - DEEP), jnp.float32)],
            axis=1,
        )
        for part in range(whole):
            narrow = narrow + total[:, part * LANES : (part + 1) * LANES]
        w_ref[k * C : (k + 1) * C, :] = narrow
    row = lax.broadcasted_iota(jnp.int32, (LANES, LANES), 0)
    lane = lax.broadcasted_iota(jnp.int32, (LANES, LANES), 1)
    result = jnp.zeros((K * C // 4, LANES), jnp.float32)
    for c in range(4):
        fold = jnp.where(lane == c * C + row % C, 1.0, 0.0)
        result = result + jnp.dot(
            w_ref[pl.ds(c, K * C // 4, stride=4), :],
            fold,
            preferred_element_type=jnp.float32,
            precision=lax.Precision.HIGHEST,
        )
    out_ref[...] = result * scale


def weight_part(blocks, delta, table, scale):
    width = delta.shape[1] - LANES
    return pl.pallas_call(
        functools.partial(weight_kernel, scale),
        out_shape=jax.ShapeDtypeStruct((K * C // 4, LANES), jnp.float32),
        in_specs=[ANY] * 4 + [LOCAL],
        out_specs=LOCAL,
        scratch_shapes=[
            pltpu.VMEM((REACH * C, width), jnp.bfloat16),
            pltpu.VMEM((2, 3 * REACH * C, width // 2 - PAD), jnp.bfloat16),
            pltpu.VMEM((2 * BLOCK, width), jnp.bfloat16),
            pltpu.VMEM((2, 2 * OUT, width // 2 - PAD), jnp.bfloat16),
            pltpu.VMEM((2 * OUT, DEEP), jnp.float32),
            pltpu.VMEM((K * C, LANES), jnp.float32),
            pltpu.VMEM((3 * CHIP * K, DEEP), jnp.float32),
            pltpu.SemaphoreType.DMA((2, 3)),
            pltpu.SemaphoreType.DMA,
        ],
        compiler_params=pltpu.CompilerParams(vmem_limit_bytes=VMEM),
        cost_estimate=work(width, 4),
        name="weight_part",
    )(*blocks, delta, table)


def moved(array, by):
    peers = lax.axis_size("lat")
    return lax.ppermute(
        array, "lat", [(i, i + by) for i in range(peers) if 0 <= i + by < peers]
    )


def swapped(array, bit=1):
    return lax.ppermute(array, "lat", [(i, i ^ bit) for i in range(lax.axis_size("lat"))])


def summed(part, bits):
    if len(bits) == 1:
        return part + swapped(part, bits[0])
    one, two = bits
    others = [swapped(part, bit) for bit in (one, two, one + two)]
    return (part + others[0]) + (others[1] + others[2])


def as_table(padded):
    parts = padded.reshape(2, OWN, SPAN, 3, 3, K)
    return jnp.transpose(parts, (0, 3, 1, 5, 2, 4)).reshape(3 * CHIP * K, 3 * SPAN)


def forward_table(pair):
    rows = pair.reshape(2, OWN, TAPS, TAPS, K)
    return as_table(
        jnp.stack(
            [
                jnp.pad(rows[:, r], ((0, 0), (r, SPAN - TAPS - r), (0, 0), (0, 0)))
                for r in range(OWN)
            ],
            axis=1,
        )
    )


def sent_table(pair):
    parts = pair[:, :, ::-1].reshape(CHIP, TAPS, 3, 3, K)
    flat = jnp.transpose(parts, (2, 4, 0, 1, 3)).reshape(3 * K, 3 * CHIP * TAPS)
    return jnp.pad(flat, ((0, C - 3 * K), (0, LANES - 3 * CHIP * TAPS)))


def body(features, cotangent, basis_table, lon_reach, weights):
    longitude = features.shape[2]
    peers = lax.axis_size("lat")

    own = features.reshape(BLOCK, longitude)
    cot_own = cotangent.reshape(BLOCK, longitude)
    own_mate = swapped(own)

    offsets = jnp.arange(TAPS, dtype=jnp.int32) - RAD
    inside = jnp.abs(offsets)[None, None, :] <= lon_reach[:, :, None]
    masked = jnp.where(inside[..., None], basis_table, jnp.zeros_like(basis_table))
    mate = swapped(masked)
    pair = jnp.where(
        core() == 0, jnp.concatenate([masked, mate]), jnp.concatenate([mate, masked])
    )
    window = chip_window(own, own_mate)
    low, high = moved(window, 2), moved(window, -2)
    cot_mate = swapped(cot_own)

    table = forward_table(pair)
    matrix = make_filter(table, weights.reshape(K * C, C))
    blocks, matrix, cot_mate = lax.optimization_barrier(
        ((low, window, high), matrix, cot_mate)
    )
    delta = forward(matrix, sent_table(pair), blocks, (cot_own, cot_mate))

    low, high = moved(delta, 2), moved(delta, -2)
    scale = 1.0 / math.sqrt(peers * OWN * longitude)
    total = weight_part(blocks, delta, table, scale)
    for bits in ((1,), (8, 16)):
        total = summed(total, bits)
    low, high, total = lax.optimization_barrier((low, high, total))
    turned = jnp.transpose(weights, (0, 2, 1)).reshape(K * C, C)
    whole, give = backward(turned, low, delta, high)
    got = swapped(give)
    for bits in ((32, 64), (2, 4)):
        total = summed(total, bits)
    grad_input = join(got, whole)
    return grad_input.reshape(OWN, C, longitude), total.reshape(K, C, C)


def solution(mesh):
    in_specs = (
        P("lat", None, None),
        P("lat", None, None),
        P("lat", None, None, None),
        P("lat", None),
        P(),
    )
    out_specs = (P("lat", None, None), P())
    return jax.shard_map(body, mesh=mesh, in_specs=in_specs, out_specs=out_specs, check_vma=False)
```

time: 141 us -> 113 us (0.80)
  the two profiles are of different devices: /device:TPU:56 before, /device:TPU:22 now
where the time goes in v3:
time: 113 us; the launch traced here: 111 us
  starting transfers between devices  32.1 us (28%)
  waiting for transfers between devices  31.9 us (28%)
  Pallas kernels  26 us (23%)
  local copies, waits for them, and re-layouts  18.7 us (17%)
  other arithmetic  1.26 us (1%)
    ppermute x14, waiting for transfers between devices, swapped(): lax.ppermute(array, 'lat', [(i, i ^ bit) for i in range(lax.axis_size('la...  23.9 us
    ppermute x4, starting transfers between devices, moved(): lax.ppermute(array, 'lat', [(i, i + by) for i in range(peers) if 0 <= i +...  16.7 us
    ppermute x14, starting transfers between devices, swapped(): lax.ppermute(array, 'lat', [(i, i ^ bit) for i in range(lax.axis_size('la...  15.4 us
    pallas_call x1, Pallas kernels, backward(): pl.pallas_call(backward_kernel, out_shape=(jax.ShapeDtypeStruct((BLOCK, 2...  8.36 us
    ppermute x4, waiting for transfers between devices, moved(): lax.ppermute(array, 'lat', [(i, i + by) for i in range(peers) if 0 <= i +...  8.06 us
    pallas_call x1, Pallas kernels, weight_part(): pl.pallas_call(functools.partial(weight_kernel, scale), out_shape=jax.Sha...  7.38 us
    unnamed x21, local copies, waits for them, and re-layouts  6.83 us
    pallas_call x1, Pallas kernels, forward(): pl.pallas_call(forward_kernel, out_shape=jax.ShapeDtypeStruct((2 * BLOCK,...  5.65 us
  transfers between devices with their start and end apart: 18, of which 8 were waited for; matrix products, arithmetic and copies ran while one was open for 12% of the time, Pallas kernels for 16%

profile of v3, /device:TPU:22, one launch (start us, length us, event | category | flops | bytes accessed | tf_op | source)
XLA Modules:
  0.0 111.1 jit_solution(11814575626517722586)
XLA Ops:
  0.7 2.9 %collective-permute-done.mate = bf16[64,8192]{1,0:T(8,128)(2,1)S(1)} collective-permute-done((bf16[64,8192]{1,0:T(8,128)(2,1)}, bf16[64,8192]{1,0:T(8,128)(2,1)S(1)}, u32[]{:S(2)}, u32[]{:S(2)}) %collective-permute-start) | collective-permute-done | bytes 1048608 | tf_op jit(solution)/shard_map/ppermute | solution.py:460
  3.6 1.0 copy-done.7
  4.6 2.3 %chip_window.1.own = bf16[128,4352]{1,0:T(8,128)(2,1)} custom-call(bf16[64,8192]{1,0:T(8,128)(2,1)} %bitcast.28, bf16[64,8192]{1,0:T(8,128)(2,1)} %copy-done.7), custom_call_target="tpu_custom_call" | custom-call | tf_op jit(solution)/shard_map/chip_window/pallas_call | solution.py:111
  6.9 4.0 %collective-permute-start.1 = (bf16[128,4352]{1,0:T(8,128)(2,1)}, bf16[128,4352]{1,0:T(8,128)(2,1)S(1)}, u32[]{:S(2)}, u32[]{:S(2)}) collective-permute-start(bf16[128,4352]{1,0:T(8,128)(2,1)} %chip_window.1.own), channel_id=1, source_target_pairs={{0,2},{1,3},{2,4},{3,5},{4,6},{5,7},{6,8},{7,9},{8,10},{9,11},{10,... | collective-permute-start | bytes 3342344 | tf_op jit(solution)/shard_map/ppermute | solution.py:454
  10.8 4.3 %collective-permute-start.2 = (bf16[128,4352]{1,0:T(8,128)(2,1)}, bf16[128,4352]{1,0:T(8,128)(2,1)S(1)}, u32[]{:S(2)}, u32[]{:S(2)}) collective-permute-start(bf16[128,4352]{1,0:T(8,128)(2,1)} %chip_window.1.own), channel_id=1, source_target_pairs={{2,0},{3,1},{4,2},{5,3},{6,4},{7,5},{8,6},{9,7},{10,8},{11,9},{12,... | collective-permute-start | bytes 3342344 | tf_op jit(solution)/shard_map/ppermute | solution.py:454
  15.3 0.1 copy.12
  15.5 0.2 broadcast_select_fusion
  15.6 0.6 collective-permute-start.3
  16.2 1.8 %collective-permute-done.3 = bf16[2,9,9,9]{3,0,2,1:T(2,128)(2,1)S(1)} collective-permute-done((bf16[2,9,9,9]{3,0,2,1:T(2,128)(2,1)S(1)}, bf16[2,9,9,9]{3,0,2,1:T(2,128)(2,1)S(1)}, u32[]{:S(2)}, u32[]{:S(2)}) %collective-permute-start.3) | collective-permute-done | bytes 2948 | tf_op jit(solution)/shard_map/ppermute | solution.py:460
  18.0 0.2 maximum_select_fusion
  18.2 0.7 rev.3
  18.8 0.8 fusion
  19.6 1.2 %copy.26 = bf16[2,1,9,9,9]{2,0,4,3,1:T(2,128)(2,1)S(1)} copy(bf16[2,1,9,9,9]{4,1,0,3,2:T(2,128)(2,1)} %get-tuple-element.22) | data formatting | bytes 5832 | tf_op jit(solution)/shard_map/squeeze | solution.py:481
  20.8 1.7 %copy.27 = bf16[2,1,9,9,9]{2,0,4,3,1:T(2,128)(2,1)} copy(bf16[2,1,9,9,9]{4,1,0,3,2:T(2,128)(2,1)} %get-tuple-element.23) | data formatting | bytes 5832 | tf_op jit(solution)/shard_map/squeeze | solution.py:481
  22.6 0.9 pad.13.clone
  23.5 0.8 maximum_bitcast_fusion
  24.3 1.9 %copy.17 = bf16[2,3,2,9,10,3]{3,2,1,0,5,4:T(2,128)(2,1)} copy(bf16[2,3,2,9,10,3]{4,0,3,5,1,2:T(2,128)(2,1)} %maximum_bitcast_fusion) | data formatting | bytes 12960 | tf_op jit(solution)/shard_map/transpose | solution.py:473
  26.1 1.0 reshape.50
  27.2 0.1 copy.18.table_ref
  27.3 1.6 %copy.29 = bf16[4,9,3,3,9]{4,2,3,1,0:T(4,128)(2,1)} copy(bf16[4,9,3,3,9]{4,0,3,2,1:T(4,128)(2,1)} %bitcast.31) | data formatting | bytes 11664 | tf_op jit(solution)/shard_map/reshape | solution.py:490
  28.9 1.0 reshape.54
  29.9 0.1 copy.20
  30.0 1.5 %make_filter.1.matrix_ref = bf16[384,960]{1,0:T(8,128)(2,1)S(1)} custom-call(bf16[108,30]{1,0:T(8,128)(2,1)S(1)} %copy.18.table_ref, bf16[288,32]{1,0:T(8,128)(2,1)S(1)} %bitcast.23), custom_call_target="tpu_custom_call" | custom-call | tf_op jit(solution)/shard_map/make_filter/pallas_call | solution.py:61
  31.5 6.8 %collective-permute-done.1.low = bf16[128,4352]{1,0:T(8,128)(2,1)S(1)} collective-permute-done((bf16[128,4352]{1,0:T(8,128)(2,1)}, bf16[128,4352]{1,0:T(8,128)(2,1)S(1)}, u32[]{:S(2)}, u32[]{:S(2)}) %collective-permute-start.1) | collective-permute-done | bytes 1114144 | tf_op jit(solution)/shard_map/ppermute | solution.py:454
  38.3 1.3 %collective-permute-done.2.high = bf16[128,4352]{1,0:T(8,128)(2,1)S(1)} collective-permute-done((bf16[128,4352]{1,0:T(8,128)(2,1)}, bf16[128,4352]{1,0:T(8,128)(2,1)S(1)}, u32[]{:S(2)}, u32[]{:S(2)}) %collective-permute-start.2) | collective-permute-done | bytes 1114144 | tf_op jit(solution)/shard_map/ppermute | solution.py:454
  39.6 1.0 copy-done.4
  40.6 1.2 %copy-done.5 = bf16[128,4352]{1,0:T(8,128)(2,1)S(1)} copy-done((bf16[128,4352]{1,0:T(8,128)(2,1)S(1)}, bf16[128,4352]{1,0:T(8,128)(2,1)}, u32[]{:S(2)}) %copy-start.5) | copy-done | bytes 1114136
  41.8 5.7 %forward_conv.1.delta.own = bf16[128,4480]{1,0:T(8,128)(2,1)S(1)} custom-call(bf16[384,960]{1,0:T(8,128)(2,1)S(1)} %make_filter.1.matrix_ref, bf16[32,128]{1,0:T(8,128)(2,1)S(1)} %pad.14.table_ref, bf16[128,4352]{1,0:T(8,128)(2,1)S(1)} %collective-permute-done.1.low, bf16[128,4352]{1,0:T(8,128)(2,1)S(1)} %copy-done, bf16[128,4352]{1,0:T(8,128)(2,1)S(1)} %copy-done.5, ...), custom_call_target="tpu_custom_call" | custom-call | flops 3208642560 | bytes 5570560 | tf_op jit(solution)/shard_map/forward_conv/pallas_call | solution.py:243
  47.5 1.0 copy-done.2
  48.5 3.5 %collective-permute-start.5 = (bf16[128,4480]{1,0:T(8,128)(2,1)S(1)}, bf16[128,4480]{1,0:T(8,128)(2,1)S(1)}, u32[]{:S(2)}, u32[]{:S(2)}) collective-permute-start(bf16[128,4480]{1,0:T(8,128)(2,1)S(1)} %forward_conv.1.delta.own), channel_id=1, source_target_pairs={{0,2},{1,3},{2,4},{3,5},{4,6},{5,7},{6,8},{7,9},{8,10},{9,11},{10,... | collective-permute-start | bytes 3440648 | tf_op jit(solution)/shard_map/ppermute | solution.py:454
  52.0 5.0 %collective-permute-start.6 = (bf16[128,4480]{1,0:T(8,128)(2,1)S(1)}, bf16[128,4480]{1,0:T(8,128)(2,1)}, u32[]{:S(2)}, u32[]{:S(2)}) collective-permute-start(bf16[128,4480]{1,0:T(8,128)(2,1)S(1)} %forward_conv.1.delta.own), channel_id=1, source_target_pairs={{2,0},{3,1},{4,2},{5,3},{6,4},{7,5},{8,6},{9,7},{10,8},{11,9},{12,... | collective-permute-start | bytes 3440648 | tf_op jit(solution)/shard_map/ppermute | solution.py:454
  57.0 1.2 %copy-done.3 = bf16[128,4352]{1,0:T(8,128)(2,1)S(1)} copy-done((bf16[128,4352]{1,0:T(8,128)(2,1)S(1)}, bf16[128,4352]{1,0:T(8,128)(2,1)}, u32[]{:S(2)}) %copy-start.3) | copy-done | bytes 1114136
  58.3 1.2 %copy-done.6 = bf16[128,4352]{1,0:T(8,128)(2,1)S(1)} copy-done((bf16[128,4352]{1,0:T(8,128)(2,1)S(1)}, bf16[128,4352]{1,0:T(8,128)(2,1)}, u32[]{:S(2)}) %copy-start.6) | copy-done | bytes 1114136
  59.5 7.4 %weight_part.1 = f32[72,128]{1,0:T(8,128)S(1)} custom-call(bf16[128,4352]{1,0:T(8,128)(2,1)S(1)} %copy-done.3, bf16[128,4352]{1,0:T(8,128)(2,1)S(1)} %copy-done, bf16[128,4352]{1,0:T(8,128)(2,1)S(1)} %copy-done.6, bf16[128,4480]{1,0:T(8,128)(2,1)S(1)} %forward_conv.1.delta.own, bf16[108,30]{1,0:T(8,128)(2,1)S(1)} %copy.18.table_ref), custom_call_target="tpu_custom_call" | custom-call | flops 3208642560 | bytes 4456448 | tf_op jit(solution)/shard_map/weight_part/pallas_call | solution.py:430
  67.0 1.2 %collective-permute-done.7 = f32[72,128]{1,0:T(8,128)S(1)} collective-permute-done((f32[72,128]{1,0:T(8,128)S(1)}, f32[72,128]{1,0:T(8,128)S(1)}, u32[]{:S(2)}, u32[]{:S(2)}) %collective-permute-start.7) | collective-permute-done | bytes 36896 | tf_op jit(solution)/shard_map/ppermute | solution.py:460
  68.2 4.4 %collective-permute-start.10 = (f32[72,128]{1,0:T(8,128)S(1)}, f32[72,128]{1,0:T(8,128)S(1)}, u32[]{:S(2)}, u32[]{:S(2)}) collective-permute-start(f32[72,128]{1,0:T(8,128)S(1)} %add.41), channel_id=1, source_target_pairs={{0,24},{1,25},{2,26},{3,27},{4,28},{5,29},{6,30},{7,31},{8,16},{9,... | collective-permute-start | bytes 110600 | tf_op jit(solution)/shard_map/ppermute | solution.py:460
  72.6 1.5 %collective-permute-start.9 = (f32[72,128]{1,0:T(8,128)S(1)}, f32[72,128]{1,0:T(8,128)S(1)}, u32[]{:S(2)}, u32[]{:S(2)}) collective-permute-start(f32[72,128]{1,0:T(8,128)S(1)} %add.41), channel_id=1, source_target_pairs={{0,16},{1,17},{2,18},{3,19},{4,20},{5,21},{6,22},{7,23},{8,24},{9,... | collective-permute-start | bytes 110600 | tf_op jit(solution)/shard_map/ppermute | solution.py:460
  74.1 0.1 copy.11
  74.3 12.9 %collective-permute-done.10 = f32[72,128]{1,0:T(8,128)S(1)} collective-permute-done((f32[72,128]{1,0:T(8,128)S(1)}, f32[72,128]{1,0:T(8,128)S(1)}, u32[]{:S(2)}, u32[]{:S(2)}) %collective-permute-start.10) | collective-permute-done | bytes 36896 | tf_op jit(solution)/shard_map/ppermute | solution.py:460
  87.2 1.8 %collective-permute-start.12 = (f32[72,128]{1,0:T(8,128)S(1)}, f32[72,128]{1,0:T(8,128)S(1)}, u32[]{:S(2)}, u32[]{:S(2)}) collective-permute-start(f32[72,128]{1,0:T(8,128)S(1)} %add_add_fusion.2), channel_id=1, source_target_pairs={{0,32},{1,33},{2,34},{3,35},{4,36},{5,37},{6,38},{7,39},{8,40},{9,... | collective-permute-start | bytes 110600 | tf_op jit(solution)/shard_map/ppermute | solution.py:460
  88.9 0.2 collective-permute-start.13
  89.1 1.6 %collective-permute-start.14 = (f32[72,128]{1,0:T(8,128)S(1)}, f32[72,128]{1,0:T(8,128)S(1)}, u32[]{:S(2)}, u32[]{:S(2)}) collective-permute-start(f32[72,128]{1,0:T(8,128)S(1)} %add_add_fusion.2), channel_id=1, source_target_pairs={{0,96},{1,97},{2,98},{3,99},{4,100},{5,101},{6,102},{7,103},{8,104... | collective-permute-start | bytes 110600 | tf_op jit(solution)/shard_map/ppermute | solution.py:460
  90.7 8.4 %input_conv.1 = (bf16[64,8192]{1,0:T(8,128)(2,1)}, bf16[64,4096]{1,0:T(8,128)(2,1)S(1)}) custom-call(bf16[288,32]{1,0:T(8,128)(2,1)S(1)} %bitcast.25, bf16[128,4480]{1,0:T(8,128)(2,1)S(1)} %collective-permute-done.5.low, bf16[128,4480]{1,0:T(8,128)(2,1)S(1)} %forward_conv.1.delta.own, bf16[128,4480]{1,0:T(8,128)(2,1)} %collective-permute-done.6.high), custom_call_target="tpu_custom_call" | custom-call | flops 3208642560 | bytes 4456448 | tf_op jit(solution)/shard_map/input_conv/pallas_call | solution.py:336
  99.3 4.9 %collective-permute-start.16 = (f32[72,128]{1,0:T(8,128)S(1)}, f32[72,128]{1,0:T(8,128)S(1)}, u32[]{:S(2)}, u32[]{:S(2)}) collective-permute-start(f32[72,128]{1,0:T(8,128)S(1)} %add_add_fusion.1), channel_id=1, source_target_pairs={{0,4},{1,5},{2,6},{3,7},{4,0},{5,1},{6,2},{7,3},{8,12},{9,13},{10,... | collective-permute-start | bytes 110600 | tf_op jit(solution)/shard_map/ppermute | solution.py:460
  104.2 2.6 %collective-permute-done.16 = f32[72,128]{1,0:T(8,128)S(1)} collective-permute-done((f32[72,128]{1,0:T(8,128)S(1)}, f32[72,128]{1,0:T(8,128)S(1)}, u32[]{:S(2)}, u32[]{:S(2)}) %collective-permute-start.16) | collective-permute-done | bytes 36896 | tf_op jit(solution)/shard_map/ppermute | solution.py:460
  106.8 2.5 %collective-permute-done.17 = f32[72,128]{1,0:T(8,128)S(1)} collective-permute-done((f32[72,128]{1,0:T(8,128)S(1)}, f32[72,128]{1,0:T(8,128)S(1)}, u32[]{:S(2)}, u32[]{:S(2)}) %collective-permute-start.17) | collective-permute-done | bytes 36896 | tf_op jit(solution)/shard_map/ppermute | solution.py:460
  109.4 0.8 reshape.56
  110.1 0.8 join.1
  (39 shorter events, 0.7 us)
Async XLA Ops:
  0.6 14.6 %copy-start.9 = (s32[2,9]{1,0:T(2,128)S(1)}, s32[2,9]{1,0:T(2,128)}, u32[]{:S(2)}) copy-start(s32[2,9]{1,0:T(2,128)} %param.8) | copy-start | bytes 220
  0.6 14.8 %copy-start.8 = (bf16[2,9,9,9]{3,0,2,1:T(2,128)(2,1)S(1)}, bf16[2,9,9,9]{3,0,2,1:T(2,128)(2,1)}, u32[]{:S(2)}) copy-start(bf16[2,9,9,9]{3,0,2,1:T(2,128)(2,1)} %param.7) | copy-start | bytes 8752
  0.6 3.0 %collective-permute-start = (bf16[64,8192]{1,0:T(8,128)(2,1)}, bf16[64,8192]{1,0:T(8,128)(2,1)S(1)}, u32[]{:S(2)}, u32[]{:S(2)}) collective-permute-start(bf16[64,8192]{1,0:T(8,128)(2,1)} %bitcast.27), channel_id=1, source_target_pairs={{0,1},{1,0},{2,3},{3,2},{4,5},{5,4},{6,7},{7,6},{8,9},{9,8},{10,11... | collective-permute-start | bytes 3145736 | tf_op jit(solution)/shard_map/ppermute | solution.py:460
  3.6 1.0 copy-start.7
  6.9 23.1 %copy-start.1 = (bf16[9,32,32]{2,1,0:T(8,128)(2,1)S(1)}, bf16[9,32,32]{2,1,0:T(8,128)(2,1)}, u32[]{:S(2)}) copy-start(bf16[9,32,32]{2,1,0:T(8,128)(2,1)} %param.9) | copy-start | bytes 55300
  6.9 31.4 %collective-permute-start.1 = (bf16[128,4352]{1,0:T(8,128)(2,1)}, bf16[128,4352]{1,0:T(8,128)(2,1)S(1)}, u32[]{:S(2)}, u32[]{:S(2)}) collective-permute-start(bf16[128,4352]{1,0:T(8,128)(2,1)} %chip_window.1.own), channel_id=1, source_target_pairs={{0,2},{1,3},{2,4},{3,5},{4,6},{5,7},{6,8},{7,9},{8,10},{9,11},{10,... | collective-permute-start | bytes 3342344 | tf_op jit(solution)/shard_map/ppermute | solution.py:454
  10.8 28.7 %collective-permute-start.2 = (bf16[128,4352]{1,0:T(8,128)(2,1)}, bf16[128,4352]{1,0:T(8,128)(2,1)S(1)}, u32[]{:S(2)}, u32[]{:S(2)}) collective-permute-start(bf16[128,4352]{1,0:T(8,128)(2,1)} %chip_window.1.own), channel_id=1, source_target_pairs={{2,0},{3,1},{4,2},{5,3},{6,4},{7,5},{8,6},{9,7},{10,8},{11,9},{12,... | collective-permute-start | bytes 3342344 | tf_op jit(solution)/shard_map/ppermute | solution.py:454
  15.2 16.4 %collective-permute-start.4 = (bf16[64,8192]{1,0:T(8,128)(2,1)}, bf16[64,8192]{1,0:T(8,128)(2,1)}, u32[]{:S(2)}, u32[]{:S(2)}) collective-permute-start(bf16[64,8192]{1,0:T(8,128)(2,1)} %bitcast.10.cot_own), channel_id=1, source_target_pairs={{0,1},{1,0},{2,3},{3,2},{4,5},{5,4},{6,7},{7,6},{8,9},{9,8},{10,11... | collective-permute-start | bytes 3145736 | tf_op jit(solution)/shard_map/ppermute | solution.py:460
  15.6 2.3 %collective-permute-start.3 = (bf16[2,9,9,9]{3,0,2,1:T(2,128)(2,1)S(1)}, bf16[2,9,9,9]{3,0,2,1:T(2,128)(2,1)S(1)}, u32[]{:S(2)}, u32[]{:S(2)}) collective-permute-start(bf16[2,9,9,9]{3,0,2,1:T(2,128)(2,1)S(1)} %broadcast_select_fusion), channel_id=1, source_target_pairs={{0,1},{1,0},{2,3},{3,2},{4,5},{5,4},{6,7},{7,6},{8,9},{9,8},{10,11... | collective-permute-start | bytes 8756 | tf_op jit(solution)/shard_map/ppermute | solution.py:460
  19.6 21.0 %copy-start = (bf16[128,4352]{1,0:T(8,128)(2,1)S(1)}, bf16[128,4352]{1,0:T(8,128)(2,1)}, u32[]{:S(2)}) copy-start(bf16[128,4352]{1,0:T(8,128)(2,1)} %chip_window.1.own) | copy-start | bytes 3342340
  39.6 1.0 copy-start.4
  40.6 1.2 %copy-start.5 = (bf16[128,4352]{1,0:T(8,128)(2,1)S(1)}, bf16[128,4352]{1,0:T(8,128)(2,1)}, u32[]{:S(2)}) copy-start(bf16[128,4352]{1,0:T(8,128)(2,1)} %copy-done.4) | copy-start | bytes 3342340
  47.5 1.0 copy-start.2
  48.5 38.6 %collective-permute-start.5 = (bf16[128,4480]{1,0:T(8,128)(2,1)S(1)}, bf16[128,4480]{1,0:T(8,128)(2,1)S(1)}, u32[]{:S(2)}, u32[]{:S(2)}) collective-permute-start(bf16[128,4480]{1,0:T(8,128)(2,1)S(1)} %forward_conv.1.delta.own), channel_id=1, source_target_pairs={{0,2},{1,3},{2,4},{3,5},{4,6},{5,7},{6,8},{7,9},{8,10},{9,11},{10,... | collective-permute-start | bytes 3440648 | tf_op jit(solution)/shard_map/ppermute | solution.py:454
  52.0 35.1 %collective-permute-start.6 = (bf16[128,4480]{1,0:T(8,128)(2,1)S(1)}, bf16[128,4480]{1,0:T(8,128)(2,1)}, u32[]{:S(2)}, u32[]{:S(2)}) collective-permute-start(bf16[128,4480]{1,0:T(8,128)(2,1)S(1)} %forward_conv.1.delta.own), channel_id=1, source_target_pairs={{2,0},{3,1},{4,2},{5,3},{6,4},{7,5},{8,6},{9,7},{10,8},{11,9},{12,... | collective-permute-start | bytes 3440648 | tf_op jit(solution)/shard_map/ppermute | solution.py:454
  57.0 1.2 %copy-start.3 = (bf16[128,4352]{1,0:T(8,128)(2,1)S(1)}, bf16[128,4352]{1,0:T(8,128)(2,1)}, u32[]{:S(2)}) copy-start(bf16[128,4352]{1,0:T(8,128)(2,1)} %copy-done.2) | copy-start | bytes 3342340
  58.3 1.2 %copy-start.6 = (bf16[128,4352]{1,0:T(8,128)(2,1)S(1)}, bf16[128,4352]{1,0:T(8,128)(2,1)}, u32[]{:S(2)}) copy-start(bf16[128,4352]{1,0:T(8,128)(2,1)} %copy-done.4) | copy-start | bytes 3342340
  66.9 1.3 %collective-permute-start.7 = (f32[72,128]{1,0:T(8,128)S(1)}, f32[72,128]{1,0:T(8,128)S(1)}, u32[]{:S(2)}, u32[]{:S(2)}) collective-permute-start(f32[72,128]{1,0:T(8,128)S(1)} %weight_part.1), channel_id=1, source_target_pairs={{0,1},{1,0},{2,3},{3,2},{4,5},{5,4},{6,7},{7,6},{8,9},{9,8},{10,11... | collective-permute-start | bytes 110600 | tf_op jit(solution)/shard_map/ppermute | solution.py:460
  68.2 18.9 %collective-permute-start.10 = (f32[72,128]{1,0:T(8,128)S(1)}, f32[72,128]{1,0:T(8,128)S(1)}, u32[]{:S(2)}, u32[]{:S(2)}) collective-permute-start(f32[72,128]{1,0:T(8,128)S(1)} %add.41), channel_id=1, source_target_pairs={{0,24},{1,25},{2,26},{3,27},{4,28},{5,29},{6,30},{7,31},{8,16},{9,... | collective-permute-start | bytes 110600 | tf_op jit(solution)/shard_map/ppermute | solution.py:460
  72.6 14.5 %collective-permute-start.8 = (f32[72,128]{1,0:T(8,128)S(1)}, f32[72,128]{1,0:T(8,128)S(1)}, u32[]{:S(2)}, u32[]{:S(2)}) collective-permute-start(f32[72,128]{1,0:T(8,128)S(1)} %add.41), channel_id=1, source_target_pairs={{0,8},{1,9},{2,10},{3,11},{4,12},{5,13},{6,14},{7,15},{8,0},{9,1},... | collective-permute-start | bytes 110600 | tf_op jit(solution)/shard_map/ppermute | solution.py:460
  72.6 14.5 %collective-permute-start.9 = (f32[72,128]{1,0:T(8,128)S(1)}, f32[72,128]{1,0:T(8,128)S(1)}, u32[]{:S(2)}, u32[]{:S(2)}) collective-permute-start(f32[72,128]{1,0:T(8,128)S(1)} %add.41), channel_id=1, source_target_pairs={{0,16},{1,17},{2,18},{3,19},{4,20},{5,21},{6,22},{7,23},{8,24},{9,... | collective-permute-start | bytes 110600 | tf_op jit(solution)/shard_map/ppermute | solution.py:460
  87.2 12.0 %collective-permute-start.12 = (f32[72,128]{1,0:T(8,128)S(1)}, f32[72,128]{1,0:T(8,128)S(1)}, u32[]{:S(2)}, u32[]{:S(2)}) collective-permute-start(f32[72,128]{1,0:T(8,128)S(1)} %add_add_fusion.2), channel_id=1, source_target_pairs={{0,32},{1,33},{2,34},{3,35},{4,36},{5,37},{6,38},{7,39},{8,40},{9,... | collective-permute-start | bytes 110600 | tf_op jit(solution)/shard_map/ppermute | solution.py:460
  88.9 10.2 %collective-permute-start.13 = (f32[72,128]{1,0:T(8,128)S(1)}, f32[72,128]{1,0:T(8,128)S(1)}, u32[]{:S(2)}, u32[]{:S(2)}) collective-permute-start(f32[72,128]{1,0:T(8,128)S(1)} %add_add_fusion.2), channel_id=1, source_target_pairs={{0,64},{1,65},{2,66},{3,67},{4,68},{5,69},{6,70},{7,71},{8,72},{9,... | collective-permute-start | bytes 110600 | tf_op jit(solution)/shard_map/ppermute | solution.py:460
  89.1 10.1 %collective-permute-start.14 = (f32[72,128]{1,0:T(8,128)S(1)}, f32[72,128]{1,0:T(8,128)S(1)}, u32[]{:S(2)}, u32[]{:S(2)}) collective-permute-start(f32[72,128]{1,0:T(8,128)S(1)} %add_add_fusion.2), channel_id=1, source_target_pairs={{0,96},{1,97},{2,98},{3,99},{4,100},{5,101},{6,102},{7,103},{8,104... | collective-permute-start | bytes 110600 | tf_op jit(solution)/shard_map/ppermute | solution.py:460
  99.1 11.0 %collective-permute-start.11 = (bf16[64,4096]{1,0:T(8,128)(2,1)S(1)}, bf16[64,4096]{1,0:T(8,128)(2,1)S(1)}, u32[]{:S(2)}, u32[]{:S(2)}) collective-permute-start(bf16[64,4096]{1,0:T(8,128)(2,1)S(1)} %get-tuple-element.19), channel_id=1, source_target_pairs={{0,1},{1,0},{2,3},{3,2},{4,5},{5,4},{6,7},{7,6},{8,9},{9,8},{10,11... | collective-permute-start | bytes 1572872 | tf_op jit(solution)/shard_map/ppermute | solution.py:460
  99.2 5.0 %collective-permute-start.15 = (f32[72,128]{1,0:T(8,128)S(1)}, f32[72,128]{1,0:T(8,128)S(1)}, u32[]{:S(2)}, u32[]{:S(2)}) collective-permute-start(f32[72,128]{1,0:T(8,128)S(1)} %add_add_fusion.1), channel_id=1, source_target_pairs={{0,2},{1,3},{2,0},{3,1},{4,6},{5,7},{6,4},{7,5},{8,10},{9,11},{10,... | collective-permute-start | bytes 110600 | tf_op jit(solution)/shard_map/ppermute | solution.py:460
  99.3 7.5 %collective-permute-start.16 = (f32[72,128]{1,0:T(8,128)S(1)}, f32[72,128]{1,0:T(8,128)S(1)}, u32[]{:S(2)}, u32[]{:S(2)}) collective-permute-start(f32[72,128]{1,0:T(8,128)S(1)} %add_add_fusion.1), channel_id=1, source_target_pairs={{0,4},{1,5},{2,6},{3,7},{4,0},{5,1},{6,2},{7,3},{8,12},{9,13},{10,... | collective-permute-start | bytes 110600 | tf_op jit(solution)/shard_map/ppermute | solution.py:460
  104.2 5.2 %collective-permute-start.17 = (f32[72,128]{1,0:T(8,128)S(1)}, f32[72,128]{1,0:T(8,128)S(1)}, u32[]{:S(2)}, u32[]{:S(2)}) collective-permute-start(f32[72,128]{1,0:T(8,128)S(1)} %add_add_fusion.1), channel_id=1, source_target_pairs={{0,6},{1,7},{2,4},{3,5},{4,2},{5,3},{6,0},{7,1},{8,14},{9,15},{10,... | collective-permute-start | bytes 110600 | tf_op jit(solution)/shard_map/ppermute | solution.py:460

commit v4 on v3

--- a/solution.py
+++ b/solution.py
@@ -114,7 +114,7 @@
         in_specs=[ANY, ANY],
         out_specs=LOCAL,
         scratch_shapes=[pltpu.SemaphoreType.DMA((2, 3))],
-        compiler_params=pltpu.CompilerParams(vmem_limit_bytes=LARGE),
+        compiler_params=pltpu.CompilerParams(vmem_limit_bytes=SMALL),
         name="chip_window",
     )(own, mate)
 
@@ -198,7 +198,8 @@
 
 
 def forward_kernel(
-    matrix_ref, table_ref, low, own, high, cot_own, cot_mate, out_ref, x_ref, x3_ref, p3_ref, cot_ref, sems, cot_sems
+    matrix_ref, table_ref, low, own, high, cot_own, cot_mate, out_ref, x_ref,
+    x3_ref, p3_ref, cot_ref, sems, cot_sems,
 ):
     width = own.shape[1]
     copies = chip_copies((low, own, high), width, x_ref, sems, PAD)
@@ -242,16 +243,19 @@
     width = blocks[0].shape[1]
     return pl.pallas_call(
         forward_kernel,
-        out_shape=jax.ShapeDtypeStruct((2 * BLOCK, width + LANES), jnp.bfloat16),
+        out_shape=(
+            jax.ShapeDtypeStruct((2 * BLOCK, width + LANES), jnp.bfloat16),
+            jax.ShapeDtypeStruct((REACH * C, width + 2 * PAD), jnp.bfloat16),
+        ),
         in_specs=[LOCAL] * 2 + [ANY] * 5,
-        out_specs=LOCAL,
-        scratch_shapes=conv_scratch(width)
+        out_specs=(LOCAL, LOCAL),
+        scratch_shapes=conv_scratch(width)[1:]
         + [
             pltpu.VMEM((2 * BLOCK, width), jnp.bfloat16),
             pltpu.SemaphoreType.DMA((2, 3)),
             pltpu.SemaphoreType.DMA((2, 3)),
         ],
-        compiler_params=pltpu.CompilerParams(vmem_limit_bytes=VMEM),
+        compiler_params=pltpu.CompilerParams(vmem_limit_bytes=VMEM - 4 * 1024 * 1024),
         cost_estimate=work(width, 5),
         name="forward_conv",
     )(matrix, chip_table, *blocks, *cots)
@@ -359,15 +363,10 @@
 
 
 def weight_kernel(
-    scale, low, own, high, delta, table_ref, out_ref,
-    x_ref, x3_ref, d_ref, d3_ref, g_ref, w_ref, table_wide, sems, dsem,
+    scale, x_ref, d_ref, table_ref, out_ref, x3_ref, d3_ref, g_ref, w_ref, table_wide
 ):
-    width = delta.shape[1] - LANES
+    width = d_ref.shape[1] - LANES
     size = width // 2 - PAD
-    copies = chip_copies((low, own, high), width, x_ref, sems, 0)
-    copies[0].append(pltpu.make_async_copy(delta.at[:, 0:width], d_ref, dsem))
-    for copy in copies[0] + copies[1]:
-        copy.start()
     table_wide[...] = jnp.dot(
         table_ref[...],
         spread_matrix("table", (3 * SPAN, DEEP)),
@@ -375,8 +374,7 @@
     )
     for tile in range(2):
         first = tile * size
-        wait_for(copies[tile])
-        pre_shift(x_ref, x3_ref.at[tile], first, size)
+        pre_shift(x_ref, x3_ref.at[tile], first + PAD, size)
         wide = d_ref[:, first : first + size + 2 * PAD]
         for f in range(3):
             start = PAD - 3 * (f - 1)
@@ -425,28 +423,24 @@
     out_ref[...] = result * scale
 
 
-def weight_part(blocks, delta, table, scale):
+def weight_part(joined, delta, table, scale):
     width = delta.shape[1] - LANES
     return pl.pallas_call(
         functools.partial(weight_kernel, scale),
         out_shape=jax.ShapeDtypeStruct((K * C // 4, LANES), jnp.float32),
-        in_specs=[ANY] * 4 + [LOCAL],
+        in_specs=[LOCAL] * 3,
         out_specs=LOCAL,
         scratch_shapes=[
-            pltpu.VMEM((REACH * C, width), jnp.bfloat16),
             pltpu.VMEM((2, 3 * REACH * C, width // 2 - PAD), jnp.bfloat16),
-            pltpu.VMEM((2 * BLOCK, width), jnp.bfloat16),
             pltpu.VMEM((2, 2 * OUT, width // 2 - PAD), jnp.bfloat16),
             pltpu.VMEM((2 * OUT, DEEP), jnp.float32),
             pltpu.VMEM((K * C, LANES), jnp.float32),
             pltpu.VMEM((3 * CHIP * K, DEEP), jnp.float32),
-            pltpu.SemaphoreType.DMA((2, 3)),
-            pltpu.SemaphoreType.DMA,
         ],
-        compiler_params=pltpu.CompilerParams(vmem_limit_bytes=VMEM),
+        compiler_params=pltpu.CompilerParams(vmem_limit_bytes=VMEM - 6 * 1024 * 1024),
         cost_estimate=work(width, 4),
         name="weight_part",
-    )(*blocks, delta, table)
+    )(joined, delta, table)
 
 
 def moved(array, by):
@@ -513,21 +507,20 @@
 
     table = forward_table(pair)
     matrix = make_filter(table, weights.reshape(K * C, C))
-    blocks, matrix, cot_mate = lax.optimization_barrier(
-        ((low, window, high), matrix, cot_mate)
-    )
-    delta = forward(matrix, sent_table(pair), blocks, (cot_own, cot_mate))
+    delta, joined = forward(
+        matrix, sent_table(pair), (low, window, high), (cot_own, cot_mate)
+    )
 
     low, high = moved(delta, 2), moved(delta, -2)
     scale = 1.0 / math.sqrt(peers * OWN * longitude)
-    total = weight_part(blocks, delta, table, scale)
-    for bits in ((1,), (8, 16)):
+    total = weight_part(joined, delta, table, scale)
+    for bits in ((1,), (32, 64)):
         total = summed(total, bits)
     low, high, total = lax.optimization_barrier((low, high, total))
     turned = jnp.transpose(weights, (0, 2, 1)).reshape(K * C, C)
     whole, give = backward(turned, low, delta, high)
     got = swapped(give)
-    for bits in ((32, 64), (2, 4)):
+    for bits in ((8, 16), (2, 4)):
         total = summed(total, bits)
     grad_input = join(got, whole)
     return grad_input.reshape(OWN, C, longitude), total.reshape(K, C, C)

time: 113 us -> 109 us (0.965); the launches traced: 111 us -> 108 us
  waiting for transfers between devices: 31.9 us -> 38.4 us
  local copies, waits for them, and re-layouts: 18.7 us -> 12.5 us
  Pallas kernels: 26 us -> 23.4 us
  starting transfers between devices: 32.1 us -> 30.8 us
    ppermute x14, waiting for transfers between devices: 23.9 us -> 28.6 us  [swapped(): lax.ppermute(array, 'lat', [(i, i ^ bit) for i in range(lax.axis_size('la...]
    unnamed x21 -> x13, local copies, waits for them, and re-layouts: 6.83 us -> 3.6 us
    pallas_call x1, Pallas kernels: 2.29 us -> 0.15 us  [chip_window(): pl.pallas_call(window_kernel, out_shape=jax.ShapeDtypeStruct((2 * BLOCK,...]
    ppermute x4, waiting for transfers between devices: 8.06 us -> 9.77 us  [moved(): lax.ppermute(array, 'lat', [(i, i + by) for i in range(peers) if 0 <= i +...]
    ppermute x14, starting transfers between devices: 15.4 us -> 13.9 us  [swapped(): lax.ppermute(array, 'lat', [(i, i ^ bit) for i in range(lax.axis_size('la...]
  transfers between devices with their start and end apart: 18 -> 18, of which waited for: 8 -> 9; matrix products, arithmetic and copies ran while one was open for 12% -> 10% of each run, Pallas kernels for 16% -> 15%
where the time goes in v4:
time: 109 us; the launch traced here: 108 us
  waiting for transfers between devices  38.4 us (35%)
  starting transfers between devices  30.8 us (28%)
  Pallas kernels  23.4 us (21%)
  local copies, waits for them, and re-layouts  12.5 us (11%)
  other arithmetic  2.12 us (2%)
  between operations  1.1 us (1%)
    ppermute x14, waiting for transfers between devices, swapped(): lax.ppermute(array, 'lat', [(i, i ^ bit) for i in range(lax.axis_size('la...  28.6 us
    ppermute x4, starting transfers between devices, moved(): lax.ppermute(array, 'lat', [(i, i + by) for i in range(peers) if 0 <= i +...  16.9 us
    ppermute x14, starting transfers between devices, swapped(): lax.ppermute(array, 'lat', [(i, i ^ bit) for i in range(lax.axis_size('la...  13.9 us
    ppermute x4, waiting for transfers between devices, moved(): lax.ppermute(array, 'lat', [(i, i + by) for i in range(peers) if 0 <= i +...  9.77 us
    pallas_call x1, Pallas kernels, backward(): pl.pallas_call(backward_kernel, out_shape=(jax.ShapeDtypeStruct((BLOCK, 2...  8.36 us
    pallas_call x1, Pallas kernels, weight_part(): pl.pallas_call(functools.partial(weight_kernel, scale), out_shape=jax.Sha...  6.8 us
    pallas_call x1, Pallas kernels, forward(): pl.pallas_call(forward_kernel, out_shape=(jax.ShapeDtypeStruct((2 * BLOCK...  5.8 us
    unnamed x13, local copies, waits for them, and re-layouts  3.6 us
  transfers between devices with their start and end apart: 18, of which 9 were waited for; matrix products, arithmetic and copies ran while one was open for 10% of the time, Pallas kernels for 15%

profile of v4, /device:TPU:22, one launch (start us, length us, event | category | flops | bytes accessed | tf_op | source)
XLA Modules:
  0.0 108.3 jit_solution(18197862820129409025)
XLA Ops:
  0.7 2.9 %collective-permute-done.1.mate = bf16[64,8192]{1,0:T(8,128)(2,1)S(1)} collective-permute-done((bf16[64,8192]{1,0:T(8,128)(2,1)}, bf16[64,8192]{1,0:T(8,128)(2,1)S(1)}, u32[]{:S(2)}, u32[]{:S(2)}) %collective-permute-start.1) | collective-permute-done | bytes 1048608 | tf_op jit(solution)/shard_map/ppermute | solution.py:454
  3.6 1.2 %copy-done = bf16[2,32,8192]{2,1,0:T(8,128)(2,1)S(1)} copy-done((bf16[2,32,8192]{2,1,0:T(8,128)(2,1)S(1)}, bf16[2,32,8192]{2,1,0:T(8,128)(2,1)}, u32[]{:S(2)}) %copy-start) | copy-done | bytes 1048600
  4.8 0.2 chip_window.1.own
  5.0 4.0 %collective-permute-start.2 = (bf16[128,4352]{1,0:T(8,128)(2,1)S(1)}, bf16[128,4352]{1,0:T(8,128)(2,1)S(1)}, u32[]{:S(2)}, u32[]{:S(2)}) collective-permute-start(bf16[128,4352]{1,0:T(8,128)(2,1)S(1)} %chip_window.1.own), channel_id=1, source_target_pairs={{0,2},{1,3},{2,4},{3,5},{4,6},{5,7},{6,8},{7,9},{8,10},{9,11},{10,... | collective-permute-start | bytes 3342344 | tf_op jit(solution)/shard_map/ppermute | solution.py:448
  9.0 4.3 %collective-permute-start.3 = (bf16[128,4352]{1,0:T(8,128)(2,1)S(1)}, bf16[128,4352]{1,0:T(8,128)(2,1)S(1)}, u32[]{:S(2)}, u32[]{:S(2)}) collective-permute-start(bf16[128,4352]{1,0:T(8,128)(2,1)S(1)} %chip_window.1.own), channel_id=1, source_target_pairs={{2,0},{3,1},{4,2},{5,3},{6,4},{7,5},{8,6},{9,7},{10,8},{11,9},{12,... | collective-permute-start | bytes 3342344 | tf_op jit(solution)/shard_map/ppermute | solution.py:448
  13.3 0.1 collective-permute-start.4
  13.4 0.1 copy.12
  13.6 0.2 broadcast_select_fusion
  13.7 0.6 collective-permute-start
  14.3 1.9 %collective-permute-done = bf16[2,9,9,9]{3,0,2,1:T(2,128)(2,1)} collective-permute-done((bf16[2,9,9,9]{3,0,2,1:T(2,128)(2,1)S(1)}, bf16[2,9,9,9]{3,0,2,1:T(2,128)(2,1)}, u32[]{:S(2)}, u32[]{:S(2)}) %collective-permute-start) | collective-permute-done | bytes 2948 | tf_op jit(solution)/shard_map/ppermute | solution.py:454
  16.2 1.1 maximum_select_fusion
  17.3 0.7 rev.3
  17.9 0.8 fusion
  18.7 1.1 %copy.26 = bf16[2,1,9,9,9]{2,0,4,3,1:T(2,128)(2,1)S(1)} copy(bf16[2,1,9,9,9]{4,1,0,3,2:T(2,128)(2,1)} %get-tuple-element.16) | data formatting | bytes 5832 | tf_op jit(solution)/shard_map/squeeze | solution.py:475
  19.8 1.1 %copy.27 = bf16[2,1,9,9,9]{2,0,4,3,1:T(2,128)(2,1)S(1)} copy(bf16[2,1,9,9,9]{4,1,0,3,2:T(2,128)(2,1)} %get-tuple-element.17) | data formatting | bytes 5832 | tf_op jit(solution)/shard_map/squeeze | solution.py:475
  21.0 0.1 pad.13.clone
  21.1 0.8 maximum_bitcast_fusion
  21.9 1.2 %copy.17 = bf16[2,3,2,9,10,3]{3,2,1,0,5,4:T(2,128)(2,1)S(1)} copy(bf16[2,3,2,9,10,3]{4,0,3,5,1,2:T(2,128)(2,1)} %maximum_bitcast_fusion) | data formatting | bytes 12960 | tf_op jit(solution)/shard_map/transpose | solution.py:467
  23.1 0.1 reshape.49
  23.2 0.1 copy.18.table_ref
  23.4 1.6 %copy.29 = bf16[4,9,3,3,9]{4,2,3,1,0:T(4,128)(2,1)} copy(bf16[4,9,3,3,9]{4,0,3,2,1:T(4,128)(2,1)} %bitcast.31) | data formatting | bytes 11664 | tf_op jit(solution)/shard_map/reshape | solution.py:484
  25.0 1.0 reshape.52
  26.0 0.1 copy.20
  26.1 1.5 %make_filter.1.matrix_ref = bf16[384,960]{1,0:T(8,128)(2,1)S(1)} custom-call(bf16[108,30]{1,0:T(8,128)(2,1)S(1)} %copy.18.table_ref, bf16[288,32]{1,0:T(8,128)(2,1)S(1)} %bitcast.25), custom_call_target="tpu_custom_call" | custom-call | tf_op jit(solution)/shard_map/make_filter/pallas_call | solution.py:61
  27.6 8.6 %collective-permute-done.2.low = bf16[128,4352]{1,0:T(8,128)(2,1)S(1)} collective-permute-done((bf16[128,4352]{1,0:T(8,128)(2,1)S(1)}, bf16[128,4352]{1,0:T(8,128)(2,1)S(1)}, u32[]{:S(2)}, u32[]{:S(2)}) %collective-permute-start.2) | collective-permute-done | bytes 1114144 | tf_op jit(solution)/shard_map/ppermute | solution.py:448
  36.2 1.2 %collective-permute-done.3.high = bf16[128,4352]{1,0:T(8,128)(2,1)S(1)} collective-permute-done((bf16[128,4352]{1,0:T(8,128)(2,1)S(1)}, bf16[128,4352]{1,0:T(8,128)(2,1)S(1)}, u32[]{:S(2)}, u32[]{:S(2)}) %collective-permute-start.3) | collective-permute-done | bytes 1114144 | tf_op jit(solution)/shard_map/ppermute | solution.py:448
  37.4 1.0 copy-done.2
  38.4 1.2 %copy-done.3 = bf16[128,4352]{1,0:T(8,128)(2,1)S(1)} copy-done((bf16[128,4352]{1,0:T(8,128)(2,1)S(1)}, bf16[128,4352]{1,0:T(8,128)(2,1)}, u32[]{:S(2)}) %copy-start.3) | copy-done | bytes 1114136
  39.6 5.8 %forward_conv.1 = (bf16[128,4480]{1,0:T(8,128)(2,1)S(1)}, bf16[384,4608]{1,0:T(8,128)(2,1)S(1)}) custom-call(bf16[384,960]{1,0:T(8,128)(2,1)S(1)} %make_filter.1.matrix_ref, bf16[32,128]{1,0:T(8,128)(2,1)S(1)} %pad.14.table_ref, bf16[128,4352]{1,0:T(8,128)(2,1)S(1)} %collective-permute-done.2.low, bf16[128,4352]{1,0:T(8,128)(2,1)S(1)} %chip_window.1.own, ...), custom_call_target="tpu_custom_call" | custom-call | flops 3208642560 | bytes 5570560 | tf_op jit(solution)/shard_map/forward_conv/pallas_call | solution.py:244
  45.4 3.6 %collective-permute-start.5 = (bf16[128,4480]{1,0:T(8,128)(2,1)S(1)}, bf16[128,4480]{1,0:T(8,128)(2,1)S(1)}, u32[]{:S(2)}, u32[]{:S(2)}) collective-permute-start(bf16[128,4480]{1,0:T(8,128)(2,1)S(1)} %get-tuple-element.9.d_ref.own), channel_id=1, source_target_pairs={{0,2},{1,3},{2,4},{3,5},{4,6},{5,7},{6,8},{7,9},{8,10},{9,11},{10,... | collective-permute-start | bytes 3440648 | tf_op jit(solution)/shard_map/ppermute | solution.py:448
  49.1 5.0 %collective-permute-start.6 = (bf16[128,4480]{1,0:T(8,128)(2,1)S(1)}, bf16[128,4480]{1,0:T(8,128)(2,1)}, u32[]{:S(2)}, u32[]{:S(2)}) collective-permute-start(bf16[128,4480]{1,0:T(8,128)(2,1)S(1)} %get-tuple-element.9.d_ref.own), channel_id=1, source_target_pairs={{2,0},{3,1},{4,2},{5,3},{6,4},{7,5},{8,6},{9,7},{10,8},{11,9},{12,... | collective-permute-start | bytes 3440648 | tf_op jit(solution)/shard_map/ppermute | solution.py:448
  54.1 6.8 %weight_part.1 = f32[72,128]{1,0:T(8,128)S(1)} custom-call(bf16[384,4608]{1,0:T(8,128)(2,1)S(1)} %get-tuple-element.10.x_ref, bf16[128,4480]{1,0:T(8,128)(2,1)S(1)} %get-tuple-element.9.d_ref.own, bf16[108,30]{1,0:T(8,128)(2,1)S(1)} %copy.18.table_ref), custom_call_target="tpu_custom_call" | custom-call | flops 3208642560 | bytes 4456448 | tf_op jit(solution)/shard_map/weight_part/pallas_call | solution.py:428
  61.0 1.2 %collective-permute-done.7 = f32[72,128]{1,0:T(8,128)S(1)} collective-permute-done((f32[72,128]{1,0:T(8,128)S(1)}, f32[72,128]{1,0:T(8,128)S(1)}, u32[]{:S(2)}, u32[]{:S(2)}) %collective-permute-start.7) | collective-permute-done | bytes 36896 | tf_op jit(solution)/shard_map/ppermute | solution.py:454
  62.2 0.4 collective-permute-start.10
  62.6 1.1 collective-permute-start.8
  63.7 2.0 %collective-permute-start.9 = (f32[72,128]{1,0:T(8,128)S(1)}, f32[72,128]{1,0:T(8,128)S(1)}, u32[]{:S(2)}, u32[]{:S(2)}) collective-permute-start(f32[72,128]{1,0:T(8,128)S(1)} %add.41), channel_id=1, source_target_pairs={{0,64},{1,65},{2,66},{3,67},{4,68},{5,69},{6,70},{7,71},{8,72},{9,... | collective-permute-start | bytes 110600 | tf_op jit(solution)/shard_map/ppermute | solution.py:454
  65.7 0.1 copy.11
  65.8 16.6 %collective-permute-done.10 = f32[72,128]{1,0:T(8,128)S(1)} collective-permute-done((f32[72,128]{1,0:T(8,128)S(1)}, f32[72,128]{1,0:T(8,128)S(1)}, u32[]{:S(2)}, u32[]{:S(2)}) %collective-permute-start.10) | collective-permute-done | bytes 36896 | tf_op jit(solution)/shard_map/ppermute | solution.py:454
  82.4 2.2 %collective-permute-done.8 = f32[72,128]{1,0:T(8,128)S(1)} collective-permute-done((f32[72,128]{1,0:T(8,128)S(1)}, f32[72,128]{1,0:T(8,128)S(1)}, u32[]{:S(2)}, u32[]{:S(2)}) %collective-permute-start.8) | collective-permute-done | bytes 36896 | tf_op jit(solution)/shard_map/ppermute | solution.py:454
  84.8 4.6 %collective-permute-start.14 = (f32[72,128]{1,0:T(8,128)S(1)}, f32[72,128]{1,0:T(8,128)S(1)}, u32[]{:S(2)}, u32[]{:S(2)}) collective-permute-start(f32[72,128]{1,0:T(8,128)S(1)} %add_add_fusion.2), channel_id=1, source_target_pairs={{0,24},{1,25},{2,26},{3,27},{4,28},{5,29},{6,30},{7,31},{8,16},{9,... | collective-permute-start | bytes 110600 | tf_op jit(solution)/shard_map/ppermute | solution.py:454
  89.4 8.4 %input_conv.1 = (bf16[64,8192]{1,0:T(8,128)(2,1)}, bf16[64,4096]{1,0:T(8,128)(2,1)S(1)}) custom-call(bf16[288,32]{1,0:T(8,128)(2,1)S(1)} %bitcast.27, bf16[128,4480]{1,0:T(8,128)(2,1)S(1)} %collective-permute-done.5.low, bf16[128,4480]{1,0:T(8,128)(2,1)S(1)} %get-tuple-element.9.d_ref.own, bf16[128,4480]{1,0:T(8,128)(2,1)} %collective-permute-done.6.high), custom_call_target="tpu_custom_call" | custom-call | flops 3208642560 | bytes 4456448 | tf_op jit(solution)/shard_map/input_conv/pallas_call | solution.py:340
  97.9 0.1 collective-permute-start.15
  98.0 3.3 %collective-permute-start.16 = (f32[72,128]{1,0:T(8,128)S(1)}, f32[72,128]{1,0:T(8,128)S(1)}, u32[]{:S(2)}, u32[]{:S(2)}) collective-permute-start(f32[72,128]{1,0:T(8,128)S(1)} %add_add_fusion.1), channel_id=1, source_target_pairs={{0,4},{1,5},{2,6},{3,7},{4,0},{5,1},{6,2},{7,3},{8,12},{9,13},{10,... | collective-permute-start | bytes 110600 | tf_op jit(solution)/shard_map/ppermute | solution.py:454
  101.4 1.3 %collective-permute-start.17 = (f32[72,128]{1,0:T(8,128)S(1)}, f32[72,128]{1,0:T(8,128)S(1)}, u32[]{:S(2)}, u32[]{:S(2)}) collective-permute-start(f32[72,128]{1,0:T(8,128)S(1)} %add_add_fusion.1), channel_id=1, source_target_pairs={{0,6},{1,7},{2,4},{3,5},{4,2},{5,3},{6,0},{7,1},{8,14},{9,15},{10,... | collective-permute-start | bytes 110600 | tf_op jit(solution)/shard_map/ppermute | solution.py:454
  102.7 1.3 %collective-permute-done.16 = f32[72,128]{1,0:T(8,128)S(1)} collective-permute-done((f32[72,128]{1,0:T(8,128)S(1)}, f32[72,128]{1,0:T(8,128)S(1)}, u32[]{:S(2)}, u32[]{:S(2)}) %collective-permute-start.16) | collective-permute-done | bytes 36896 | tf_op jit(solution)/shard_map/ppermute | solution.py:454
  104.0 2.5 %collective-permute-done.17 = f32[72,128]{1,0:T(8,128)S(1)} collective-permute-done((f32[72,128]{1,0:T(8,128)S(1)}, f32[72,128]{1,0:T(8,128)S(1)}, u32[]{:S(2)}, u32[]{:S(2)}) %collective-permute-start.17) | collective-permute-done | bytes 36896 | tf_op jit(solution)/shard_map/ppermute | solution.py:454
  106.6 0.8 reshape.56
  107.3 0.8 join.1
  (31 shorter events, 0.7 us)
Async XLA Ops:
  0.6 12.7 %copy-start.5 = (s32[2,9]{1,0:T(2,128)S(1)}, s32[2,9]{1,0:T(2,128)}, u32[]{:S(2)}) copy-start(s32[2,9]{1,0:T(2,128)} %param.8) | copy-start | bytes 220
  0.6 3.0 %collective-permute-start.1 = (bf16[64,8192]{1,0:T(8,128)(2,1)}, bf16[64,8192]{1,0:T(8,128)(2,1)S(1)}, u32[]{:S(2)}, u32[]{:S(2)}) collective-permute-start(bf16[64,8192]{1,0:T(8,128)(2,1)} %bitcast.23), channel_id=1, source_target_pairs={{0,1},{1,0},{2,3},{3,2},{4,5},{5,4},{6,7},{7,6},{8,9},{9,8},{10,11... | collective-permute-start | bytes 3145736 | tf_op jit(solution)/shard_map/ppermute | solution.py:454
  3.6 1.2 %copy-start = (bf16[2,32,8192]{2,1,0:T(8,128)(2,1)S(1)}, bf16[2,32,8192]{2,1,0:T(8,128)(2,1)}, u32[]{:S(2)}) copy-start(bf16[2,32,8192]{2,1,0:T(8,128)(2,1)} %param.5) | copy-start | bytes 3145732
  4.8 8.8 %copy-start.4 = (bf16[2,9,9,9]{3,0,2,1:T(2,128)(2,1)S(1)}, bf16[2,9,9,9]{3,0,2,1:T(2,128)(2,1)}, u32[]{:S(2)}) copy-start(bf16[2,9,9,9]{3,0,2,1:T(2,128)(2,1)} %param.7) | copy-start | bytes 8752
  5.0 21.1 %copy-start.1 = (bf16[9,32,32]{2,1,0:T(8,128)(2,1)S(1)}, bf16[9,32,32]{2,1,0:T(8,128)(2,1)}, u32[]{:S(2)}) copy-start(bf16[9,32,32]{2,1,0:T(8,128)(2,1)} %param.9) | copy-start | bytes 55300
  5.0 31.2 %collective-permute-start.2 = (bf16[128,4352]{1,0:T(8,128)(2,1)S(1)}, bf16[128,4352]{1,0:T(8,128)(2,1)S(1)}, u32[]{:S(2)}, u32[]{:S(2)}) collective-permute-start(bf16[128,4352]{1,0:T(8,128)(2,1)S(1)} %chip_window.1.own), channel_id=1, source_target_pairs={{0,2},{1,3},{2,4},{3,5},{4,6},{5,7},{6,8},{7,9},{8,10},{9,11},{10,... | collective-permute-start | bytes 3342344 | tf_op jit(solution)/shard_map/ppermute | solution.py:448
  9.0 28.4 %collective-permute-start.3 = (bf16[128,4352]{1,0:T(8,128)(2,1)S(1)}, bf16[128,4352]{1,0:T(8,128)(2,1)S(1)}, u32[]{:S(2)}, u32[]{:S(2)}) collective-permute-start(bf16[128,4352]{1,0:T(8,128)(2,1)S(1)} %chip_window.1.own), channel_id=1, source_target_pairs={{2,0},{3,1},{4,2},{5,3},{6,4},{7,5},{8,6},{9,7},{10,8},{11,9},{12,... | collective-permute-start | bytes 3342344 | tf_op jit(solution)/shard_map/ppermute | solution.py:448
  13.3 14.3 %collective-permute-start.4 = (bf16[64,8192]{1,0:T(8,128)(2,1)}, bf16[64,8192]{1,0:T(8,128)(2,1)}, u32[]{:S(2)}, u32[]{:S(2)}) collective-permute-start(bf16[64,8192]{1,0:T(8,128)(2,1)} %bitcast.12.cot_own), channel_id=1, source_target_pairs={{0,1},{1,0},{2,3},{3,2},{4,5},{5,4},{6,7},{7,6},{8,9},{9,8},{10,11... | collective-permute-start | bytes 3145736 | tf_op jit(solution)/shard_map/ppermute | solution.py:454
  13.7 2.5 %collective-permute-start = (bf16[2,9,9,9]{3,0,2,1:T(2,128)(2,1)S(1)}, bf16[2,9,9,9]{3,0,2,1:T(2,128)(2,1)}, u32[]{:S(2)}, u32[]{:S(2)}) collective-permute-start(bf16[2,9,9,9]{3,0,2,1:T(2,128)(2,1)S(1)} %broadcast_select_fusion), channel_id=1, source_target_pairs={{0,1},{1,0},{2,3},{3,2},{4,5},{5,4},{6,7},{7,6},{8,9},{9,8},{10,11... | collective-permute-start | bytes 8756 | tf_op jit(solution)/shard_map/ppermute | solution.py:454
  37.4 1.0 copy-start.2
  38.4 1.2 %copy-start.3 = (bf16[128,4352]{1,0:T(8,128)(2,1)S(1)}, bf16[128,4352]{1,0:T(8,128)(2,1)}, u32[]{:S(2)}) copy-start(bf16[128,4352]{1,0:T(8,128)(2,1)} %copy-done.2) | copy-start | bytes 3342340
  45.4 39.2 %collective-permute-start.5 = (bf16[128,4480]{1,0:T(8,128)(2,1)S(1)}, bf16[128,4480]{1,0:T(8,128)(2,1)S(1)}, u32[]{:S(2)}, u32[]{:S(2)}) collective-permute-start(bf16[128,4480]{1,0:T(8,128)(2,1)S(1)} %get-tuple-element.9.d_ref.own), channel_id=1, source_target_pairs={{0,2},{1,3},{2,4},{3,5},{4,6},{5,7},{6,8},{7,9},{8,10},{9,11},{10,... | collective-permute-start | bytes 3440648 | tf_op jit(solution)/shard_map/ppermute | solution.py:448
  49.1 35.6 %collective-permute-start.6 = (bf16[128,4480]{1,0:T(8,128)(2,1)S(1)}, bf16[128,4480]{1,0:T(8,128)(2,1)}, u32[]{:S(2)}, u32[]{:S(2)}) collective-permute-start(bf16[128,4480]{1,0:T(8,128)(2,1)S(1)} %get-tuple-element.9.d_ref.own), channel_id=1, source_target_pairs={{2,0},{3,1},{4,2},{5,3},{6,4},{7,5},{8,6},{9,7},{10,8},{11,9},{12,... | collective-permute-start | bytes 3440648 | tf_op jit(solution)/shard_map/ppermute | solution.py:448
  60.9 1.3 %collective-permute-start.7 = (f32[72,128]{1,0:T(8,128)S(1)}, f32[72,128]{1,0:T(8,128)S(1)}, u32[]{:S(2)}, u32[]{:S(2)}) collective-permute-start(f32[72,128]{1,0:T(8,128)S(1)} %weight_part.1), channel_id=1, source_target_pairs={{0,1},{1,0},{2,3},{3,2},{4,5},{5,4},{6,7},{7,6},{8,9},{9,8},{10,11... | collective-permute-start | bytes 110600 | tf_op jit(solution)/shard_map/ppermute | solution.py:454
  62.2 20.2 %collective-permute-start.10 = (f32[72,128]{1,0:T(8,128)S(1)}, f32[72,128]{1,0:T(8,128)S(1)}, u32[]{:S(2)}, u32[]{:S(2)}) collective-permute-start(f32[72,128]{1,0:T(8,128)S(1)} %add.41), channel_id=1, source_target_pairs={{0,96},{1,97},{2,98},{3,99},{4,100},{5,101},{6,102},{7,103},{8,104... | collective-permute-start | bytes 110600 | tf_op jit(solution)/shard_map/ppermute | solution.py:454
  62.6 22.0 %collective-permute-start.8 = (f32[72,128]{1,0:T(8,128)S(1)}, f32[72,128]{1,0:T(8,128)S(1)}, u32[]{:S(2)}, u32[]{:S(2)}) collective-permute-start(f32[72,128]{1,0:T(8,128)S(1)} %add.41), channel_id=1, source_target_pairs={{0,32},{1,33},{2,34},{3,35},{4,36},{5,37},{6,38},{7,39},{8,40},{9,... | collective-permute-start | bytes 110600 | tf_op jit(solution)/shard_map/ppermute | solution.py:454
  63.7 20.9 %collective-permute-start.9 = (f32[72,128]{1,0:T(8,128)S(1)}, f32[72,128]{1,0:T(8,128)S(1)}, u32[]{:S(2)}, u32[]{:S(2)}) collective-permute-start(f32[72,128]{1,0:T(8,128)S(1)} %add.41), channel_id=1, source_target_pairs={{0,64},{1,65},{2,66},{3,67},{4,68},{5,69},{6,70},{7,71},{8,72},{9,... | collective-permute-start | bytes 110600 | tf_op jit(solution)/shard_map/ppermute | solution.py:454
  84.7 13.2 %collective-permute-start.12 = (f32[72,128]{1,0:T(8,128)S(1)}, f32[72,128]{1,0:T(8,128)S(1)}, u32[]{:S(2)}, u32[]{:S(2)}) collective-permute-start(f32[72,128]{1,0:T(8,128)S(1)} %add_add_fusion.2), channel_id=1, source_target_pairs={{0,8},{1,9},{2,10},{3,11},{4,12},{5,13},{6,14},{7,15},{8,0},{9,1},... | collective-permute-start | bytes 110600 | tf_op jit(solution)/shard_map/ppermute | solution.py:454
  84.7 13.2 %collective-permute-start.13 = (f32[72,128]{1,0:T(8,128)S(1)}, f32[72,128]{1,0:T(8,128)S(1)}, u32[]{:S(2)}, u32[]{:S(2)}) collective-permute-start(f32[72,128]{1,0:T(8,128)S(1)} %add_add_fusion.2), channel_id=1, source_target_pairs={{0,16},{1,17},{2,18},{3,19},{4,20},{5,21},{6,22},{7,23},{8,24},{9,... | collective-permute-start | bytes 110600 | tf_op jit(solution)/shard_map/ppermute | solution.py:454
  84.8 13.1 %collective-permute-start.14 = (f32[72,128]{1,0:T(8,128)S(1)}, f32[72,128]{1,0:T(8,128)S(1)}, u32[]{:S(2)}, u32[]{:S(2)}) collective-permute-start(f32[72,128]{1,0:T(8,128)S(1)} %add_add_fusion.2), channel_id=1, source_target_pairs={{0,24},{1,25},{2,26},{3,27},{4,28},{5,29},{6,30},{7,31},{8,16},{9,... | collective-permute-start | bytes 110600 | tf_op jit(solution)/shard_map/ppermute | solution.py:454
  97.8 9.5 %collective-permute-start.11 = (bf16[64,4096]{1,0:T(8,128)(2,1)S(1)}, bf16[64,4096]{1,0:T(8,128)(2,1)S(1)}, u32[]{:S(2)}, u32[]{:S(2)}) collective-permute-start(bf16[64,4096]{1,0:T(8,128)(2,1)S(1)} %get-tuple-element.13), channel_id=1, source_target_pairs={{0,1},{1,0},{2,3},{3,2},{4,5},{5,4},{6,7},{7,6},{8,9},{9,8},{10,11... | collective-permute-start | bytes 1572872 | tf_op jit(solution)/shard_map/ppermute | solution.py:454
  97.9 4.8 %collective-permute-start.15 = (f32[72,128]{1,0:T(8,128)S(1)}, f32[72,128]{1,0:T(8,128)S(1)}, u32[]{:S(2)}, u32[]{:S(2)}) collective-permute-start(f32[72,128]{1,0:T(8,128)S(1)} %add_add_fusion.1), channel_id=1, source_target_pairs={{0,2},{1,3},{2,0},{3,1},{4,6},{5,7},{6,4},{7,5},{8,10},{9,11},{10,... | collective-permute-start | bytes 110600 | tf_op jit(solution)/shard_map/ppermute | solution.py:454
  98.0 6.0 %collective-permute-start.16 = (f32[72,128]{1,0:T(8,128)S(1)}, f32[72,128]{1,0:T(8,128)S(1)}, u32[]{:S(2)}, u32[]{:S(2)}) collective-permute-start(f32[72,128]{1,0:T(8,128)S(1)} %add_add_fusion.1), channel_id=1, source_target_pairs={{0,4},{1,5},{2,6},{3,7},{4,0},{5,1},{6,2},{7,3},{8,12},{9,13},{10,... | collective-permute-start | bytes 110600 | tf_op jit(solution)/shard_map/ppermute | solution.py:454
  101.4 5.2 %collective-permute-start.17 = (f32[72,128]{1,0:T(8,128)S(1)}, f32[72,128]{1,0:T(8,128)S(1)}, u32[]{:S(2)}, u32[]{:S(2)}) collective-permute-start(f32[72,128]{1,0:T(8,128)S(1)} %add_add_fusion.1), channel_id=1, source_target_pairs={{0,6},{1,7},{2,4},{3,5},{4,2},{5,3},{6,0},{7,1},{8,14},{9,15},{10,... | collective-permute-start | bytes 110600 | tf_op jit(solution)/shard_map/ppermute | solution.py:454

commit v5 on v4

--- a/solution.py
+++ b/solution.py
@@ -22,8 +22,8 @@
 OUT = 3 * BLOCK
 PAD = 128
 LANES = 128
-VMEM = 24 * 1024 * 1024
-SMALL = 8 * 1024 * 1024
+VMEM = 26 * 1024 * 1024
+SMALL = VMEM
 LARGE = 58 * 1024 * 1024
 ANY = pl.BlockSpec(memory_space=pl.ANY)
 LOCAL = pl.BlockSpec(memory_space=pltpu.VMEM)
@@ -100,23 +100,66 @@
     return copies
 
 
-def window_kernel(own, mate, out_ref, sems):
-    copies = window_copies(own, mate, out_ref, sems)
+def window_pieces(whole, target, row, sems):
+    longitude = whole.shape[1]
+    half = longitude // 2
+    return [
+        pltpu.make_async_copy(
+            whole.at[:, pl.ds(pl.multiple_of(source, PAD), size)],
+            target.at[pl.ds(row, BLOCK), pl.ds(start, size)],
+            sems.at[at],
+        )
+        for at, (source, start, size) in enumerate(
+            (
+                (core() * half, PAD, half),
+                (longitude - PAD - core() * half, 0, PAD),
+                (half - core() * half, PAD + half, PAD),
+            )
+        )
+    ]
+
+
+def own_kernel(own, out_ref, sems):
+    copies = window_pieces(own, out_ref, 0, sems)
     for copy in copies:
         copy.start()
     wait_for(copies)
 
 
-def chip_window(own, mate):
-    return pl.pallas_call(
-        window_kernel,
-        out_shape=jax.ShapeDtypeStruct((2 * BLOCK, own.shape[1] // 2 + 2 * PAD), own.dtype),
+def own_window(own):
+    return pl.pallas_call(
+        own_kernel,
+        out_shape=jax.ShapeDtypeStruct((BLOCK, own.shape[1] // 2 + 2 * PAD), own.dtype),
+        in_specs=[ANY],
+        out_specs=LOCAL,
+        scratch_shapes=[pltpu.SemaphoreType.DMA((3,))],
+        compiler_params=pltpu.CompilerParams(vmem_limit_bytes=SMALL),
+        name="own_window",
+    )(own)
+
+
+def chip_kernel(piece, mate, out_ref, sems, piece_sem):
+    row = pl.multiple_of((1 - core()) * BLOCK, BLOCK)
+    copies = window_pieces(mate, out_ref, row, sems)
+    own_row = pl.multiple_of(core() * BLOCK, BLOCK)
+    copies.append(
+        pltpu.make_async_copy(piece, out_ref.at[pl.ds(own_row, BLOCK), :], piece_sem)
+    )
+    for copy in copies:
+        copy.start()
+    wait_for(copies)
+
+
+def chip_window(piece, mate):
+    return pl.pallas_call(
+        chip_kernel,
+        out_shape=jax.ShapeDtypeStruct((2 * BLOCK, piece.shape[1]), piece.dtype),
         in_specs=[ANY, ANY],
         out_specs=LOCAL,
-        scratch_shapes=[pltpu.SemaphoreType.DMA((2, 3))],
+        scratch_shapes=[pltpu.SemaphoreType.DMA((3,)), pltpu.SemaphoreType.DMA],
         compiler_params=pltpu.CompilerParams(vmem_limit_bytes=SMALL),
         name="chip_window",
-    )(own, mate)
+    )(piece, mate)
 
 
 def join_kernel(got, whole, out, sem):
@@ -255,7 +298,7 @@
             pltpu.SemaphoreType.DMA((2, 3)),
             pltpu.SemaphoreType.DMA((2, 3)),
         ],
-        compiler_params=pltpu.CompilerParams(vmem_limit_bytes=VMEM - 4 * 1024 * 1024),
+        compiler_params=pltpu.CompilerParams(vmem_limit_bytes=VMEM),
         cost_estimate=work(width, 5),
         name="forward_conv",
     )(matrix, chip_table, *blocks, *cots)
@@ -356,7 +399,7 @@
             pltpu.SemaphoreType.DMA((3,)),
             pltpu.SemaphoreType.DMA((2,)),
         ],
-        compiler_params=pltpu.CompilerParams(vmem_limit_bytes=VMEM + 2 * 1024 * 1024),
+        compiler_params=pltpu.CompilerParams(vmem_limit_bytes=VMEM),
         cost_estimate=work(width, 4),
         name="input_conv",
     )(weights, low, own, high)
@@ -437,7 +480,7 @@
             pltpu.VMEM((K * C, LANES), jnp.float32),
             pltpu.VMEM((3 * CHIP * K, DEEP), jnp.float32),
         ],
-        compiler_params=pltpu.CompilerParams(vmem_limit_bytes=VMEM - 6 * 1024 * 1024),
+        compiler_params=pltpu.CompilerParams(vmem_limit_bytes=VMEM),
         cost_estimate=work(width, 4),
         name="weight_part",
     )(joined, delta, table)
@@ -501,7 +544,7 @@
     pair = jnp.where(
         core() == 0, jnp.concatenate([masked, mate]), jnp.concatenate([mate, masked])
     )
-    window = chip_window(own, own_mate)
+    window = chip_window(own_window(own), own_mate)
     low, high = moved(window, 2), moved(window, -2)
     cot_mate = swapped(cot_own)
 

time: 109 us -> 107 us (0.982)
  waiting for transfers between devices: 38.4 us -> 37.3 us
    ppermute x14, waiting for transfers between devices: 28.6 us -> 27.5 us  [swapped(): lax.ppermute(array, 'lat', [(i, i ^ bit) for i in range(lax.axis_size('la...]
where the time goes in v5:
time: 107 us
  waiting for transfers between devices  37.3 us (35%)
  starting transfers between devices  30.8 us (29%)
  Pallas kernels  23.1 us (22%)
  local copies, waits for them, and re-layouts  12.5 us (12%)
  other arithmetic  2.12 us (2%)
  between operations  1.12 us (1%)
    ppermute x14, waiting for transfers between devices, swapped(): lax.ppermute(array, 'lat', [(i, i ^ bit) for i in range(lax.axis_size('la...  27.5 us
    ppermute x4, starting transfers between devices, moved(): lax.ppermute(array, 'lat', [(i, i + by) for i in range(peers) if 0 <= i +...  16.9 us
    ppermute x14, starting transfers between devices, swapped(): lax.ppermute(array, 'lat', [(i, i ^ bit) for i in range(lax.axis_size('la...  13.9 us
    ppermute x4, waiting for transfers between devices, moved(): lax.ppermute(array, 'lat', [(i, i + by) for i in range(peers) if 0 <= i +...  9.77 us
    pallas_call x1, Pallas kernels, backward(): pl.pallas_call(backward_kernel, out_shape=(jax.ShapeDtypeStruct((BLOCK, 2...  8.37 us
    pallas_call x1, Pallas kernels, weight_part(): pl.pallas_call(functools.partial(weight_kernel, scale), out_shape=jax.Sha...  6.54 us
    pallas_call x1, Pallas kernels, forward(): pl.pallas_call(forward_kernel, out_shape=(jax.ShapeDtypeStruct((2 * BLOCK...  5.64 us
    unnamed x13, local copies, waits for them, and re-layouts  3.6 us
  transfers between devices with their start and end apart: 18, of which 9 were waited for; matrix products, arithmetic and copies ran while one was open for 10% of the time, Pallas kernels for 15%

profile of v5, /device:TPU:22, one launch (start us, length us, event | category | flops | bytes accessed | tf_op | source)
XLA Modules:
  0.0 106.9 jit_solution(55528351410227163)
XLA Ops:
  0.7 1.2 %copy-done = bf16[2,32,8192]{2,1,0:T(8,128)(2,1)S(1)} copy-done((bf16[2,32,8192]{2,1,0:T(8,128)(2,1)S(1)}, bf16[2,32,8192]{2,1,0:T(8,128)(2,1)}, u32[]{:S(2)}) %copy-start) | copy-done | bytes 1048600
  2.1 1.5 %collective-permute-done.1.mate = bf16[64,8192]{1,0:T(8,128)(2,1)S(1)} collective-permute-done((bf16[64,8192]{1,0:T(8,128)(2,1)}, bf16[64,8192]{1,0:T(8,128)(2,1)S(1)}, u32[]{:S(2)}, u32[]{:S(2)}) %collective-permute-start.1) | collective-permute-done | bytes 1048608 | tf_op jit(solution)/shard_map/ppermute | solution.py:497
  3.6 0.2 chip_window.1.own
  3.8 4.0 %collective-permute-start.2 = (bf16[128,4352]{1,0:T(8,128)(2,1)S(1)}, bf16[128,4352]{1,0:T(8,128)(2,1)S(1)}, u32[]{:S(2)}, u32[]{:S(2)}) collective-permute-start(bf16[128,4352]{1,0:T(8,128)(2,1)S(1)} %chip_window.1.own), channel_id=1, source_target_pairs={{0,2},{1,3},{2,4},{3,5},{4,6},{5,7},{6,8},{7,9},{8,10},{9,11},{10,... | collective-permute-start | bytes 3342344 | tf_op jit(solution)/shard_map/ppermute | solution.py:491
  7.7 4.3 %collective-permute-start.3 = (bf16[128,4352]{1,0:T(8,128)(2,1)S(1)}, bf16[128,4352]{1,0:T(8,128)(2,1)S(1)}, u32[]{:S(2)}, u32[]{:S(2)}) collective-permute-start(bf16[128,4352]{1,0:T(8,128)(2,1)S(1)} %chip_window.1.own), channel_id=1, source_target_pairs={{2,0},{3,1},{4,2},{5,3},{6,4},{7,5},{8,6},{9,7},{10,8},{11,9},{12,... | collective-permute-start | bytes 3342344 | tf_op jit(solution)/shard_map/ppermute | solution.py:491
  12.0 0.1 collective-permute-start.4
  12.2 0.1 copy.12
  12.3 0.2 broadcast_select_fusion
  12.5 0.6 collective-permute-start
  13.1 1.9 %collective-permute-done = bf16[2,9,9,9]{3,0,2,1:T(2,128)(2,1)} collective-permute-done((bf16[2,9,9,9]{3,0,2,1:T(2,128)(2,1)S(1)}, bf16[2,9,9,9]{3,0,2,1:T(2,128)(2,1)}, u32[]{:S(2)}, u32[]{:S(2)}) %collective-permute-start) | collective-permute-done | bytes 2948 | tf_op jit(solution)/shard_map/ppermute | solution.py:497
  15.0 1.1 maximum_select_fusion
  16.0 0.7 rev.3
  16.7 0.8 fusion
  17.5 1.1 %copy.26 = bf16[2,1,9,9,9]{2,0,4,3,1:T(2,128)(2,1)S(1)} copy(bf16[2,1,9,9,9]{4,1,0,3,2:T(2,128)(2,1)} %get-tuple-element.16) | data formatting | bytes 5832 | tf_op jit(solution)/shard_map/squeeze | solution.py:518
  18.6 1.1 %copy.27 = bf16[2,1,9,9,9]{2,0,4,3,1:T(2,128)(2,1)S(1)} copy(bf16[2,1,9,9,9]{4,1,0,3,2:T(2,128)(2,1)} %get-tuple-element.17) | data formatting | bytes 5832 | tf_op jit(solution)/shard_map/squeeze | solution.py:518
  19.8 0.1 pad.13.clone
  19.9 0.8 maximum_bitcast_fusion
  20.7 1.2 %copy.17 = bf16[2,3,2,9,10,3]{3,2,1,0,5,4:T(2,128)(2,1)S(1)} copy(bf16[2,3,2,9,10,3]{4,0,3,5,1,2:T(2,128)(2,1)} %maximum_bitcast_fusion) | data formatting | bytes 12960 | tf_op jit(solution)/shard_map/transpose | solution.py:510
  21.9 0.1 reshape.49
  22.0 0.1 copy.18.table_ref
  22.1 1.6 %copy.29 = bf16[4,9,3,3,9]{4,2,3,1,0:T(4,128)(2,1)} copy(bf16[4,9,3,3,9]{4,0,3,2,1:T(4,128)(2,1)} %bitcast.31) | data formatting | bytes 11664 | tf_op jit(solution)/shard_map/reshape | solution.py:527
  23.7 1.0 reshape.52
  24.7 0.1 copy.20
  24.9 1.5 %make_filter.1.matrix_ref = bf16[384,960]{1,0:T(8,128)(2,1)S(1)} custom-call(bf16[108,30]{1,0:T(8,128)(2,1)S(1)} %copy.18.table_ref, bf16[288,32]{1,0:T(8,128)(2,1)S(1)} %bitcast.25), custom_call_target="tpu_custom_call" | custom-call | tf_op jit(solution)/shard_map/make_filter/pallas_call | solution.py:61
  26.4 8.6 %collective-permute-done.2.low = bf16[128,4352]{1,0:T(8,128)(2,1)S(1)} collective-permute-done((bf16[128,4352]{1,0:T(8,128)(2,1)S(1)}, bf16[128,4352]{1,0:T(8,128)(2,1)S(1)}, u32[]{:S(2)}, u32[]{:S(2)}) %collective-permute-start.2) | collective-permute-done | bytes 1114144 | tf_op jit(solution)/shard_map/ppermute | solution.py:491
  35.0 1.2 %collective-permute-done.3.high = bf16[128,4352]{1,0:T(8,128)(2,1)S(1)} collective-permute-done((bf16[128,4352]{1,0:T(8,128)(2,1)S(1)}, bf16[128,4352]{1,0:T(8,128)(2,1)S(1)}, u32[]{:S(2)}, u32[]{:S(2)}) %collective-permute-start.3) | collective-permute-done | bytes 1114144 | tf_op jit(solution)/shard_map/ppermute | solution.py:491
  36.1 1.0 copy-done.2
  37.2 1.2 %copy-done.3 = bf16[128,4352]{1,0:T(8,128)(2,1)S(1)} copy-done((bf16[128,4352]{1,0:T(8,128)(2,1)S(1)}, bf16[128,4352]{1,0:T(8,128)(2,1)}, u32[]{:S(2)}) %copy-start.3) | copy-done | bytes 1114136
  38.4 5.6 %forward_conv.1 = (bf16[128,4480]{1,0:T(8,128)(2,1)S(1)}, bf16[384,4608]{1,0:T(8,128)(2,1)S(1)}) custom-call(bf16[384,960]{1,0:T(8,128)(2,1)S(1)} %make_filter.1.matrix_ref, bf16[32,128]{1,0:T(8,128)(2,1)S(1)} %pad.14.table_ref, bf16[128,4352]{1,0:T(8,128)(2,1)S(1)} %collective-permute-done.2.low, bf16[128,4352]{1,0:T(8,128)(2,1)S(1)} %chip_window.1.own, ...), custom_call_target="tpu_custom_call" | custom-call | flops 3208642560 | bytes 5570560 | tf_op jit(solution)/shard_map/forward_conv/pallas_call | solution.py:287
  44.1 3.6 %collective-permute-start.5 = (bf16[128,4480]{1,0:T(8,128)(2,1)S(1)}, bf16[128,4480]{1,0:T(8,128)(2,1)S(1)}, u32[]{:S(2)}, u32[]{:S(2)}) collective-permute-start(bf16[128,4480]{1,0:T(8,128)(2,1)S(1)} %get-tuple-element.9.d_ref.own), channel_id=1, source_target_pairs={{0,2},{1,3},{2,4},{3,5},{4,6},{5,7},{6,8},{7,9},{8,10},{9,11},{10,... | collective-permute-start | bytes 3440648 | tf_op jit(solution)/shard_map/ppermute | solution.py:491
  47.7 5.0 %collective-permute-start.6 = (bf16[128,4480]{1,0:T(8,128)(2,1)S(1)}, bf16[128,4480]{1,0:T(8,128)(2,1)}, u32[]{:S(2)}, u32[]{:S(2)}) collective-permute-start(bf16[128,4480]{1,0:T(8,128)(2,1)S(1)} %get-tuple-element.9.d_ref.own), channel_id=1, source_target_pairs={{2,0},{3,1},{4,2},{5,3},{6,4},{7,5},{8,6},{9,7},{10,8},{11,9},{12,... | collective-permute-start | bytes 3440648 | tf_op jit(solution)/shard_map/ppermute | solution.py:491
  52.7 6.5 %weight_part.1 = f32[72,128]{1,0:T(8,128)S(1)} custom-call(bf16[384,4608]{1,0:T(8,128)(2,1)S(1)} %get-tuple-element.10.x_ref, bf16[128,4480]{1,0:T(8,128)(2,1)S(1)} %get-tuple-element.9.d_ref.own, bf16[108,30]{1,0:T(8,128)(2,1)S(1)} %copy.18.table_ref), custom_call_target="tpu_custom_call" | custom-call | flops 3208642560 | bytes 4456448 | tf_op jit(solution)/shard_map/weight_part/pallas_call | solution.py:471
  59.3 1.2 %collective-permute-done.7 = f32[72,128]{1,0:T(8,128)S(1)} collective-permute-done((f32[72,128]{1,0:T(8,128)S(1)}, f32[72,128]{1,0:T(8,128)S(1)}, u32[]{:S(2)}, u32[]{:S(2)}) %collective-permute-start.7) | collective-permute-done | bytes 36896 | tf_op jit(solution)/shard_map/ppermute | solution.py:497
  60.5 0.4 collective-permute-start.10
  61.0 1.1 collective-permute-start.8
  62.0 2.0 %collective-permute-start.9 = (f32[72,128]{1,0:T(8,128)S(1)}, f32[72,128]{1,0:T(8,128)S(1)}, u32[]{:S(2)}, u32[]{:S(2)}) collective-permute-start(f32[72,128]{1,0:T(8,128)S(1)} %add.41), channel_id=1, source_target_pairs={{0,64},{1,65},{2,66},{3,67},{4,68},{5,69},{6,70},{7,71},{8,72},{9,... | collective-permute-start | bytes 110600 | tf_op jit(solution)/shard_map/ppermute | solution.py:497
  64.0 0.1 copy.11
  64.1 16.9 %collective-permute-done.10 = f32[72,128]{1,0:T(8,128)S(1)} collective-permute-done((f32[72,128]{1,0:T(8,128)S(1)}, f32[72,128]{1,0:T(8,128)S(1)}, u32[]{:S(2)}, u32[]{:S(2)}) %collective-permute-start.10) | collective-permute-done | bytes 36896 | tf_op jit(solution)/shard_map/ppermute | solution.py:497
  81.0 2.2 %collective-permute-done.8 = f32[72,128]{1,0:T(8,128)S(1)} collective-permute-done((f32[72,128]{1,0:T(8,128)S(1)}, f32[72,128]{1,0:T(8,128)S(1)}, u32[]{:S(2)}, u32[]{:S(2)}) %collective-permute-start.8) | collective-permute-done | bytes 36896 | tf_op jit(solution)/shard_map/ppermute | solution.py:497
  83.5 4.6 %collective-permute-start.14 = (f32[72,128]{1,0:T(8,128)S(1)}, f32[72,128]{1,0:T(8,128)S(1)}, u32[]{:S(2)}, u32[]{:S(2)}) collective-permute-start(f32[72,128]{1,0:T(8,128)S(1)} %add_add_fusion.2), channel_id=1, source_target_pairs={{0,24},{1,25},{2,26},{3,27},{4,28},{5,29},{6,30},{7,31},{8,16},{9,... | collective-permute-start | bytes 110600 | tf_op jit(solution)/shard_map/ppermute | solution.py:497
  88.1 8.4 %input_conv.1 = (bf16[64,8192]{1,0:T(8,128)(2,1)}, bf16[64,4096]{1,0:T(8,128)(2,1)S(1)}) custom-call(bf16[288,32]{1,0:T(8,128)(2,1)S(1)} %bitcast.27, bf16[128,4480]{1,0:T(8,128)(2,1)S(1)} %collective-permute-done.5.low, bf16[128,4480]{1,0:T(8,128)(2,1)S(1)} %get-tuple-element.9.d_ref.own, bf16[128,4480]{1,0:T(8,128)(2,1)} %collective-permute-done.6.high), custom_call_target="tpu_custom_call" | custom-call | flops 3208642560 | bytes 4456448 | tf_op jit(solution)/shard_map/input_conv/pallas_call | solution.py:383
  96.6 0.1 collective-permute-start.15
  96.7 3.3 %collective-permute-start.16 = (f32[72,128]{1,0:T(8,128)S(1)}, f32[72,128]{1,0:T(8,128)S(1)}, u32[]{:S(2)}, u32[]{:S(2)}) collective-permute-start(f32[72,128]{1,0:T(8,128)S(1)} %add_add_fusion.1), channel_id=1, source_target_pairs={{0,4},{1,5},{2,6},{3,7},{4,0},{5,1},{6,2},{7,3},{8,12},{9,13},{10,... | collective-permute-start | bytes 110600 | tf_op jit(solution)/shard_map/ppermute | solution.py:497
  100.0 1.4 %collective-permute-start.17 = (f32[72,128]{1,0:T(8,128)S(1)}, f32[72,128]{1,0:T(8,128)S(1)}, u32[]{:S(2)}, u32[]{:S(2)}) collective-permute-start(f32[72,128]{1,0:T(8,128)S(1)} %add_add_fusion.1), channel_id=1, source_target_pairs={{0,6},{1,7},{2,4},{3,5},{4,2},{5,3},{6,0},{7,1},{8,14},{9,15},{10,... | collective-permute-start | bytes 110600 | tf_op jit(solution)/shard_map/ppermute | solution.py:497
  101.4 1.3 %collective-permute-done.16 = f32[72,128]{1,0:T(8,128)S(1)} collective-permute-done((f32[72,128]{1,0:T(8,128)S(1)}, f32[72,128]{1,0:T(8,128)S(1)}, u32[]{:S(2)}, u32[]{:S(2)}) %collective-permute-start.16) | collective-permute-done | bytes 36896 | tf_op jit(solution)/shard_map/ppermute | solution.py:497
  102.6 2.5 %collective-permute-done.17 = f32[72,128]{1,0:T(8,128)S(1)} collective-permute-done((f32[72,128]{1,0:T(8,128)S(1)}, f32[72,128]{1,0:T(8,128)S(1)}, u32[]{:S(2)}, u32[]{:S(2)}) %collective-permute-start.17) | collective-permute-done | bytes 36896 | tf_op jit(solution)/shard_map/ppermute | solution.py:497
  105.2 0.8 reshape.56
  105.9 0.8 join.1
  (32 shorter events, 0.7 us)
Async XLA Ops:
  0.6 3.0 %collective-permute-start.1 = (bf16[64,8192]{1,0:T(8,128)(2,1)}, bf16[64,8192]{1,0:T(8,128)(2,1)S(1)}, u32[]{:S(2)}, u32[]{:S(2)}) collective-permute-start(bf16[64,8192]{1,0:T(8,128)(2,1)} %bitcast.23), channel_id=1, source_target_pairs={{0,1},{1,0},{2,3},{3,2},{4,5},{5,4},{6,7},{7,6},{8,9},{9,8},{10,11... | collective-permute-start | bytes 3145736 | tf_op jit(solution)/shard_map/ppermute | solution.py:497
  0.7 1.2 %copy-start = (bf16[2,32,8192]{2,1,0:T(8,128)(2,1)S(1)}, bf16[2,32,8192]{2,1,0:T(8,128)(2,1)}, u32[]{:S(2)}) copy-start(bf16[2,32,8192]{2,1,0:T(8,128)(2,1)} %param.5) | copy-start | bytes 3145732
  2.0 10.1 %copy-start.5 = (s32[2,9]{1,0:T(2,128)S(1)}, s32[2,9]{1,0:T(2,128)}, u32[]{:S(2)}) copy-start(s32[2,9]{1,0:T(2,128)} %param.8) | copy-start | bytes 220
  2.0 10.3 %copy-start.4 = (bf16[2,9,9,9]{3,0,2,1:T(2,128)(2,1)S(1)}, bf16[2,9,9,9]{3,0,2,1:T(2,128)(2,1)}, u32[]{:S(2)}) copy-start(bf16[2,9,9,9]{3,0,2,1:T(2,128)(2,1)} %param.7) | copy-start | bytes 8752
  3.8 21.1 %copy-start.1 = (bf16[9,32,32]{2,1,0:T(8,128)(2,1)S(1)}, bf16[9,32,32]{2,1,0:T(8,128)(2,1)}, u32[]{:S(2)}) copy-start(bf16[9,32,32]{2,1,0:T(8,128)(2,1)} %param.9) | copy-start | bytes 55300
  3.8 31.2 %collective-permute-start.2 = (bf16[128,4352]{1,0:T(8,128)(2,1)S(1)}, bf16[128,4352]{1,0:T(8,128)(2,1)S(1)}, u32[]{:S(2)}, u32[]{:S(2)}) collective-permute-start(bf16[128,4352]{1,0:T(8,128)(2,1)S(1)} %chip_window.1.own), channel_id=1, source_target_pairs={{0,2},{1,3},{2,4},{3,5},{4,6},{5,7},{6,8},{7,9},{8,10},{9,11},{10,... | collective-permute-start | bytes 3342344 | tf_op jit(solution)/shard_map/ppermute | solution.py:491
  7.7 28.4 %collective-permute-start.3 = (bf16[128,4352]{1,0:T(8,128)(2,1)S(1)}, bf16[128,4352]{1,0:T(8,128)(2,1)S(1)}, u32[]{:S(2)}, u32[]{:S(2)}) collective-permute-start(bf16[128,4352]{1,0:T(8,128)(2,1)S(1)} %chip_window.1.own), channel_id=1, source_target_pairs={{2,0},{3,1},{4,2},{5,3},{6,4},{7,5},{8,6},{9,7},{10,8},{11,9},{12,... | collective-permute-start | bytes 3342344 | tf_op jit(solution)/shard_map/ppermute | solution.py:491
  12.0 14.3 %collective-permute-start.4 = (bf16[64,8192]{1,0:T(8,128)(2,1)}, bf16[64,8192]{1,0:T(8,128)(2,1)}, u32[]{:S(2)}, u32[]{:S(2)}) collective-permute-start(bf16[64,8192]{1,0:T(8,128)(2,1)} %bitcast.12.cot_own), channel_id=1, source_target_pairs={{0,1},{1,0},{2,3},{3,2},{4,5},{5,4},{6,7},{7,6},{8,9},{9,8},{10,11... | collective-permute-start | bytes 3145736 | tf_op jit(solution)/shard_map/ppermute | solution.py:497
  12.5 2.5 %collective-permute-start = (bf16[2,9,9,9]{3,0,2,1:T(2,128)(2,1)S(1)}, bf16[2,9,9,9]{3,0,2,1:T(2,128)(2,1)}, u32[]{:S(2)}, u32[]{:S(2)}) collective-permute-start(bf16[2,9,9,9]{3,0,2,1:T(2,128)(2,1)S(1)} %broadcast_select_fusion), channel_id=1, source_target_pairs={{0,1},{1,0},{2,3},{3,2},{4,5},{5,4},{6,7},{7,6},{8,9},{9,8},{10,11... | collective-permute-start | bytes 8756 | tf_op jit(solution)/shard_map/ppermute | solution.py:497
  36.1 1.0 copy-start.2
  37.2 1.2 %copy-start.3 = (bf16[128,4352]{1,0:T(8,128)(2,1)S(1)}, bf16[128,4352]{1,0:T(8,128)(2,1)}, u32[]{:S(2)}) copy-start(bf16[128,4352]{1,0:T(8,128)(2,1)} %copy-done.2) | copy-start | bytes 3342340
  44.1 39.2 %collective-permute-start.5 = (bf16[128,4480]{1,0:T(8,128)(2,1)S(1)}, bf16[128,4480]{1,0:T(8,128)(2,1)S(1)}, u32[]{:S(2)}, u32[]{:S(2)}) collective-permute-start(bf16[128,4480]{1,0:T(8,128)(2,1)S(1)} %get-tuple-element.9.d_ref.own), channel_id=1, source_target_pairs={{0,2},{1,3},{2,4},{3,5},{4,6},{5,7},{6,8},{7,9},{8,10},{9,11},{10,... | collective-permute-start | bytes 3440648 | tf_op jit(solution)/shard_map/ppermute | solution.py:491
  47.7 35.6 %collective-permute-start.6 = (bf16[128,4480]{1,0:T(8,128)(2,1)S(1)}, bf16[128,4480]{1,0:T(8,128)(2,1)}, u32[]{:S(2)}, u32[]{:S(2)}) collective-permute-start(bf16[128,4480]{1,0:T(8,128)(2,1)S(1)} %get-tuple-element.9.d_ref.own), channel_id=1, source_target_pairs={{2,0},{3,1},{4,2},{5,3},{6,4},{7,5},{8,6},{9,7},{10,8},{11,9},{12,... | collective-permute-start | bytes 3440648 | tf_op jit(solution)/shard_map/ppermute | solution.py:491
  59.2 1.3 %collective-permute-start.7 = (f32[72,128]{1,0:T(8,128)S(1)}, f32[72,128]{1,0:T(8,128)S(1)}, u32[]{:S(2)}, u32[]{:S(2)}) collective-permute-start(f32[72,128]{1,0:T(8,128)S(1)} %weight_part.1), channel_id=1, source_target_pairs={{0,1},{1,0},{2,3},{3,2},{4,5},{5,4},{6,7},{7,6},{8,9},{9,8},{10,11... | collective-permute-start | bytes 110600 | tf_op jit(solution)/shard_map/ppermute | solution.py:497
  60.5 20.5 %collective-permute-start.10 = (f32[72,128]{1,0:T(8,128)S(1)}, f32[72,128]{1,0:T(8,128)S(1)}, u32[]{:S(2)}, u32[]{:S(2)}) collective-permute-start(f32[72,128]{1,0:T(8,128)S(1)} %add.41), channel_id=1, source_target_pairs={{0,96},{1,97},{2,98},{3,99},{4,100},{5,101},{6,102},{7,103},{8,104... | collective-permute-start | bytes 110600 | tf_op jit(solution)/shard_map/ppermute | solution.py:497
  61.0 22.3 %collective-permute-start.8 = (f32[72,128]{1,0:T(8,128)S(1)}, f32[72,128]{1,0:T(8,128)S(1)}, u32[]{:S(2)}, u32[]{:S(2)}) collective-permute-start(f32[72,128]{1,0:T(8,128)S(1)} %add.41), channel_id=1, source_target_pairs={{0,32},{1,33},{2,34},{3,35},{4,36},{5,37},{6,38},{7,39},{8,40},{9,... | collective-permute-start | bytes 110600 | tf_op jit(solution)/shard_map/ppermute | solution.py:497
  62.0 21.2 %collective-permute-start.9 = (f32[72,128]{1,0:T(8,128)S(1)}, f32[72,128]{1,0:T(8,128)S(1)}, u32[]{:S(2)}, u32[]{:S(2)}) collective-permute-start(f32[72,128]{1,0:T(8,128)S(1)} %add.41), channel_id=1, source_target_pairs={{0,64},{1,65},{2,66},{3,67},{4,68},{5,69},{6,70},{7,71},{8,72},{9,... | collective-permute-start | bytes 110600 | tf_op jit(solution)/shard_map/ppermute | solution.py:497
  83.3 13.3 %collective-permute-start.12 = (f32[72,128]{1,0:T(8,128)S(1)}, f32[72,128]{1,0:T(8,128)S(1)}, u32[]{:S(2)}, u32[]{:S(2)}) collective-permute-start(f32[72,128]{1,0:T(8,128)S(1)} %add_add_fusion.2), channel_id=1, source_target_pairs={{0,8},{1,9},{2,10},{3,11},{4,12},{5,13},{6,14},{7,15},{8,0},{9,1},... | collective-permute-start | bytes 110600 | tf_op jit(solution)/shard_map/ppermute | solution.py:497
  83.4 13.2 %collective-permute-start.13 = (f32[72,128]{1,0:T(8,128)S(1)}, f32[72,128]{1,0:T(8,128)S(1)}, u32[]{:S(2)}, u32[]{:S(2)}) collective-permute-start(f32[72,128]{1,0:T(8,128)S(1)} %add_add_fusion.2), channel_id=1, source_target_pairs={{0,16},{1,17},{2,18},{3,19},{4,20},{5,21},{6,22},{7,23},{8,24},{9,... | collective-permute-start | bytes 110600 | tf_op jit(solution)/shard_map/ppermute | solution.py:497
  83.5 13.1 %collective-permute-start.14 = (f32[72,128]{1,0:T(8,128)S(1)}, f32[72,128]{1,0:T(8,128)S(1)}, u32[]{:S(2)}, u32[]{:S(2)}) collective-permute-start(f32[72,128]{1,0:T(8,128)S(1)} %add_add_fusion.2), channel_id=1, source_target_pairs={{0,24},{1,25},{2,26},{3,27},{4,28},{5,29},{6,30},{7,31},{8,16},{9,... | collective-permute-start | bytes 110600 | tf_op jit(solution)/shard_map/ppermute | solution.py:497
  96.4 9.5 %collective-permute-start.11 = (bf16[64,4096]{1,0:T(8,128)(2,1)S(1)}, bf16[64,4096]{1,0:T(8,128)(2,1)S(1)}, u32[]{:S(2)}, u32[]{:S(2)}) collective-permute-start(bf16[64,4096]{1,0:T(8,128)(2,1)S(1)} %get-tuple-element.13), channel_id=1, source_target_pairs={{0,1},{1,0},{2,3},{3,2},{4,5},{5,4},{6,7},{7,6},{8,9},{9,8},{10,11... | collective-permute-start | bytes 1572872 | tf_op jit(solution)/shard_map/ppermute | solution.py:497
  96.6 4.8 %collective-permute-start.15 = (f32[72,128]{1,0:T(8,128)S(1)}, f32[72,128]{1,0:T(8,128)S(1)}, u32[]{:S(2)}, u32[]{:S(2)}) collective-permute-start(f32[72,128]{1,0:T(8,128)S(1)} %add_add_fusion.1), channel_id=1, source_target_pairs={{0,2},{1,3},{2,0},{3,1},{4,6},{5,7},{6,4},{7,5},{8,10},{9,11},{10,... | collective-permute-start | bytes 110600 | tf_op jit(solution)/shard_map/ppermute | solution.py:497
  96.7 5.9 %collective-permute-start.16 = (f32[72,128]{1,0:T(8,128)S(1)}, f32[72,128]{1,0:T(8,128)S(1)}, u32[]{:S(2)}, u32[]{:S(2)}) collective-permute-start(f32[72,128]{1,0:T(8,128)S(1)} %add_add_fusion.1), channel_id=1, source_target_pairs={{0,4},{1,5},{2,6},{3,7},{4,0},{5,1},{6,2},{7,3},{8,12},{9,13},{10,... | collective-permute-start | bytes 110600 | tf_op jit(solution)/shard_map/ppermute | solution.py:497
  100.0 5.2 %collective-permute-start.17 = (f32[72,128]{1,0:T(8,128)S(1)}, f32[72,128]{1,0:T(8,128)S(1)}, u32[]{:S(2)}, u32[]{:S(2)}) collective-permute-start(f32[72,128]{1,0:T(8,128)S(1)} %add_add_fusion.1), channel_id=1, source_target_pairs={{0,6},{1,7},{2,4},{3,5},{4,2},{5,3},{6,0},{7,1},{8,14},{9,15},{10,... | collective-permute-start | bytes 110600 | tf_op jit(solution)/shard_map/ppermute | solution.py:497

commit v6 on v5

--- a/solution.py
+++ b/solution.py
@@ -247,8 +247,6 @@
     width = own.shape[1]
     copies = chip_copies((low, own, high), width, x_ref, sems, PAD)
     cot_copies = window_copies(cot_own, cot_mate, cot_ref, cot_sems)
-    out_ref[:C, width:] = table_ref[...]
-    out_ref[C:, width:] = jnp.zeros((2 * BLOCK - C, LANES), out_ref.dtype)
     for copy in copies[0] + cot_copies + copies[1]:
         copy.start()
 
@@ -264,6 +262,11 @@
             out_ref[rows, first:last] = total.astype(out_ref.dtype)
 
     convolve(matrix_ref, x_ref, x3_ref, p3_ref, width, copies, finish)
+    lane = lax.broadcasted_iota(jnp.int32, (C, LANES), 1)
+    edge = out_ref[:C, :LANES].astype(jnp.float32)
+    table = table_ref[...].astype(jnp.float32)
+    table = jnp.where(lane < 3 * CHIP * TAPS, table, jnp.where(lane < PAD - RAD, 0.0, edge))
+    out_ref[:C, :LANES] = table.astype(out_ref.dtype)
 
 
 def conv_scratch(width):
@@ -287,7 +290,7 @@
     return pl.pallas_call(
         forward_kernel,
         out_shape=(
-            jax.ShapeDtypeStruct((2 * BLOCK, width + LANES), jnp.bfloat16),
+            jax.ShapeDtypeStruct((2 * BLOCK, width), jnp.bfloat16),
             jax.ShapeDtypeStruct((REACH * C, width + 2 * PAD), jnp.bfloat16),
         ),
         in_specs=[LOCAL] * 2 + [ANY] * 5,
@@ -338,11 +341,11 @@
     x_ref, x3_ref, p3_ref, o_ref, t_ref, matrix_ref, weight_wide, table_wide,
     sems, table_sems, out_sems,
 ):
-    width = own.shape[1] - LANES
+    width = own.shape[1]
     half = width - 2 * PAD
     table_copies = [
         pltpu.make_async_copy(
-            block.at[0:C, width : width + LANES],
+            block.at[0:C, 0:LANES],
             t_ref.at[:, chip * LANES : (chip + 1) * LANES],
             table_sems.at[chip],
         )
@@ -378,7 +381,7 @@
 
 
 def backward(weights, low, own, high):
-    width = own.shape[1] - LANES
+    width = own.shape[1]
     half = width - 2 * PAD
     return pl.pallas_call(
         backward_kernel,
@@ -408,7 +411,7 @@
 def weight_kernel(
     scale, x_ref, d_ref, table_ref, out_ref, x3_ref, d3_ref, g_ref, w_ref, table_wide
 ):
-    width = d_ref.shape[1] - LANES
+    width = d_ref.shape[1]
     size = width // 2 - PAD
     table_wide[...] = jnp.dot(
         table_ref[...],
@@ -467,7 +470,7 @@
 
 
 def weight_part(joined, delta, table, scale):
-    width = delta.shape[1] - LANES
+    width = delta.shape[1]
     return pl.pallas_call(
         functools.partial(weight_kernel, scale),
         out_shape=jax.ShapeDtypeStruct((K * C // 4, LANES), jnp.float32),

time: 107 us -> 106 us (level)
  local copies, waits for them, and re-layouts: 12.5 us -> 10 us
  Pallas kernels: 23.1 us -> 25.3 us
  waiting for transfers between devices: 37.3 us -> 35.8 us
    unnamed x13 -> x9, local copies, waits for them, and re-layouts: 3.6 us -> 1.33 us
    ppermute x14, waiting for transfers between devices: 27.5 us -> 25.8 us  [swapped(): lax.ppermute(array, 'lat', [(i, i ^ bit) for i in range(lax.axis_size('la...]
    pallas_call x1, Pallas kernels: 6.54 us -> 7.71 us  [weight_part(): pl.pallas_call(functools.partial(weight_kernel, scale), out_shape=jax.Sha...]
  transfers between devices with their start and end apart: 18 -> 18, of which waited for: 9 -> 9; matrix products, arithmetic and copies ran while one was open for 10% -> 10% of each run, Pallas kernels for 15% -> 17%
where the time goes in v6:
time: 106 us; the launch traced here: 105 us
  waiting for transfers between devices  35.8 us (34%)
  starting transfers between devices  30.8 us (29%)
  Pallas kernels  25.3 us (24%)
  local copies, waits for them, and re-layouts  10 us (9%)
  other arithmetic  2.12 us (2%)
  between operations  1.11 us (1%)
    ppermute x14, waiting for transfers between devices, swapped(): lax.ppermute(array, 'lat', [(i, i ^ bit) for i in range(lax.axis_size('la...  25.8 us
    ppermute x4, starting transfers between devices, moved(): lax.ppermute(array, 'lat', [(i, i + by) for i in range(peers) if 0 <= i +...  16.9 us
    ppermute x14, starting transfers between devices, swapped(): lax.ppermute(array, 'lat', [(i, i ^ bit) for i in range(lax.axis_size('la...  13.9 us
    ppermute x4, waiting for transfers between devices, moved(): lax.ppermute(array, 'lat', [(i, i + by) for i in range(peers) if 0 <= i +...  9.97 us
    pallas_call x1, Pallas kernels, backward(): pl.pallas_call(backward_kernel, out_shape=(jax.ShapeDtypeStruct((BLOCK, 2...  8.36 us
    pallas_call x1, Pallas kernels, weight_part(): pl.pallas_call(functools.partial(weight_kernel, scale), out_shape=jax.Sha...  7.71 us
    pallas_call x1, Pallas kernels, forward(): pl.pallas_call(forward_kernel, out_shape=(jax.ShapeDtypeStruct((2 * BLOCK...  6.66 us
    squeeze x2, local copies, waits for them, and re-layouts, forward_table(): rows[:, r]  2.24 us
  transfers between devices with their start and end apart: 18, of which 9 were waited for; matrix products, arithmetic and copies ran while one was open for 10% of the time, Pallas kernels for 17%

profile of v6, /device:TPU:22, one launch (start us, length us, event | category | flops | bytes accessed | tf_op | source)
XLA Modules:
  0.0 105.1 jit_solution(13345279302128317774)
XLA Ops:
  0.7 1.2 %copy-done = bf16[2,32,8192]{2,1,0:T(8,128)(2,1)S(1)} copy-done((bf16[2,32,8192]{2,1,0:T(8,128)(2,1)S(1)}, bf16[2,32,8192]{2,1,0:T(8,128)(2,1)}, u32[]{:S(2)}) %copy-start) | copy-done | bytes 1048600
  2.1 1.5 %collective-permute-done.1.mate = bf16[64,8192]{1,0:T(8,128)(2,1)S(1)} collective-permute-done((bf16[64,8192]{1,0:T(8,128)(2,1)}, bf16[64,8192]{1,0:T(8,128)(2,1)S(1)}, u32[]{:S(2)}, u32[]{:S(2)}) %collective-permute-start.1) | collective-permute-done | bytes 1048608 | tf_op jit(solution)/shard_map/ppermute | solution.py:500
  3.6 0.2 chip_window.1.own
  3.8 4.0 %collective-permute-start.2 = (bf16[128,4352]{1,0:T(8,128)(2,1)S(1)}, bf16[128,4352]{1,0:T(8,128)(2,1)S(1)}, u32[]{:S(2)}, u32[]{:S(2)}) collective-permute-start(bf16[128,4352]{1,0:T(8,128)(2,1)S(1)} %chip_window.1.own), channel_id=1, source_target_pairs={{0,2},{1,3},{2,4},{3,5},{4,6},{5,7},{6,8},{7,9},{8,10},{9,11},{10,... | collective-permute-start | bytes 3342344 | tf_op jit(solution)/shard_map/ppermute | solution.py:494
  7.7 4.3 %collective-permute-start.3 = (bf16[128,4352]{1,0:T(8,128)(2,1)S(1)}, bf16[128,4352]{1,0:T(8,128)(2,1)S(1)}, u32[]{:S(2)}, u32[]{:S(2)}) collective-permute-start(bf16[128,4352]{1,0:T(8,128)(2,1)S(1)} %chip_window.1.own), channel_id=1, source_target_pairs={{2,0},{3,1},{4,2},{5,3},{6,4},{7,5},{8,6},{9,7},{10,8},{11,9},{12,... | collective-permute-start | bytes 3342344 | tf_op jit(solution)/shard_map/ppermute | solution.py:494
  12.0 0.1 collective-permute-start.4
  12.2 0.1 copy.12
  12.3 0.2 broadcast_select_fusion
  12.5 0.6 collective-permute-start
  13.1 1.9 %collective-permute-done = bf16[2,9,9,9]{3,0,2,1:T(2,128)(2,1)} collective-permute-done((bf16[2,9,9,9]{3,0,2,1:T(2,128)(2,1)S(1)}, bf16[2,9,9,9]{3,0,2,1:T(2,128)(2,1)}, u32[]{:S(2)}, u32[]{:S(2)}) %collective-permute-start) | collective-permute-done | bytes 2948 | tf_op jit(solution)/shard_map/ppermute | solution.py:500
  15.0 1.1 %maximum_select_fusion = bf16[4,9,9,9]{3,0,2,1:T(4,128)(2,1)S(1)} fusion(bf16[2,9,9,9]{3,0,2,1:T(2,128)(2,1)} %collective-permute-done, bf16[2,9,9,9]{3,0,2,1:T(2,128)(2,1)S(1)} %broadcast_select_fusion, pred[]{:T(512)S(6)} %eq.3), kind=kLoop, calls=%fused_computation.1 | loop fusion | flops 26244 | bytes 11665 | tf_op jit(solution)/shard_map/jit(_where)/select_n | solution.py:547
  16.0 0.7 rev.3
  16.7 0.8 fusion
  17.5 1.1 %copy.26 = bf16[2,1,9,9,9]{2,0,4,3,1:T(2,128)(2,1)S(1)} copy(bf16[2,1,9,9,9]{4,1,0,3,2:T(2,128)(2,1)} %get-tuple-element.16) | data formatting | bytes 5832 | tf_op jit(solution)/shard_map/squeeze | solution.py:521
  18.6 1.1 %copy.27 = bf16[2,1,9,9,9]{2,0,4,3,1:T(2,128)(2,1)S(1)} copy(bf16[2,1,9,9,9]{4,1,0,3,2:T(2,128)(2,1)} %get-tuple-element.17) | data formatting | bytes 5832 | tf_op jit(solution)/shard_map/squeeze | solution.py:521
  19.8 0.1 pad.13.clone
  19.9 0.8 maximum_bitcast_fusion
  20.7 1.2 %copy.17 = bf16[2,3,2,9,10,3]{3,2,1,0,5,4:T(2,128)(2,1)S(1)} copy(bf16[2,3,2,9,10,3]{4,0,3,5,1,2:T(2,128)(2,1)} %maximum_bitcast_fusion) | data formatting | bytes 12960 | tf_op jit(solution)/shard_map/transpose | solution.py:513
  21.9 0.1 reshape.49
  22.0 0.1 copy.18.table_ref
  22.1 0.9 copy.29
  23.1 0.7 reshape.52
  23.8 0.8 copy.20
  24.7 1.5 %make_filter.1.matrix_ref = bf16[384,960]{1,0:T(8,128)(2,1)S(1)} custom-call(bf16[108,30]{1,0:T(8,128)(2,1)S(1)} %copy.18.table_ref, bf16[288,32]{1,0:T(8,128)(2,1)S(1)} %bitcast.25), custom_call_target="tpu_custom_call" | custom-call | tf_op jit(solution)/shard_map/make_filter/pallas_call | solution.py:61
  26.2 8.8 %collective-permute-done.2.low = bf16[128,4352]{1,0:T(8,128)(2,1)S(1)} collective-permute-done((bf16[128,4352]{1,0:T(8,128)(2,1)S(1)}, bf16[128,4352]{1,0:T(8,128)(2,1)S(1)}, u32[]{:S(2)}, u32[]{:S(2)}) %collective-permute-start.2) | collective-permute-done | bytes 1114144 | tf_op jit(solution)/shard_map/ppermute | solution.py:494
  35.0 1.2 %collective-permute-done.3.high = bf16[128,4352]{1,0:T(8,128)(2,1)S(1)} collective-permute-done((bf16[128,4352]{1,0:T(8,128)(2,1)S(1)}, bf16[128,4352]{1,0:T(8,128)(2,1)S(1)}, u32[]{:S(2)}, u32[]{:S(2)}) %collective-permute-start.3) | collective-permute-done | bytes 1114144 | tf_op jit(solution)/shard_map/ppermute | solution.py:494
  36.1 6.7 %forward_conv.1 = (bf16[128,4352]{1,0:T(8,128)(2,1)}, bf16[384,4608]{1,0:T(8,128)(2,1)S(1)}) custom-call(bf16[384,960]{1,0:T(8,128)(2,1)S(1)} %make_filter.1.matrix_ref, bf16[32,128]{1,0:T(8,128)(2,1)S(1)} %pad.14.table_ref, bf16[128,4352]{1,0:T(8,128)(2,1)S(1)} %collective-permute-done.2.low, bf16[128,4352]{1,0:T(8,128)(2,1)S(1)} %chip_window.1.own, ...), custom_call_target="tpu_custom_call" | custom-call | flops 3208642560 | bytes 5570560 | tf_op jit(solution)/shard_map/forward_conv/pallas_call | solution.py:290
  42.8 3.6 %collective-permute-start.5 = (bf16[128,4352]{1,0:T(8,128)(2,1)}, bf16[128,4352]{1,0:T(8,128)(2,1)S(1)}, u32[]{:S(2)}, u32[]{:S(2)}) collective-permute-start(bf16[128,4352]{1,0:T(8,128)(2,1)} %get-tuple-element.9.d_ref.own), channel_id=1, source_target_pairs={{0,2},{1,3},{2,4},{3,5},{4,6},{5,7},{6,8},{7,9},{8,10},{9,11},{10,... | collective-permute-start | bytes 3342344 | tf_op jit(solution)/shard_map/ppermute | solution.py:494
  46.5 5.0 %collective-permute-start.6 = (bf16[128,4352]{1,0:T(8,128)(2,1)}, bf16[128,4352]{1,0:T(8,128)(2,1)S(1)}, u32[]{:S(2)}, u32[]{:S(2)}) collective-permute-start(bf16[128,4352]{1,0:T(8,128)(2,1)} %get-tuple-element.9.d_ref.own), channel_id=1, source_target_pairs={{2,0},{3,1},{4,2},{5,3},{6,4},{7,5},{8,6},{9,7},{10,8},{11,9},{12,... | collective-permute-start | bytes 3342344 | tf_op jit(solution)/shard_map/ppermute | solution.py:494
  51.4 7.7 %weight_part.1 = f32[72,128]{1,0:T(8,128)S(1)} custom-call(bf16[384,4608]{1,0:T(8,128)(2,1)S(1)} %get-tuple-element.10.x_ref, bf16[128,4352]{1,0:T(8,128)(2,1)} %get-tuple-element.9.d_ref.own, bf16[108,30]{1,0:T(8,128)(2,1)S(1)} %copy.18.table_ref), custom_call_target="tpu_custom_call" | custom-call | flops 3208642560 | bytes 4456448 | tf_op jit(solution)/shard_map/weight_part/pallas_call | solution.py:474
  59.1 0.1 collective-permute-start.7
  59.2 1.2 %collective-permute-done.7 = f32[72,128]{1,0:T(8,128)S(1)} collective-permute-done((f32[72,128]{1,0:T(8,128)S(1)}, f32[72,128]{1,0:T(8,128)S(1)}, u32[]{:S(2)}, u32[]{:S(2)}) %collective-permute-start.7) | collective-permute-done | bytes 36896 | tf_op jit(solution)/shard_map/ppermute | solution.py:500
  60.4 0.5 collective-permute-start.10
  60.9 1.1 %collective-permute-start.8 = (f32[72,128]{1,0:T(8,128)S(1)}, f32[72,128]{1,0:T(8,128)S(1)}, u32[]{:S(2)}, u32[]{:S(2)}) collective-permute-start(f32[72,128]{1,0:T(8,128)S(1)} %add.41), channel_id=1, source_target_pairs={{0,32},{1,33},{2,34},{3,35},{4,36},{5,37},{6,38},{7,39},{8,40},{9,... | collective-permute-start | bytes 110600 | tf_op jit(solution)/shard_map/ppermute | solution.py:500
  61.9 2.0 %collective-permute-start.9 = (f32[72,128]{1,0:T(8,128)S(1)}, f32[72,128]{1,0:T(8,128)S(1)}, u32[]{:S(2)}, u32[]{:S(2)}) collective-permute-start(f32[72,128]{1,0:T(8,128)S(1)} %add.41), channel_id=1, source_target_pairs={{0,64},{1,65},{2,66},{3,67},{4,68},{5,69},{6,70},{7,71},{8,72},{9,... | collective-permute-start | bytes 110600 | tf_op jit(solution)/shard_map/ppermute | solution.py:500
  63.9 0.1 copy.11
  64.0 15.2 %collective-permute-done.10 = f32[72,128]{1,0:T(8,128)S(1)} collective-permute-done((f32[72,128]{1,0:T(8,128)S(1)}, f32[72,128]{1,0:T(8,128)S(1)}, u32[]{:S(2)}, u32[]{:S(2)}) %collective-permute-start.10) | collective-permute-done | bytes 36896 | tf_op jit(solution)/shard_map/ppermute | solution.py:500
  79.2 2.2 %collective-permute-done.8 = f32[72,128]{1,0:T(8,128)S(1)} collective-permute-done((f32[72,128]{1,0:T(8,128)S(1)}, f32[72,128]{1,0:T(8,128)S(1)}, u32[]{:S(2)}, u32[]{:S(2)}) %collective-permute-start.8) | collective-permute-done | bytes 36896 | tf_op jit(solution)/shard_map/ppermute | solution.py:500
  81.6 0.1 collective-permute-start.13
  81.7 4.6 %collective-permute-start.14 = (f32[72,128]{1,0:T(8,128)S(1)}, f32[72,128]{1,0:T(8,128)S(1)}, u32[]{:S(2)}, u32[]{:S(2)}) collective-permute-start(f32[72,128]{1,0:T(8,128)S(1)} %add_add_fusion.2), channel_id=1, source_target_pairs={{0,24},{1,25},{2,26},{3,27},{4,28},{5,29},{6,30},{7,31},{8,16},{9,... | collective-permute-start | bytes 110600 | tf_op jit(solution)/shard_map/ppermute | solution.py:500
  86.3 8.4 %input_conv.1 = (bf16[64,8192]{1,0:T(8,128)(2,1)}, bf16[64,4096]{1,0:T(8,128)(2,1)S(1)}) custom-call(bf16[288,32]{1,0:T(8,128)(2,1)S(1)} %bitcast.27, bf16[128,4352]{1,0:T(8,128)(2,1)S(1)} %collective-permute-done.5.low, bf16[128,4352]{1,0:T(8,128)(2,1)} %get-tuple-element.9.d_ref.own, bf16[128,4352]{1,0:T(8,128)(2,1)S(1)} %collective-permute-done.6.high), custom_call_target="tpu_custom_call" | custom-call | flops 3208642560 | bytes 4456448 | tf_op jit(solution)/shard_map/input_conv/pallas_call | solution.py:386
  94.8 0.1 collective-permute-start.15
  94.9 3.2 %collective-permute-start.16 = (f32[72,128]{1,0:T(8,128)S(1)}, f32[72,128]{1,0:T(8,128)S(1)}, u32[]{:S(2)}, u32[]{:S(2)}) collective-permute-start(f32[72,128]{1,0:T(8,128)S(1)} %add_add_fusion.1), channel_id=1, source_target_pairs={{0,4},{1,5},{2,6},{3,7},{4,0},{5,1},{6,2},{7,3},{8,12},{9,13},{10,... | collective-permute-start | bytes 110600 | tf_op jit(solution)/shard_map/ppermute | solution.py:500
  98.1 1.5 %collective-permute-start.17 = (f32[72,128]{1,0:T(8,128)S(1)}, f32[72,128]{1,0:T(8,128)S(1)}, u32[]{:S(2)}, u32[]{:S(2)}) collective-permute-start(f32[72,128]{1,0:T(8,128)S(1)} %add_add_fusion.1), channel_id=1, source_target_pairs={{0,6},{1,7},{2,4},{3,5},{4,2},{5,3},{6,0},{7,1},{8,14},{9,15},{10,... | collective-permute-start | bytes 110600 | tf_op jit(solution)/shard_map/ppermute | solution.py:500
  99.6 1.2 %collective-permute-done.16 = f32[72,128]{1,0:T(8,128)S(1)} collective-permute-done((f32[72,128]{1,0:T(8,128)S(1)}, f32[72,128]{1,0:T(8,128)S(1)}, u32[]{:S(2)}, u32[]{:S(2)}) %collective-permute-start.16) | collective-permute-done | bytes 36896 | tf_op jit(solution)/shard_map/ppermute | solution.py:500
  100.8 2.5 %collective-permute-done.17 = f32[72,128]{1,0:T(8,128)S(1)} collective-permute-done((f32[72,128]{1,0:T(8,128)S(1)}, f32[72,128]{1,0:T(8,128)S(1)}, u32[]{:S(2)}, u32[]{:S(2)}) %collective-permute-start.17) | collective-permute-done | bytes 36896 | tf_op jit(solution)/shard_map/ppermute | solution.py:500
  103.3 0.8 reshape.56
  104.1 0.8 join.1
  (28 shorter events, 0.6 us)
Async XLA Ops:
  0.6 3.0 %collective-permute-start.1 = (bf16[64,8192]{1,0:T(8,128)(2,1)}, bf16[64,8192]{1,0:T(8,128)(2,1)S(1)}, u32[]{:S(2)}, u32[]{:S(2)}) collective-permute-start(bf16[64,8192]{1,0:T(8,128)(2,1)} %bitcast.23), channel_id=1, source_target_pairs={{0,1},{1,0},{2,3},{3,2},{4,5},{5,4},{6,7},{7,6},{8,9},{9,8},{10,11... | collective-permute-start | bytes 3145736 | tf_op jit(solution)/shard_map/ppermute | solution.py:500
  0.7 1.2 %copy-start = (bf16[2,32,8192]{2,1,0:T(8,128)(2,1)S(1)}, bf16[2,32,8192]{2,1,0:T(8,128)(2,1)}, u32[]{:S(2)}) copy-start(bf16[2,32,8192]{2,1,0:T(8,128)(2,1)} %param.5) | copy-start | bytes 3145732
  2.0 10.1 %copy-start.3 = (s32[2,9]{1,0:T(2,128)S(1)}, s32[2,9]{1,0:T(2,128)}, u32[]{:S(2)}) copy-start(s32[2,9]{1,0:T(2,128)} %param.8) | copy-start | bytes 220
  2.0 10.3 %copy-start.2 = (bf16[2,9,9,9]{3,0,2,1:T(2,128)(2,1)S(1)}, bf16[2,9,9,9]{3,0,2,1:T(2,128)(2,1)}, u32[]{:S(2)}) copy-start(bf16[2,9,9,9]{3,0,2,1:T(2,128)(2,1)} %param.7) | copy-start | bytes 8752
  3.8 20.9 %copy-start.1 = (bf16[9,32,32]{2,1,0:T(8,128)(2,1)S(1)}, bf16[9,32,32]{2,1,0:T(8,128)(2,1)}, u32[]{:S(2)}) copy-start(bf16[9,32,32]{2,1,0:T(8,128)(2,1)} %param.9) | copy-start | bytes 55300
  3.8 31.2 %collective-permute-start.2 = (bf16[128,4352]{1,0:T(8,128)(2,1)S(1)}, bf16[128,4352]{1,0:T(8,128)(2,1)S(1)}, u32[]{:S(2)}, u32[]{:S(2)}) collective-permute-start(bf16[128,4352]{1,0:T(8,128)(2,1)S(1)} %chip_window.1.own), channel_id=1, source_target_pairs={{0,2},{1,3},{2,4},{3,5},{4,6},{5,7},{6,8},{7,9},{8,10},{9,11},{10,... | collective-permute-start | bytes 3342344 | tf_op jit(solution)/shard_map/ppermute | solution.py:494
  7.7 28.4 %collective-permute-start.3 = (bf16[128,4352]{1,0:T(8,128)(2,1)S(1)}, bf16[128,4352]{1,0:T(8,128)(2,1)S(1)}, u32[]{:S(2)}, u32[]{:S(2)}) collective-permute-start(bf16[128,4352]{1,0:T(8,128)(2,1)S(1)} %chip_window.1.own), channel_id=1, source_target_pairs={{2,0},{3,1},{4,2},{5,3},{6,4},{7,5},{8,6},{9,7},{10,8},{11,9},{12,... | collective-permute-start | bytes 3342344 | tf_op jit(solution)/shard_map/ppermute | solution.py:494
  12.0 14.1 %collective-permute-start.4 = (bf16[64,8192]{1,0:T(8,128)(2,1)}, bf16[64,8192]{1,0:T(8,128)(2,1)}, u32[]{:S(2)}, u32[]{:S(2)}) collective-permute-start(bf16[64,8192]{1,0:T(8,128)(2,1)} %bitcast.12.cot_own), channel_id=1, source_target_pairs={{0,1},{1,0},{2,3},{3,2},{4,5},{5,4},{6,7},{7,6},{8,9},{9,8},{10,11... | collective-permute-start | bytes 3145736 | tf_op jit(solution)/shard_map/ppermute | solution.py:500
  12.5 2.5 %collective-permute-start = (bf16[2,9,9,9]{3,0,2,1:T(2,128)(2,1)S(1)}, bf16[2,9,9,9]{3,0,2,1:T(2,128)(2,1)}, u32[]{:S(2)}, u32[]{:S(2)}) collective-permute-start(bf16[2,9,9,9]{3,0,2,1:T(2,128)(2,1)S(1)} %broadcast_select_fusion), channel_id=1, source_target_pairs={{0,1},{1,0},{2,3},{3,2},{4,5},{5,4},{6,7},{7,6},{8,9},{9,8},{10,11... | collective-permute-start | bytes 8756 | tf_op jit(solution)/shard_map/ppermute | solution.py:500
  42.8 38.7 %collective-permute-start.5 = (bf16[128,4352]{1,0:T(8,128)(2,1)}, bf16[128,4352]{1,0:T(8,128)(2,1)S(1)}, u32[]{:S(2)}, u32[]{:S(2)}) collective-permute-start(bf16[128,4352]{1,0:T(8,128)(2,1)} %get-tuple-element.9.d_ref.own), channel_id=1, source_target_pairs={{0,2},{1,3},{2,4},{3,5},{4,6},{5,7},{6,8},{7,9},{8,10},{9,11},{10,... | collective-permute-start | bytes 3342344 | tf_op jit(solution)/shard_map/ppermute | solution.py:494
  46.5 35.1 %collective-permute-start.6 = (bf16[128,4352]{1,0:T(8,128)(2,1)}, bf16[128,4352]{1,0:T(8,128)(2,1)S(1)}, u32[]{:S(2)}, u32[]{:S(2)}) collective-permute-start(bf16[128,4352]{1,0:T(8,128)(2,1)} %get-tuple-element.9.d_ref.own), channel_id=1, source_target_pairs={{2,0},{3,1},{4,2},{5,3},{6,4},{7,5},{8,6},{9,7},{10,8},{11,9},{12,... | collective-permute-start | bytes 3342344 | tf_op jit(solution)/shard_map/ppermute | solution.py:494
  59.1 1.3 %collective-permute-start.7 = (f32[72,128]{1,0:T(8,128)S(1)}, f32[72,128]{1,0:T(8,128)S(1)}, u32[]{:S(2)}, u32[]{:S(2)}) collective-permute-start(f32[72,128]{1,0:T(8,128)S(1)} %weight_part.1), channel_id=1, source_target_pairs={{0,1},{1,0},{2,3},{3,2},{4,5},{5,4},{6,7},{7,6},{8,9},{9,8},{10,11... | collective-permute-start | bytes 110600 | tf_op jit(solution)/shard_map/ppermute | solution.py:500
  60.4 18.8 %collective-permute-start.10 = (f32[72,128]{1,0:T(8,128)S(1)}, f32[72,128]{1,0:T(8,128)S(1)}, u32[]{:S(2)}, u32[]{:S(2)}) collective-permute-start(f32[72,128]{1,0:T(8,128)S(1)} %add.41), channel_id=1, source_target_pairs={{0,96},{1,97},{2,98},{3,99},{4,100},{5,101},{6,102},{7,103},{8,104... | collective-permute-start | bytes 110600 | tf_op jit(solution)/shard_map/ppermute | solution.py:500
  60.9 20.6 %collective-permute-start.8 = (f32[72,128]{1,0:T(8,128)S(1)}, f32[72,128]{1,0:T(8,128)S(1)}, u32[]{:S(2)}, u32[]{:S(2)}) collective-permute-start(f32[72,128]{1,0:T(8,128)S(1)} %add.41), channel_id=1, source_target_pairs={{0,32},{1,33},{2,34},{3,35},{4,36},{5,37},{6,38},{7,39},{8,40},{9,... | collective-permute-start | bytes 110600 | tf_op jit(solution)/shard_map/ppermute | solution.py:500
  61.9 19.5 %collective-permute-start.9 = (f32[72,128]{1,0:T(8,128)S(1)}, f32[72,128]{1,0:T(8,128)S(1)}, u32[]{:S(2)}, u32[]{:S(2)}) collective-permute-start(f32[72,128]{1,0:T(8,128)S(1)} %add.41), channel_id=1, source_target_pairs={{0,64},{1,65},{2,66},{3,67},{4,68},{5,69},{6,70},{7,71},{8,72},{9,... | collective-permute-start | bytes 110600 | tf_op jit(solution)/shard_map/ppermute | solution.py:500
  81.5 13.2 %collective-permute-start.12 = (f32[72,128]{1,0:T(8,128)S(1)}, f32[72,128]{1,0:T(8,128)S(1)}, u32[]{:S(2)}, u32[]{:S(2)}) collective-permute-start(f32[72,128]{1,0:T(8,128)S(1)} %add_add_fusion.2), channel_id=1, source_target_pairs={{0,8},{1,9},{2,10},{3,11},{4,12},{5,13},{6,14},{7,15},{8,0},{9,1},... | collective-permute-start | bytes 110600 | tf_op jit(solution)/shard_map/ppermute | solution.py:500
  81.6 13.2 %collective-permute-start.13 = (f32[72,128]{1,0:T(8,128)S(1)}, f32[72,128]{1,0:T(8,128)S(1)}, u32[]{:S(2)}, u32[]{:S(2)}) collective-permute-start(f32[72,128]{1,0:T(8,128)S(1)} %add_add_fusion.2), channel_id=1, source_target_pairs={{0,16},{1,17},{2,18},{3,19},{4,20},{5,21},{6,22},{7,23},{8,24},{9,... | collective-permute-start | bytes 110600 | tf_op jit(solution)/shard_map/ppermute | solution.py:500
  81.7 13.1 %collective-permute-start.14 = (f32[72,128]{1,0:T(8,128)S(1)}, f32[72,128]{1,0:T(8,128)S(1)}, u32[]{:S(2)}, u32[]{:S(2)}) collective-permute-start(f32[72,128]{1,0:T(8,128)S(1)} %add_add_fusion.2), channel_id=1, source_target_pairs={{0,24},{1,25},{2,26},{3,27},{4,28},{5,29},{6,30},{7,31},{8,16},{9,... | collective-permute-start | bytes 110600 | tf_op jit(solution)/shard_map/ppermute | solution.py:500
  94.7 9.4 %collective-permute-start.11 = (bf16[64,4096]{1,0:T(8,128)(2,1)S(1)}, bf16[64,4096]{1,0:T(8,128)(2,1)S(1)}, u32[]{:S(2)}, u32[]{:S(2)}) collective-permute-start(bf16[64,4096]{1,0:T(8,128)(2,1)S(1)} %get-tuple-element.13), channel_id=1, source_target_pairs={{0,1},{1,0},{2,3},{3,2},{4,5},{5,4},{6,7},{7,6},{8,9},{9,8},{10,11... | collective-permute-start | bytes 1572872 | tf_op jit(solution)/shard_map/ppermute | solution.py:500
  94.8 4.8 %collective-permute-start.15 = (f32[72,128]{1,0:T(8,128)S(1)}, f32[72,128]{1,0:T(8,128)S(1)}, u32[]{:S(2)}, u32[]{:S(2)}) collective-permute-start(f32[72,128]{1,0:T(8,128)S(1)} %add_add_fusion.1), channel_id=1, source_target_pairs={{0,2},{1,3},{2,0},{3,1},{4,6},{5,7},{6,4},{7,5},{8,10},{9,11},{10,... | collective-permute-start | bytes 110600 | tf_op jit(solution)/shard_map/ppermute | solution.py:500
  94.9 5.9 %collective-permute-start.16 = (f32[72,128]{1,0:T(8,128)S(1)}, f32[72,128]{1,0:T(8,128)S(1)}, u32[]{:S(2)}, u32[]{:S(2)}) collective-permute-start(f32[72,128]{1,0:T(8,128)S(1)} %add_add_fusion.1), channel_id=1, source_target_pairs={{0,4},{1,5},{2,6},{3,7},{4,0},{5,1},{6,2},{7,3},{8,12},{9,13},{10,... | collective-permute-start | bytes 110600 | tf_op jit(solution)/shard_map/ppermute | solution.py:500
  98.1 5.2 %collective-permute-start.17 = (f32[72,128]{1,0:T(8,128)S(1)}, f32[72,128]{1,0:T(8,128)S(1)}, u32[]{:S(2)}, u32[]{:S(2)}) collective-permute-start(f32[72,128]{1,0:T(8,128)S(1)} %add_add_fusion.1), channel_id=1, source_target_pairs={{0,6},{1,7},{2,4},{3,5},{4,2},{5,3},{6,0},{7,1},{8,14},{9,15},{10,... | collective-permute-start | bytes 110600 | tf_op jit(solution)/shard_map/ppermute | solution.py:500

commit v7 on v6

--- a/solution.py
+++ b/solution.py
@@ -227,7 +227,7 @@
                 x3_ref[tile, b * STEP : b * STEP + DEEP, :],
                 preferred_element_type=jnp.float32,
             )
-        finish(0 if tile == 0 else size - PAD, width if tile == 1 else size - PAD)
+            finish(b, 0 if tile == 0 else size - PAD, width if tile == 1 else size - PAD)
 
 
 def post_shift(p3_ref, b, first, last):
@@ -250,16 +250,15 @@
     for copy in copies[0] + cot_copies + copies[1]:
         copy.start()
 
-    def finish(first, last):
-        if first == 0:
+    def finish(b, first, last):
+        if first == 0 and b == 0:
             wait_for(cot_copies)
-        for b in range(2):
-            rows = slice(b * BLOCK, (b + 1) * BLOCK)
-            total = post_shift(p3_ref, b, first, last)
-            cot = cot_ref[rows, first:last].astype(jnp.float32)
-            sg = jax.nn.sigmoid(total)
-            total = cot * sg * (1.0 + total * (1.0 - sg))
-            out_ref[rows, first:last] = total.astype(out_ref.dtype)
+        rows = slice(b * BLOCK, (b + 1) * BLOCK)
+        total = post_shift(p3_ref, b, first, last)
+        cot = cot_ref[rows, first:last].astype(jnp.float32)
+        sg = jax.nn.sigmoid(total)
+        total = cot * sg * (1.0 + total * (1.0 - sg))
+        out_ref[rows, first:last] = total.astype(out_ref.dtype)
 
     convolve(matrix_ref, x_ref, x3_ref, p3_ref, width, copies, finish)
     lane = lax.broadcasted_iota(jnp.int32, (C, LANES), 1)
@@ -357,13 +356,10 @@
     wait_for(table_copies)
     input_filter(t_ref[...], weight_ref, matrix_ref, weight_wide, table_wide)
 
-    def finish(first, last):
+    def finish(b, first, last):
         first, last = max(first, PAD), min(last, width - PAD)
-        for b in range(2):
-            total = post_shift(p3_ref, b, first, last)
-            o_ref[b * BLOCK : (b + 1) * BLOCK, first - PAD : last - PAD] = total.astype(
-                o_ref.dtype
-            )
+        total = post_shift(p3_ref, b, first, last)
+        o_ref[b * BLOCK : (b + 1) * BLOCK, first - PAD : last - PAD] = total.astype(o_ref.dtype)
 
     convolve(matrix_ref, x_ref, x3_ref, p3_ref, width, copies, finish)
     mine = pl.multiple_of(core() * BLOCK, BLOCK)

time: 106 us -> 105 us (level)
  no operation moved by 1% of the time
where the time goes in v7:
time: 105 us
  waiting for transfers between devices  35.8 us (34%)
  starting transfers between devices  30.8 us (29%)
  Pallas kernels  24.9 us (24%)
  local copies, waits for them, and re-layouts  10 us (10%)
  other arithmetic  2.12 us (2%)
  between operations  1.11 us (1%)
    ppermute x14, waiting for transfers between devices, swapped(): lax.ppermute(array, 'lat', [(i, i ^ bit) for i in range(lax.axis_size('la...  25.8 us
    ppermute x4, starting transfers between devices, moved(): lax.ppermute(array, 'lat', [(i, i + by) for i in range(peers) if 0 <= i +...  16.9 us
    ppermute x14, starting transfers between devices, swapped(): lax.ppermute(array, 'lat', [(i, i ^ bit) for i in range(lax.axis_size('la...  13.9 us
    ppermute x4, waiting for transfers between devices, moved(): lax.ppermute(array, 'lat', [(i, i + by) for i in range(peers) if 0 <= i +...  9.97 us
    pallas_call x1, Pallas kernels, backward(): pl.pallas_call(backward_kernel, out_shape=(jax.ShapeDtypeStruct((BLOCK, 2...  8.36 us
    pallas_call x1, Pallas kernels, weight_part(): pl.pallas_call(functools.partial(weight_kernel, scale), out_shape=jax.Sha...  7.71 us
    pallas_call x1, Pallas kernels, forward(): pl.pallas_call(forward_kernel, out_shape=(jax.ShapeDtypeStruct((2 * BLOCK...  6.29 us
    squeeze x2, local copies, waits for them, and re-layouts, forward_table(): rows[:, r]  2.24 us
  transfers between devices with their start and end apart: 18, of which 9 were waited for; matrix products, arithmetic and copies ran while one was open for 10% of the time, Pallas kernels for 17%

profile of v7, /device:TPU:22, one launch (start us, length us, event | category | flops | bytes accessed | tf_op | source)
XLA Modules:
  0.0 104.7 jit_solution(15435002511486859839)
XLA Ops:
  0.7 1.2 %copy-done = bf16[2,32,8192]{2,1,0:T(8,128)(2,1)S(1)} copy-done((bf16[2,32,8192]{2,1,0:T(8,128)(2,1)S(1)}, bf16[2,32,8192]{2,1,0:T(8,128)(2,1)}, u32[]{:S(2)}) %copy-start) | copy-done | bytes 1048600
  2.1 1.5 %collective-permute-done.1.mate = bf16[64,8192]{1,0:T(8,128)(2,1)S(1)} collective-permute-done((bf16[64,8192]{1,0:T(8,128)(2,1)}, bf16[64,8192]{1,0:T(8,128)(2,1)S(1)}, u32[]{:S(2)}, u32[]{:S(2)}) %collective-permute-start.1) | collective-permute-done | bytes 1048608 | tf_op jit(solution)/shard_map/ppermute | solution.py:496
  3.6 0.2 chip_window.1.own
  3.8 4.0 %collective-permute-start.2 = (bf16[128,4352]{1,0:T(8,128)(2,1)S(1)}, bf16[128,4352]{1,0:T(8,128)(2,1)S(1)}, u32[]{:S(2)}, u32[]{:S(2)}) collective-permute-start(bf16[128,4352]{1,0:T(8,128)(2,1)S(1)} %chip_window.1.own), channel_id=1, source_target_pairs={{0,2},{1,3},{2,4},{3,5},{4,6},{5,7},{6,8},{7,9},{8,10},{9,11},{10,... | collective-permute-start | bytes 3342344 | tf_op jit(solution)/shard_map/ppermute | solution.py:490
  7.7 4.3 %collective-permute-start.3 = (bf16[128,4352]{1,0:T(8,128)(2,1)S(1)}, bf16[128,4352]{1,0:T(8,128)(2,1)S(1)}, u32[]{:S(2)}, u32[]{:S(2)}) collective-permute-start(bf16[128,4352]{1,0:T(8,128)(2,1)S(1)} %chip_window.1.own), channel_id=1, source_target_pairs={{2,0},{3,1},{4,2},{5,3},{6,4},{7,5},{8,6},{9,7},{10,8},{11,9},{12,... | collective-permute-start | bytes 3342344 | tf_op jit(solution)/shard_map/ppermute | solution.py:490
  12.0 0.1 collective-permute-start.4
  12.2 0.1 copy.12
  12.3 0.2 broadcast_select_fusion
  12.5 0.6 collective-permute-start
  13.1 1.9 %collective-permute-done = bf16[2,9,9,9]{3,0,2,1:T(2,128)(2,1)} collective-permute-done((bf16[2,9,9,9]{3,0,2,1:T(2,128)(2,1)S(1)}, bf16[2,9,9,9]{3,0,2,1:T(2,128)(2,1)}, u32[]{:S(2)}, u32[]{:S(2)}) %collective-permute-start) | collective-permute-done | bytes 2948 | tf_op jit(solution)/shard_map/ppermute | solution.py:496
  15.0 1.1 %maximum_select_fusion = bf16[4,9,9,9]{3,0,2,1:T(4,128)(2,1)S(1)} fusion(bf16[2,9,9,9]{3,0,2,1:T(2,128)(2,1)} %collective-permute-done, bf16[2,9,9,9]{3,0,2,1:T(2,128)(2,1)S(1)} %broadcast_select_fusion, pred[]{:T(512)S(6)} %eq.3), kind=kLoop, calls=%fused_computation.1 | loop fusion | flops 26244 | bytes 11665 | tf_op jit(solution)/shard_map/jit(_where)/select_n | solution.py:543
  16.0 0.7 rev.3
  16.7 0.8 fusion
  17.5 1.1 %copy.26 = bf16[2,1,9,9,9]{2,0,4,3,1:T(2,128)(2,1)S(1)} copy(bf16[2,1,9,9,9]{4,1,0,3,2:T(2,128)(2,1)} %get-tuple-element.16) | data formatting | bytes 5832 | tf_op jit(solution)/shard_map/squeeze | solution.py:517
  18.6 1.1 %copy.27 = bf16[2,1,9,9,9]{2,0,4,3,1:T(2,128)(2,1)S(1)} copy(bf16[2,1,9,9,9]{4,1,0,3,2:T(2,128)(2,1)} %get-tuple-element.17) | data formatting | bytes 5832 | tf_op jit(solution)/shard_map/squeeze | solution.py:517
  19.8 0.1 pad.13.clone
  19.9 0.8 maximum_bitcast_fusion
  20.7 1.2 %copy.17 = bf16[2,3,2,9,10,3]{3,2,1,0,5,4:T(2,128)(2,1)S(1)} copy(bf16[2,3,2,9,10,3]{4,0,3,5,1,2:T(2,128)(2,1)} %maximum_bitcast_fusion) | data formatting | bytes 12960 | tf_op jit(solution)/shard_map/transpose | solution.py:509
  21.9 0.1 reshape.49
  22.0 0.1 copy.18.table_ref
  22.1 0.9 copy.29
  23.1 0.7 reshape.52
  23.8 0.8 copy.20
  24.7 1.5 %make_filter.1.matrix_ref = bf16[384,960]{1,0:T(8,128)(2,1)S(1)} custom-call(bf16[108,30]{1,0:T(8,128)(2,1)S(1)} %copy.18.table_ref, bf16[288,32]{1,0:T(8,128)(2,1)S(1)} %bitcast.25), custom_call_target="tpu_custom_call" | custom-call | tf_op jit(solution)/shard_map/make_filter/pallas_call | solution.py:61
  26.2 8.8 %collective-permute-done.2.low = bf16[128,4352]{1,0:T(8,128)(2,1)S(1)} collective-permute-done((bf16[128,4352]{1,0:T(8,128)(2,1)S(1)}, bf16[128,4352]{1,0:T(8,128)(2,1)S(1)}, u32[]{:S(2)}, u32[]{:S(2)}) %collective-permute-start.2) | collective-permute-done | bytes 1114144 | tf_op jit(solution)/shard_map/ppermute | solution.py:490
  35.0 1.2 %collective-permute-done.3.high = bf16[128,4352]{1,0:T(8,128)(2,1)S(1)} collective-permute-done((bf16[128,4352]{1,0:T(8,128)(2,1)S(1)}, bf16[128,4352]{1,0:T(8,128)(2,1)S(1)}, u32[]{:S(2)}, u32[]{:S(2)}) %collective-permute-start.3) | collective-permute-done | bytes 1114144 | tf_op jit(solution)/shard_map/ppermute | solution.py:490
  36.1 6.3 %forward_conv.1 = (bf16[128,4352]{1,0:T(8,128)(2,1)}, bf16[384,4608]{1,0:T(8,128)(2,1)S(1)}) custom-call(bf16[384,960]{1,0:T(8,128)(2,1)S(1)} %make_filter.1.matrix_ref, bf16[32,128]{1,0:T(8,128)(2,1)S(1)} %pad.14.table_ref, bf16[128,4352]{1,0:T(8,128)(2,1)S(1)} %collective-permute-done.2.low, bf16[128,4352]{1,0:T(8,128)(2,1)S(1)} %chip_window.1.own, ...), custom_call_target="tpu_custom_call" | custom-call | flops 3208642560 | bytes 5570560 | tf_op jit(solution)/shard_map/forward_conv/pallas_call | solution.py:289
  42.4 3.6 %collective-permute-start.5 = (bf16[128,4352]{1,0:T(8,128)(2,1)}, bf16[128,4352]{1,0:T(8,128)(2,1)S(1)}, u32[]{:S(2)}, u32[]{:S(2)}) collective-permute-start(bf16[128,4352]{1,0:T(8,128)(2,1)} %get-tuple-element.9.d_ref.own), channel_id=1, source_target_pairs={{0,2},{1,3},{2,4},{3,5},{4,6},{5,7},{6,8},{7,9},{8,10},{9,11},{10,... | collective-permute-start | bytes 3342344 | tf_op jit(solution)/shard_map/ppermute | solution.py:490
  46.1 5.0 %collective-permute-start.6 = (bf16[128,4352]{1,0:T(8,128)(2,1)}, bf16[128,4352]{1,0:T(8,128)(2,1)S(1)}, u32[]{:S(2)}, u32[]{:S(2)}) collective-permute-start(bf16[128,4352]{1,0:T(8,128)(2,1)} %get-tuple-element.9.d_ref.own), channel_id=1, source_target_pairs={{2,0},{3,1},{4,2},{5,3},{6,4},{7,5},{8,6},{9,7},{10,8},{11,9},{12,... | collective-permute-start | bytes 3342344 | tf_op jit(solution)/shard_map/ppermute | solution.py:490
  51.1 7.7 %weight_part.1 = f32[72,128]{1,0:T(8,128)S(1)} custom-call(bf16[384,4608]{1,0:T(8,128)(2,1)S(1)} %get-tuple-element.10.x_ref, bf16[128,4352]{1,0:T(8,128)(2,1)} %get-tuple-element.9.d_ref.own, bf16[108,30]{1,0:T(8,128)(2,1)S(1)} %copy.18.table_ref), custom_call_target="tpu_custom_call" | custom-call | flops 3208642560 | bytes 4456448 | tf_op jit(solution)/shard_map/weight_part/pallas_call | solution.py:470
  58.8 0.1 collective-permute-start.7
  58.9 1.2 %collective-permute-done.7 = f32[72,128]{1,0:T(8,128)S(1)} collective-permute-done((f32[72,128]{1,0:T(8,128)S(1)}, f32[72,128]{1,0:T(8,128)S(1)}, u32[]{:S(2)}, u32[]{:S(2)}) %collective-permute-start.7) | collective-permute-done | bytes 36896 | tf_op jit(solution)/shard_map/ppermute | solution.py:496
  60.1 0.4 collective-permute-start.10
  60.5 1.1 %collective-permute-start.8 = (f32[72,128]{1,0:T(8,128)S(1)}, f32[72,128]{1,0:T(8,128)S(1)}, u32[]{:S(2)}, u32[]{:S(2)}) collective-permute-start(f32[72,128]{1,0:T(8,128)S(1)} %add.41), channel_id=1, source_target_pairs={{0,32},{1,33},{2,34},{3,35},{4,36},{5,37},{6,38},{7,39},{8,40},{9,... | collective-permute-start | bytes 110600 | tf_op jit(solution)/shard_map/ppermute | solution.py:496
  61.6 2.0 %collective-permute-start.9 = (f32[72,128]{1,0:T(8,128)S(1)}, f32[72,128]{1,0:T(8,128)S(1)}, u32[]{:S(2)}, u32[]{:S(2)}) collective-permute-start(f32[72,128]{1,0:T(8,128)S(1)} %add.41), channel_id=1, source_target_pairs={{0,64},{1,65},{2,66},{3,67},{4,68},{5,69},{6,70},{7,71},{8,72},{9,... | collective-permute-start | bytes 110600 | tf_op jit(solution)/shard_map/ppermute | solution.py:496
  63.6 0.1 copy.11
  63.7 15.2 %collective-permute-done.10 = f32[72,128]{1,0:T(8,128)S(1)} collective-permute-done((f32[72,128]{1,0:T(8,128)S(1)}, f32[72,128]{1,0:T(8,128)S(1)}, u32[]{:S(2)}, u32[]{:S(2)}) %collective-permute-start.10) | collective-permute-done | bytes 36896 | tf_op jit(solution)/shard_map/ppermute | solution.py:496
  78.9 2.3 %collective-permute-done.8 = f32[72,128]{1,0:T(8,128)S(1)} collective-permute-done((f32[72,128]{1,0:T(8,128)S(1)}, f32[72,128]{1,0:T(8,128)S(1)}, u32[]{:S(2)}, u32[]{:S(2)}) %collective-permute-start.8) | collective-permute-done | bytes 36896 | tf_op jit(solution)/shard_map/ppermute | solution.py:496
  81.2 0.1 collective-permute-start.12
  81.3 4.6 %collective-permute-start.14 = (f32[72,128]{1,0:T(8,128)S(1)}, f32[72,128]{1,0:T(8,128)S(1)}, u32[]{:S(2)}, u32[]{:S(2)}) collective-permute-start(f32[72,128]{1,0:T(8,128)S(1)} %add_add_fusion.2), channel_id=1, source_target_pairs={{0,24},{1,25},{2,26},{3,27},{4,28},{5,29},{6,30},{7,31},{8,16},{9,... | collective-permute-start | bytes 110600 | tf_op jit(solution)/shard_map/ppermute | solution.py:496
  85.9 8.4 %input_conv.1 = (bf16[64,8192]{1,0:T(8,128)(2,1)}, bf16[64,4096]{1,0:T(8,128)(2,1)S(1)}) custom-call(bf16[288,32]{1,0:T(8,128)(2,1)S(1)} %bitcast.27, bf16[128,4352]{1,0:T(8,128)(2,1)S(1)} %collective-permute-done.5.low, bf16[128,4352]{1,0:T(8,128)(2,1)} %get-tuple-element.9.d_ref.own, bf16[128,4352]{1,0:T(8,128)(2,1)S(1)} %collective-permute-done.6.high), custom_call_target="tpu_custom_call" | custom-call | flops 3208642560 | bytes 4456448 | tf_op jit(solution)/shard_map/input_conv/pallas_call | solution.py:382
  94.4 0.1 collective-permute-start.15
  94.5 3.2 %collective-permute-start.16 = (f32[72,128]{1,0:T(8,128)S(1)}, f32[72,128]{1,0:T(8,128)S(1)}, u32[]{:S(2)}, u32[]{:S(2)}) collective-permute-start(f32[72,128]{1,0:T(8,128)S(1)} %add_add_fusion.1), channel_id=1, source_target_pairs={{0,4},{1,5},{2,6},{3,7},{4,0},{5,1},{6,2},{7,3},{8,12},{9,13},{10,... | collective-permute-start | bytes 110600 | tf_op jit(solution)/shard_map/ppermute | solution.py:496
  97.8 1.5 %collective-permute-start.17 = (f32[72,128]{1,0:T(8,128)S(1)}, f32[72,128]{1,0:T(8,128)S(1)}, u32[]{:S(2)}, u32[]{:S(2)}) collective-permute-start(f32[72,128]{1,0:T(8,128)S(1)} %add_add_fusion.1), channel_id=1, source_target_pairs={{0,6},{1,7},{2,4},{3,5},{4,2},{5,3},{6,0},{7,1},{8,14},{9,15},{10,... | collective-permute-start | bytes 110600 | tf_op jit(solution)/shard_map/ppermute | solution.py:496
  99.2 1.2 %collective-permute-done.16 = f32[72,128]{1,0:T(8,128)S(1)} collective-permute-done((f32[72,128]{1,0:T(8,128)S(1)}, f32[72,128]{1,0:T(8,128)S(1)}, u32[]{:S(2)}, u32[]{:S(2)}) %collective-permute-start.16) | collective-permute-done | bytes 36896 | tf_op jit(solution)/shard_map/ppermute | solution.py:496
  100.4 2.5 %collective-permute-done.17 = f32[72,128]{1,0:T(8,128)S(1)} collective-permute-done((f32[72,128]{1,0:T(8,128)S(1)}, f32[72,128]{1,0:T(8,128)S(1)}, u32[]{:S(2)}, u32[]{:S(2)}) %collective-permute-start.17) | collective-permute-done | bytes 36896 | tf_op jit(solution)/shard_map/ppermute | solution.py:496
  102.9 0.8 reshape.56
  103.7 0.8 join.1
  (28 shorter events, 0.6 us)
Async XLA Ops:
  0.6 3.0 %collective-permute-start.1 = (bf16[64,8192]{1,0:T(8,128)(2,1)}, bf16[64,8192]{1,0:T(8,128)(2,1)S(1)}, u32[]{:S(2)}, u32[]{:S(2)}) collective-permute-start(bf16[64,8192]{1,0:T(8,128)(2,1)} %bitcast.23), channel_id=1, source_target_pairs={{0,1},{1,0},{2,3},{3,2},{4,5},{5,4},{6,7},{7,6},{8,9},{9,8},{10,11... | collective-permute-start | bytes 3145736 | tf_op jit(solution)/shard_map/ppermute | solution.py:496
  0.7 1.2 %copy-start = (bf16[2,32,8192]{2,1,0:T(8,128)(2,1)S(1)}, bf16[2,32,8192]{2,1,0:T(8,128)(2,1)}, u32[]{:S(2)}) copy-start(bf16[2,32,8192]{2,1,0:T(8,128)(2,1)} %param.5) | copy-start | bytes 3145732
  2.0 10.1 %copy-start.3 = (s32[2,9]{1,0:T(2,128)S(1)}, s32[2,9]{1,0:T(2,128)}, u32[]{:S(2)}) copy-start(s32[2,9]{1,0:T(2,128)} %param.8) | copy-start | bytes 220
  2.0 10.3 %copy-start.2 = (bf16[2,9,9,9]{3,0,2,1:T(2,128)(2,1)S(1)}, bf16[2,9,9,9]{3,0,2,1:T(2,128)(2,1)}, u32[]{:S(2)}) copy-start(bf16[2,9,9,9]{3,0,2,1:T(2,128)(2,1)} %param.7) | copy-start | bytes 8752
  3.8 20.9 %copy-start.1 = (bf16[9,32,32]{2,1,0:T(8,128)(2,1)S(1)}, bf16[9,32,32]{2,1,0:T(8,128)(2,1)}, u32[]{:S(2)}) copy-start(bf16[9,32,32]{2,1,0:T(8,128)(2,1)} %param.9) | copy-start | bytes 55300
  3.8 31.2 %collective-permute-start.2 = (bf16[128,4352]{1,0:T(8,128)(2,1)S(1)}, bf16[128,4352]{1,0:T(8,128)(2,1)S(1)}, u32[]{:S(2)}, u32[]{:S(2)}) collective-permute-start(bf16[128,4352]{1,0:T(8,128)(2,1)S(1)} %chip_window.1.own), channel_id=1, source_target_pairs={{0,2},{1,3},{2,4},{3,5},{4,6},{5,7},{6,8},{7,9},{8,10},{9,11},{10,... | collective-permute-start | bytes 3342344 | tf_op jit(solution)/shard_map/ppermute | solution.py:490
  7.7 28.4 %collective-permute-start.3 = (bf16[128,4352]{1,0:T(8,128)(2,1)S(1)}, bf16[128,4352]{1,0:T(8,128)(2,1)S(1)}, u32[]{:S(2)}, u32[]{:S(2)}) collective-permute-start(bf16[128,4352]{1,0:T(8,128)(2,1)S(1)} %chip_window.1.own), channel_id=1, source_target_pairs={{2,0},{3,1},{4,2},{5,3},{6,4},{7,5},{8,6},{9,7},{10,8},{11,9},{12,... | collective-permute-start | bytes 3342344 | tf_op jit(solution)/shard_map/ppermute | solution.py:490
  12.0 14.1 %collective-permute-start.4 = (bf16[64,8192]{1,0:T(8,128)(2,1)}, bf16[64,8192]{1,0:T(8,128)(2,1)}, u32[]{:S(2)}, u32[]{:S(2)}) collective-permute-start(bf16[64,8192]{1,0:T(8,128)(2,1)} %bitcast.12.cot_own), channel_id=1, source_target_pairs={{0,1},{1,0},{2,3},{3,2},{4,5},{5,4},{6,7},{7,6},{8,9},{9,8},{10,11... | collective-permute-start | bytes 3145736 | tf_op jit(solution)/shard_map/ppermute | solution.py:496
  12.5 2.5 %collective-permute-start = (bf16[2,9,9,9]{3,0,2,1:T(2,128)(2,1)S(1)}, bf16[2,9,9,9]{3,0,2,1:T(2,128)(2,1)}, u32[]{:S(2)}, u32[]{:S(2)}) collective-permute-start(bf16[2,9,9,9]{3,0,2,1:T(2,128)(2,1)S(1)} %broadcast_select_fusion), channel_id=1, source_target_pairs={{0,1},{1,0},{2,3},{3,2},{4,5},{5,4},{6,7},{7,6},{8,9},{9,8},{10,11... | collective-permute-start | bytes 8756 | tf_op jit(solution)/shard_map/ppermute | solution.py:496
  42.4 38.7 %collective-permute-start.5 = (bf16[128,4352]{1,0:T(8,128)(2,1)}, bf16[128,4352]{1,0:T(8,128)(2,1)S(1)}, u32[]{:S(2)}, u32[]{:S(2)}) collective-permute-start(bf16[128,4352]{1,0:T(8,128)(2,1)} %get-tuple-element.9.d_ref.own), channel_id=1, source_target_pairs={{0,2},{1,3},{2,4},{3,5},{4,6},{5,7},{6,8},{7,9},{8,10},{9,11},{10,... | collective-permute-start | bytes 3342344 | tf_op jit(solution)/shard_map/ppermute | solution.py:490
  46.1 35.1 %collective-permute-start.6 = (bf16[128,4352]{1,0:T(8,128)(2,1)}, bf16[128,4352]{1,0:T(8,128)(2,1)S(1)}, u32[]{:S(2)}, u32[]{:S(2)}) collective-permute-start(bf16[128,4352]{1,0:T(8,128)(2,1)} %get-tuple-element.9.d_ref.own), channel_id=1, source_target_pairs={{2,0},{3,1},{4,2},{5,3},{6,4},{7,5},{8,6},{9,7},{10,8},{11,9},{12,... | collective-permute-start | bytes 3342344 | tf_op jit(solution)/shard_map/ppermute | solution.py:490
  58.8 1.3 %collective-permute-start.7 = (f32[72,128]{1,0:T(8,128)S(1)}, f32[72,128]{1,0:T(8,128)S(1)}, u32[]{:S(2)}, u32[]{:S(2)}) collective-permute-start(f32[72,128]{1,0:T(8,128)S(1)} %weight_part.1), channel_id=1, source_target_pairs={{0,1},{1,0},{2,3},{3,2},{4,5},{5,4},{6,7},{7,6},{8,9},{9,8},{10,11... | collective-permute-start | bytes 110600 | tf_op jit(solution)/shard_map/ppermute | solution.py:496
  60.1 18.8 %collective-permute-start.10 = (f32[72,128]{1,0:T(8,128)S(1)}, f32[72,128]{1,0:T(8,128)S(1)}, u32[]{:S(2)}, u32[]{:S(2)}) collective-permute-start(f32[72,128]{1,0:T(8,128)S(1)} %add.41), channel_id=1, source_target_pairs={{0,96},{1,97},{2,98},{3,99},{4,100},{5,101},{6,102},{7,103},{8,104... | collective-permute-start | bytes 110600 | tf_op jit(solution)/shard_map/ppermute | solution.py:496
  60.5 20.6 %collective-permute-start.8 = (f32[72,128]{1,0:T(8,128)S(1)}, f32[72,128]{1,0:T(8,128)S(1)}, u32[]{:S(2)}, u32[]{:S(2)}) collective-permute-start(f32[72,128]{1,0:T(8,128)S(1)} %add.41), channel_id=1, source_target_pairs={{0,32},{1,33},{2,34},{3,35},{4,36},{5,37},{6,38},{7,39},{8,40},{9,... | collective-permute-start | bytes 110600 | tf_op jit(solution)/shard_map/ppermute | solution.py:496
  61.6 19.5 %collective-permute-start.9 = (f32[72,128]{1,0:T(8,128)S(1)}, f32[72,128]{1,0:T(8,128)S(1)}, u32[]{:S(2)}, u32[]{:S(2)}) collective-permute-start(f32[72,128]{1,0:T(8,128)S(1)} %add.41), channel_id=1, source_target_pairs={{0,64},{1,65},{2,66},{3,67},{4,68},{5,69},{6,70},{7,71},{8,72},{9,... | collective-permute-start | bytes 110600 | tf_op jit(solution)/shard_map/ppermute | solution.py:496
  81.2 13.2 %collective-permute-start.12 = (f32[72,128]{1,0:T(8,128)S(1)}, f32[72,128]{1,0:T(8,128)S(1)}, u32[]{:S(2)}, u32[]{:S(2)}) collective-permute-start(f32[72,128]{1,0:T(8,128)S(1)} %add_add_fusion.2), channel_id=1, source_target_pairs={{0,8},{1,9},{2,10},{3,11},{4,12},{5,13},{6,14},{7,15},{8,0},{9,1},... | collective-permute-start | bytes 110600 | tf_op jit(solution)/shard_map/ppermute | solution.py:496
  81.2 13.2 %collective-permute-start.13 = (f32[72,128]{1,0:T(8,128)S(1)}, f32[72,128]{1,0:T(8,128)S(1)}, u32[]{:S(2)}, u32[]{:S(2)}) collective-permute-start(f32[72,128]{1,0:T(8,128)S(1)} %add_add_fusion.2), channel_id=1, source_target_pairs={{0,16},{1,17},{2,18},{3,19},{4,20},{5,21},{6,22},{7,23},{8,24},{9,... | collective-permute-start | bytes 110600 | tf_op jit(solution)/shard_map/ppermute | solution.py:496
  81.3 13.1 %collective-permute-start.14 = (f32[72,128]{1,0:T(8,128)S(1)}, f32[72,128]{1,0:T(8,128)S(1)}, u32[]{:S(2)}, u32[]{:S(2)}) collective-permute-start(f32[72,128]{1,0:T(8,128)S(1)} %add_add_fusion.2), channel_id=1, source_target_pairs={{0,24},{1,25},{2,26},{3,27},{4,28},{5,29},{6,30},{7,31},{8,16},{9,... | collective-permute-start | bytes 110600 | tf_op jit(solution)/shard_map/ppermute | solution.py:496
  94.3 9.4 %collective-permute-start.11 = (bf16[64,4096]{1,0:T(8,128)(2,1)S(1)}, bf16[64,4096]{1,0:T(8,128)(2,1)S(1)}, u32[]{:S(2)}, u32[]{:S(2)}) collective-permute-start(bf16[64,4096]{1,0:T(8,128)(2,1)S(1)} %get-tuple-element.13), channel_id=1, source_target_pairs={{0,1},{1,0},{2,3},{3,2},{4,5},{5,4},{6,7},{7,6},{8,9},{9,8},{10,11... | collective-permute-start | bytes 1572872 | tf_op jit(solution)/shard_map/ppermute | solution.py:496
  94.4 4.8 %collective-permute-start.15 = (f32[72,128]{1,0:T(8,128)S(1)}, f32[72,128]{1,0:T(8,128)S(1)}, u32[]{:S(2)}, u32[]{:S(2)}) collective-permute-start(f32[72,128]{1,0:T(8,128)S(1)} %add_add_fusion.1), channel_id=1, source_target_pairs={{0,2},{1,3},{2,0},{3,1},{4,6},{5,7},{6,4},{7,5},{8,10},{9,11},{10,... | collective-permute-start | bytes 110600 | tf_op jit(solution)/shard_map/ppermute | solution.py:496
  94.5 5.8 %collective-permute-start.16 = (f32[72,128]{1,0:T(8,128)S(1)}, f32[72,128]{1,0:T(8,128)S(1)}, u32[]{:S(2)}, u32[]{:S(2)}) collective-permute-start(f32[72,128]{1,0:T(8,128)S(1)} %add_add_fusion.1), channel_id=1, source_target_pairs={{0,4},{1,5},{2,6},{3,7},{4,0},{5,1},{6,2},{7,3},{8,12},{9,13},{10,... | collective-permute-start | bytes 110600 | tf_op jit(solution)/shard_map/ppermute | solution.py:496
  97.8 5.2 %collective-permute-start.17 = (f32[72,128]{1,0:T(8,128)S(1)}, f32[72,128]{1,0:T(8,128)S(1)}, u32[]{:S(2)}, u32[]{:S(2)}) collective-permute-start(f32[72,128]{1,0:T(8,128)S(1)} %add_add_fusion.1), channel_id=1, source_target_pairs={{0,6},{1,7},{2,4},{3,5},{4,2},{5,3},{6,0},{7,1},{8,14},{9,15},{10,... | collective-permute-start | bytes 110600 | tf_op jit(solution)/shard_map/ppermute | solution.py:496
